TPU v7x, 32 devices: a whole 2x2x4 slice. The times are simulated.
32 devices in a mesh: dp: 8 (over y, x, core), seq: 4 (over z).
Axes of the slice: x: 2, y: 2, z: 4, core: 2. Of those that a mesh axis runs over, the one named last changes fastest.
Arguments:
- tokens: bfloat16 [8, 1024, 2048], P('dp', 'seq'), may hold values from -6 to 6
- lengths: int32 [8], P('dp'), may hold values from 128 to 1024, as said below
- repos: int32 [8], P('dp'), may hold values from 0 to 3
- ln1_gain: bfloat16 [2048], P(('dp', 'seq')), may hold values from 0.25 to 1.75
- ln1_bias: bfloat16 [2048], P(('dp', 'seq')), may hold values from -2 to 2
- w_query: bfloat16 [2048, 2048], P(('dp', 'seq')), may hold values from -0.125 to 0.125
- b_query: bfloat16 [2048], P(('dp', 'seq')), may hold values from -3 to 3
- w_key: bfloat16 [2048, 128], P(('dp', 'seq')), may hold values from -0.125 to 0.125
- w_value: bfloat16 [2048, 128], P(('dp', 'seq')), may hold values from -0.125 to 0.125
- b_value: bfloat16 [128], P(('dp', 'seq')), may hold values from -0.29882812 to 0.29882812
- w_out: bfloat16 [2048, 2048], P(('dp', 'seq')), may hold values from -1.5 to 1.5
- b_out: bfloat16 [2048], P(('dp', 'seq')), may hold values from -3 to 3
- ln2_gain: bfloat16 [2048], P(('dp', 'seq')), may hold values from 0.25 to 1.75
- ln2_bias: bfloat16 [2048], P(('dp', 'seq')), may hold values from -2 to 2
- w_fc: bfloat16 [2048, 8192], P(('dp', 'seq')), may hold values from -0.125 to 0.125
- b_fc: bfloat16 [8192], P(('dp', 'seq')), may hold values from -3 to 3
- w_proj: bfloat16 [8192, 2048], P(('dp', 'seq')), may hold values from -0.0625 to 0.0625
- b_proj: bfloat16 [2048], P(('dp', 'seq')), may hold values from -3 to 3
- grad_out: bfloat16 [8, 1024, 2048], P('dp', 'seq'), may hold values from -6 to 6
Outputs:
- output: bfloat16 [8, 1024, 2048], P('dp', 'seq')
- grad_tokens: bfloat16 [8, 1024, 2048], P('dp', 'seq')
- d_ln1_gain: float32 [2048], P(('dp', 'seq'))
- d_ln1_bias: float32 [2048], P(('dp', 'seq'))
- d_w_query: float32 [2048, 2048], P(('dp', 'seq'))
- d_b_query: float32 [2048], P(('dp', 'seq'))
- d_w_key: float32 [2048, 128], P(('dp', 'seq'))
- d_w_value: float32 [2048, 128], P(('dp', 'seq'))
- d_b_value: float32 [128], P(('dp', 'seq'))
- d_w_out: float32 [2048, 2048], P(('dp', 'seq'))
- d_b_out: float32 [2048], P(('dp', 'seq'))
- d_ln2_gain: float32 [2048], P(('dp', 'seq'))
- d_ln2_bias: float32 [2048], P(('dp', 'seq'))
- d_w_fc: float32 [2048, 8192], P(('dp', 'seq'))
- d_b_fc: float32 [8192], P(('dp', 'seq'))
- d_w_proj: float32 [8192, 2048], P(('dp', 'seq'))
- d_b_proj: float32 [2048], P(('dp', 'seq'))
Inputs may be any that keep to these rules, and one draw needn't show every extreme that they name: `lengths`: tokens at positions at or beyond a window's length are padding.
All inputs are finite; a program needn't handle non-finite values.
Results may differ from a plain program's by a relative error of at most 0.014.
Values may be sent and summed in bfloat16 or wider, within the bound.
No kernel may reach another device: no remote copies, remote signals or barrier semaphores. Data moves between devices by JAX's collectives and lax.ppermute only.
A program may use at most 384 MiB of HBM per device.

v0:
```python
import math

import jax
import jax.numpy as jnp
from jax import lax
from jax.sharding import PartitionSpec as P

HEADS = 16
HEAD = 128
REPOS = 4


norm_epsilon = 1e-05


def normalize(values, gain, offset):
    centre = jnp.mean(values, axis=-1, keepdims=True)
    shifted = values - centre
    inverse = lax.rsqrt(jnp.mean(shifted * shifted, axis=-1, keepdims=True) + norm_epsilon)
    normed = shifted * inverse
    return (normed * gain + offset, normed, inverse)


def normalize_back(grad_in, normed, inverse, gain):
    scaled = grad_in * gain
    first_mean = jnp.mean(scaled, axis=-1, keepdims=True)
    second_mean = jnp.mean(scaled * normed, axis=-1, keepdims=True)
    grad_values = inverse * (scaled - first_mean - normed * second_mean)
    return (grad_values, jnp.sum(grad_in * normed, axis=0), jnp.sum(grad_in, axis=0))


def gelu_tanh(values):
    return jax.nn.gelu(values, approximate=True)


def block_scores(query_block, block_start, key_rows, scale):
    scores = (
        jnp.einsum("thd,jd->thj", query_block, key_rows, preferred_element_type=jnp.float32) * scale
    )
    places = block_start + jnp.arange(query_block.shape[0], dtype=jnp.int32)
    allowed = jnp.arange(key_rows.shape[0], dtype=jnp.int32)[None, None, :] <= places[:, None, None]
    return jnp.where(allowed, scores, -1e30)


def local(
    tokens,
    lengths,
    repos,
    ln1_gain,
    ln1_bias,
    w_query,
    b_query,
    w_key,
    w_value,
    b_value,
    w_out,
    b_out,
    ln2_gain,
    ln2_bias,
    w_fc,
    b_fc,
    w_proj,
    b_proj,
    grad_out,
):
    windows, span, width = tokens.shape
    rows = windows * span
    scale = 1.0 / math.sqrt(HEAD)
    block_len = math.gcd(span, max(1, 1024 // HEADS))
    blocks = span // block_len
    repo_ids = jnp.arange(REPOS, dtype=jnp.int32)
    member = (repos[:, None] == repo_ids[None, :]).astype(jnp.float32)
    local_counts = jnp.sum(member * lengths.astype(jnp.float32)[:, None], axis=0)
    counts = lax.psum(local_counts, "dp")
    overall = jnp.sum(counts)
    own_count = jnp.sum(member * counts[None, :], axis=1)
    window_weight = overall / (REPOS * own_count)
    first_place = lax.axis_index("seq") * span
    places = first_place + jnp.arange(span, dtype=jnp.int32)
    valid = (places[None, :] < lengths[:, None]).astype(jnp.float32)
    valid_rows = valid.reshape(rows, 1)
    (
        full_ln1_gain,
        full_ln1_bias,
        full_w_query,
        full_b_query,
        full_w_key,
        full_w_value,
        full_b_value,
        full_w_out,
        full_b_out,
        full_ln2_gain,
        full_ln2_bias,
        full_w_fc,
        full_b_fc,
        full_w_proj,
        full_b_proj,
    ) = (
        lax.all_gather(ln1_gain, ("dp", "seq"), axis=0, tiled=True),
        lax.all_gather(ln1_bias, ("dp", "seq"), axis=0, tiled=True),
        lax.all_gather(w_query, ("dp", "seq"), axis=0, tiled=True),
        lax.all_gather(b_query, ("dp", "seq"), axis=0, tiled=True),
        lax.all_gather(w_key, ("dp", "seq"), axis=0, tiled=True),
        lax.all_gather(w_value, ("dp", "seq"), axis=0, tiled=True),
        lax.all_gather(b_value, ("dp", "seq"), axis=0, tiled=True),
        lax.all_gather(w_out, ("dp", "seq"), axis=0, tiled=True),
        lax.all_gather(b_out, ("dp", "seq"), axis=0, tiled=True),
        lax.all_gather(ln2_gain, ("dp", "seq"), axis=0, tiled=True),
        lax.all_gather(ln2_bias, ("dp", "seq"), axis=0, tiled=True),
        lax.all_gather(w_fc, ("dp", "seq"), axis=0, tiled=True),
        lax.all_gather(b_fc, ("dp", "seq"), axis=0, tiled=True),
        lax.all_gather(w_proj, ("dp", "seq"), axis=0, tiled=True),
        lax.all_gather(b_proj, ("dp", "seq"), axis=0, tiled=True),
    )
    inputs32 = tokens.reshape(rows, width).astype(jnp.float32)
    normed1_out, normed1, inverse1 = normalize(
        inputs32, full_ln1_gain.astype(jnp.float32), full_ln1_bias.astype(jnp.float32)
    )
    attn_in = normed1_out.astype(jnp.bfloat16)
    query_low = (
        jnp.dot(attn_in, full_w_query, preferred_element_type=jnp.float32)
        + full_b_query.astype(jnp.float32)
    ).astype(jnp.bfloat16)
    key_low = jnp.dot(attn_in, full_w_key, preferred_element_type=jnp.float32).astype(jnp.bfloat16)
    value_low = (
        jnp.dot(attn_in, full_w_value, preferred_element_type=jnp.float32)
        + full_b_value.astype(jnp.float32)
    ).astype(jnp.bfloat16)
    key_all, value_all = (
        lax.all_gather(key_low.reshape(windows, span, HEAD), "seq", axis=1, tiled=True),
        lax.all_gather(value_low.reshape(windows, span, HEAD), "seq", axis=1, tiled=True),
    )
    query_blocks = query_low.reshape(windows, blocks, block_len, HEADS, HEAD)
    starts = first_place + jnp.arange(blocks, dtype=jnp.int32) * block_len

    def forward_window(window_args):
        query_set, key_rows, value_rows = window_args

        def forward_block(block_args):
            query_block, block_start = block_args
            scores = block_scores(query_block, block_start, key_rows, scale)
            top_score = jnp.max(scores, axis=-1, keepdims=True)
            expo = jnp.exp(scores - top_score)
            totals = jnp.sum(expo, axis=-1, keepdims=True)
            probs = expo / totals
            log_total = (top_score + jnp.log(totals))[..., 0]
            attended = jnp.einsum(
                "thj,jd->thd",
                probs.astype(jnp.bfloat16),
                value_rows,
                preferred_element_type=jnp.float32,
            )
            return (attended, log_total)

        return lax.map(forward_block, (query_set, starts))

    attended, log_totals = lax.map(forward_window, (query_blocks, key_all, value_all))
    attn_low = (attended.reshape(rows, width) * valid_rows).astype(jnp.bfloat16)
    hidden_one = (
        inputs32
        + jnp.dot(attn_low, full_w_out, preferred_element_type=jnp.float32)
        + full_b_out.astype(jnp.float32)
    )
    normed2_out, normed2, inverse2 = normalize(
        hidden_one, full_ln2_gain.astype(jnp.float32), full_ln2_bias.astype(jnp.float32)
    )
    mlp_in = normed2_out.astype(jnp.bfloat16)
    pre_act = jnp.dot(mlp_in, full_w_fc, preferred_element_type=jnp.float32) + full_b_fc.astype(
        jnp.float32
    )
    act_low = gelu_tanh(pre_act).astype(jnp.bfloat16)
    branch_two = jnp.dot(
        act_low, full_w_proj, preferred_element_type=jnp.float32
    ) + full_b_proj.astype(jnp.float32)
    output = (hidden_one + branch_two).astype(jnp.bfloat16).reshape(windows, span, width)
    (
        back_ln1_gain,
        back_w_query,
        back_w_key,
        back_w_value,
        back_w_out,
        back_ln2_gain,
        back_w_fc,
        back_w_proj,
    ) = (
        lax.all_gather(ln1_gain, ("dp", "seq"), axis=0, tiled=True),
        lax.all_gather(w_query, ("dp", "seq"), axis=0, tiled=True),
        lax.all_gather(w_key, ("dp", "seq"), axis=0, tiled=True),
        lax.all_gather(w_value, ("dp", "seq"), axis=0, tiled=True),
        lax.all_gather(w_out, ("dp", "seq"), axis=0, tiled=True),
        lax.all_gather(ln2_gain, ("dp", "seq"), axis=0, tiled=True),
        lax.all_gather(w_fc, ("dp", "seq"), axis=0, tiled=True),
        lax.all_gather(w_proj, ("dp", "seq"), axis=0, tiled=True),
    )
    row_scale = (valid * window_weight[:, None]).reshape(rows, 1)
    grad_top = grad_out.reshape(rows, width).astype(jnp.float32) * row_scale
    grad_two = grad_top.astype(jnp.bfloat16)
    d_w_proj = jnp.einsum("tf,td->fd", act_low, grad_two, preferred_element_type=jnp.float32)
    d_b_proj = jnp.sum(grad_two.astype(jnp.float32), axis=0)
    grad_act = jnp.einsum("td,fd->tf", grad_two, back_w_proj, preferred_element_type=jnp.float32)
    unused_value, gelu_pull = jax.vjp(gelu_tanh, pre_act)
    grad_pre_low = gelu_pull(grad_act)[0].astype(jnp.bfloat16)
    d_w_fc = jnp.einsum("td,tf->df", mlp_in, grad_pre_low, preferred_element_type=jnp.float32)
    d_b_fc = jnp.sum(grad_pre_low.astype(jnp.float32), axis=0)
    grad_mlp_in = jnp.einsum(
        "tf,df->td", grad_pre_low, back_w_fc, preferred_element_type=jnp.float32
    )
    grad_norm2, d_ln2_gain, d_ln2_bias = normalize_back(
        grad_mlp_in, normed2, inverse2, back_ln2_gain.astype(jnp.float32)
    )
    grad_mid = grad_top + grad_norm2
    grad_one = grad_mid.astype(jnp.bfloat16)
    d_w_out = jnp.einsum("tc,td->cd", attn_low, grad_one, preferred_element_type=jnp.float32)
    d_b_out = jnp.sum(grad_one.astype(jnp.float32), axis=0)
    grad_att = (
        jnp.einsum("td,cd->tc", grad_one, back_w_out, preferred_element_type=jnp.float32)
        * valid_rows
    ).astype(jnp.bfloat16)
    grad_blocks = grad_att.reshape(windows, blocks, block_len, HEADS, HEAD)

    def backward_window(window_args):
        query_set, key_rows, value_rows, grad_set, total_set = window_args

        def backward_block(carry, block_args):
            key_grad, value_grad = carry
            query_block, grad_block, log_total, block_start = block_args
            scores = block_scores(query_block, block_start, key_rows, scale)
            probs = jnp.exp(scores - log_total[..., None])
            dprobs = jnp.einsum(
                "thd,jd->thj", grad_block, value_rows, preferred_element_type=jnp.float32
            )
            dscores = probs * (dprobs - jnp.sum(probs * dprobs, axis=-1, keepdims=True))
            dscores_low = dscores.astype(jnp.bfloat16)
            query_grad = (
                jnp.einsum("thj,jd->thd", dscores_low, key_rows, preferred_element_type=jnp.float32)
                * scale
            )
            key_part = (
                jnp.einsum(
                    "thj,thd->jd", dscores_low, query_block, preferred_element_type=jnp.float32
                )
                * scale
            )
            value_part = jnp.einsum(
                "thj,thd->jd",
                probs.astype(jnp.bfloat16),
                grad_block,
                preferred_element_type=jnp.float32,
            )
            return ((key_grad + key_part, value_grad + value_part), query_grad)

        zero_rows = jnp.zeros(key_rows.shape, jnp.float32)
        (key_grad, value_grad), query_grad = lax.scan(
            backward_block, (zero_rows, zero_rows), (query_set, grad_set, total_set, starts)
        )
        return (key_grad, value_grad, query_grad)

    key_grads, value_grads, query_grads = lax.map(
        backward_window, (query_blocks, key_all, value_all, grad_blocks, log_totals)
    )
    key_share, value_share = (
        lax.psum_scatter(
            key_grads.astype(jnp.bfloat16), "seq", scatter_dimension=1, tiled=True
        ).astype(jnp.float32),
        lax.psum_scatter(
            value_grads.astype(jnp.bfloat16), "seq", scatter_dimension=1, tiled=True
        ).astype(jnp.float32),
    )
    key_grad_low = key_share.reshape(rows, HEAD).astype(jnp.bfloat16)
    value_grad_low = value_share.reshape(rows, HEAD).astype(jnp.bfloat16)
    query_grad_low = query_grads.reshape(rows, width).astype(jnp.bfloat16)
    d_w_query = jnp.einsum("tc,td->cd", attn_in, query_grad_low, preferred_element_type=jnp.float32)
    d_b_query = jnp.sum(query_grad_low.astype(jnp.float32), axis=0)
    d_w_key = jnp.einsum("tc,td->cd", attn_in, key_grad_low, preferred_element_type=jnp.float32)
    d_w_value = jnp.einsum("tc,td->cd", attn_in, value_grad_low, preferred_element_type=jnp.float32)
    d_b_value = jnp.sum(value_grad_low.astype(jnp.float32), axis=0)
    grad_attn_in = jnp.einsum(
        "td,cd->tc", query_grad_low, back_w_query, preferred_element_type=jnp.float32
    )
    grad_attn_in = grad_attn_in + jnp.einsum(
        "td,cd->tc", key_grad_low, back_w_key, preferred_element_type=jnp.float32
    )
    grad_attn_in = grad_attn_in + jnp.einsum(
        "td,cd->tc", value_grad_low, back_w_value, preferred_element_type=jnp.float32
    )
    grad_norm1, d_ln1_gain, d_ln1_bias = normalize_back(
        grad_attn_in, normed1, inverse1, back_ln1_gain.astype(jnp.float32)
    )
    grad_tokens = (grad_mid + grad_norm1).astype(jnp.bfloat16).reshape(windows, span, width)
    shares = (
        lax.psum_scatter(d_ln1_gain, ("dp", "seq"), scatter_dimension=0, tiled=True),
        lax.psum_scatter(d_ln1_bias, ("dp", "seq"), scatter_dimension=0, tiled=True),
        lax.psum_scatter(d_w_query, ("dp", "seq"), scatter_dimension=0, tiled=True),
        lax.psum_scatter(d_b_query, ("dp", "seq"), scatter_dimension=0, tiled=True),
        lax.psum_scatter(d_w_key, ("dp", "seq"), scatter_dimension=0, tiled=True),
        lax.psum_scatter(d_w_value, ("dp", "seq"), scatter_dimension=0, tiled=True),
        lax.psum_scatter(d_b_value, ("dp", "seq"), scatter_dimension=0, tiled=True),
        lax.psum_scatter(d_w_out, ("dp", "seq"), scatter_dimension=0, tiled=True),
        lax.psum_scatter(d_b_out, ("dp", "seq"), scatter_dimension=0, tiled=True),
        lax.psum_scatter(d_ln2_gain, ("dp", "seq"), scatter_dimension=0, tiled=True),
        lax.psum_scatter(d_ln2_bias, ("dp", "seq"), scatter_dimension=0, tiled=True),
        lax.psum_scatter(d_w_fc, ("dp", "seq"), scatter_dimension=0, tiled=True),
        lax.psum_scatter(d_b_fc, ("dp", "seq"), scatter_dimension=0, tiled=True),
        lax.psum_scatter(d_w_proj, ("dp", "seq"), scatter_dimension=0, tiled=True),
        lax.psum_scatter(d_b_proj, ("dp", "seq"), scatter_dimension=0, tiled=True),
    )
    return (
        output,
        grad_tokens,
        shares[0],
        shares[1],
        shares[2],
        shares[3],
        shares[4],
        shares[5],
        shares[6],
        shares[7],
        shares[8],
        shares[9],
        shares[10],
        shares[11],
        shares[12],
        shares[13],
        shares[14],
    )


def solution(mesh):
    return jax.shard_map(
        local,
        mesh=mesh,
        in_specs=(
            P("dp", "seq", None),
            P("dp"),
            P("dp"),
            P(("dp", "seq")),
            P(("dp", "seq")),
            P(("dp", "seq"), None),
            P(("dp", "seq")),
            P(("dp", "seq"), None),
            P(("dp", "seq"), None),
            P(("dp", "seq")),
            P(("dp", "seq"), None),
            P(("dp", "seq")),
            P(("dp", "seq")),
            P(("dp", "seq")),
            P(("dp", "seq"), None),
            P(("dp", "seq")),
            P(("dp", "seq"), None),
            P(("dp", "seq")),
            P("dp", "seq", None),
        ),
        out_specs=(
            P("dp", "seq", None),
            P("dp", "seq", None),
            P(("dp", "seq")),
            P(("dp", "seq")),
            P(("dp", "seq"), None),
            P(("dp", "seq")),
            P(("dp", "seq"), None),
            P(("dp", "seq"), None),
            P(("dp", "seq")),
            P(("dp", "seq"), None),
            P(("dp", "seq")),
            P(("dp", "seq")),
            P(("dp", "seq")),
            P(("dp", "seq"), None),
            P(("dp", "seq")),
            P(("dp", "seq"), None),
            P(("dp", "seq")),
        ),
        check_vma=False,
    )
```

profile of v0, /device:TPU:9, one launch (start us, length us, event | category | flops | bytes accessed | tf_op | source)
XLA Modules:
  0.0 4695.3 jit_solution(6478847893672574098)
XLA Ops:
  11.4 11.8 psum.7
  25.3 42.9 all-reduce.18
  68.3 59.8 %all-gather.2 = bf16[32,1,256]{2,1,0:T(2,128)(2,1)S(1)} all-gather(bf16[1,1,256]{2,1,0:T(2,128)(2,1)S(1)} %reshape.341), channel_id=1, replica_groups=mesh['dp'=8,'seq'=4] {'dp','seq'}, dimensions={0}, use_global_device_ids=true | all-gather | bytes 16896 | tf_op jit(solution)/shard_map/all_gather | solution.py:111
  131.4 74.5 %all_gather.63 = bf16[2048,128]{1,0:T(8,128)(2,1)S(1)} all-gather(bf16[64,128]{1,0:T(8,128)(2,1)S(1)} %copy-done.30), channel_id=1, replica_groups=mesh['dp'=8,'seq'=4] {'dp','seq'}, dimensions={0}, use_global_device_ids=true | all-gather | bytes 540672 | tf_op jit(solution)/shard_map/all_gather | solution.py:103
  206.7 10.0 all-gather
  216.7 81.3 %all_gather.65 = bf16[2048,128]{1,0:T(8,128)(2,1)S(1)} all-gather(bf16[64,128]{1,0:T(8,128)(2,1)S(1)} %copy-done.31), channel_id=1, replica_groups=mesh['dp'=8,'seq'=4] {'dp','seq'}, dimensions={0}, use_global_device_ids=true | all-gather | bytes 540672 | tf_op jit(solution)/shard_map/all_gather | solution.py:104
  299.4 21.5 all-gather.1
  322.1 5.8 fusion.84
  329.1 29.4 while.49
  359.9 7.1 fusion.119
  367.4 13.8 all-gather.12.cloned.1.call-done
  381.2 17.3 convolution_add_fusion
  398.5 178.9 %all-gather.14.cloned.1.call-done = bf16[8192,2048]{1,0:T(8,128)(2,1)} async-done(((bf16[256,2048]{1,0:T(8,128)(2,1)}), bf16[8192,2048]{1,0:T(8,128)(2,1)}) %all-gather.14.cloned.1.call-update) | async-done | bytes 33554448 | tf_op jit(solution)/shard_map/all_gather | solution.py:112
  577.4 21.7 convert_reduce_fusion
  599.1 18.4 multiply_reduce_fusion.1
  620.8 6.5 fusion.83
  628.6 62.3 %while.50 = (s32[]{:T(128)}, f32[1024,128]{1,0:T(8,128)}, f32[1024,128]{1,0:T(8,128)}, bf16[4,64,16,128]{3,2,1,0:T(8,128)(2,1)}, s32[4]{0:T(128)S(1)}, /*index=5...) while((s32[]{:T(128)}, f32[1024,128]{1,0:T(8,128)}, ...), condition=%wide.region_15.16_spmd.clone.clone, body=%wide.region_13.15_spmd.clone.sunk.clone | while | flops 1358756864 | bytes 82342736 | solution.py:253
  694.8 7.1 fusion.90
  702.7 5.5 reduce-scatter.11.cloned.1.call-done
  709.6 19.3 reduce-scatter.9.cloned.1.call-done
  737.8 8.1 fusion.88
  747.5 10.4 fusion.103
  759.5 25.5 fusion.114
  785.7 27.7 fusion.106
  814.0 19.5 fusion.66
  837.6 25.2 all-reduce.21.cloned.1.call-done
  874.1 119.1 %reduce-scatter.15.cloned.1.call-done = f32[64,128]{1,0:T(8,128)} async-done(((f32[2048,128]{1,0:T(8,128)}), f32[64,128]{1,0:T(8,128)}) %reduce-scatter.15.cloned.1.call-update) | async-done | bytes 32784 | tf_op jit(solution)/shard_map/reduce_scatter | solution.py:295
  993.2 135.0 %reduce-scatter.17.cloned.1.call-done = f32[64,128]{1,0:T(8,128)} async-done(((f32[2048,128]{1,0:T(8,128)}), f32[64,128]{1,0:T(8,128)}) %reduce-scatter.17.cloned.1.call-update) | async-done | bytes 32784 | tf_op jit(solution)/shard_map/reduce_scatter | solution.py:296
  1128.3 369.3 %reduce-scatter.13.cloned.1.call-done = f32[64,2048]{1,0:T(8,128)} async-done(((f32[2048,2048]{1,0:T(8,128)}), f32[64,2048]{1,0:T(8,128)}) %reduce-scatter.13.cloned.1.call-update) | async-done | bytes 524304 | tf_op jit(solution)/shard_map/reduce_scatter | solution.py:293
  1497.6 365.2 %reduce-scatter.19.cloned.1.call-done = f32[64,2048]{1,0:T(8,128)} async-done(((f32[2048,2048]{1,0:T(8,128)}), f32[64,2048]{1,0:T(8,128)}) %reduce-scatter.19.cloned.1.call-update) | async-done | bytes 524304 | tf_op jit(solution)/shard_map/reduce_scatter | solution.py:298
  1862.7 1412.1 %reduce-scatter.21.cloned.1.call-done = f32[64,8192]{1,0:T(8,128)} async-done(((f32[2048,8192]{1,0:T(8,128)}), f32[64,8192]{1,0:T(8,128)}) %reduce-scatter.21.cloned.1.call-update) | async-done | bytes 2097168 | tf_op jit(solution)/shard_map/reduce_scatter | solution.py:302
  3274.9 1413.7 %reduce-scatter.23.cloned.1.call-done = f32[256,2048]{1,0:T(8,128)} async-done(((f32[8192,2048]{1,0:T(8,128)}), f32[256,2048]{1,0:T(8,128)}) %reduce-scatter.23.cloned.1.call-update) | async-done | bytes 2097168 | tf_op jit(solution)/shard_map/reduce_scatter | solution.py:304
  (294 shorter events, 143.2 us)
Async XLA Ops:
  7.3 17.8 copy-start.44
  7.3 61.0 %copy-start.45 = (bf16[256]{0:T(256)(128)(2,1)S(1)}, bf16[256]{0:T(256)(128)(2,1)}, u32[]{:S(2)}) copy-start(bf16[256]{0:T(256)(128)(2,1)} %param.38) | copy-start | bytes 1540
  7.3 123.4 %copy-start.2 = (bf16[1,256,2048]{2,1,0:T(8,128)(2,1)S(1)}, bf16[1,256,2048]{2,1,0:T(8,128)(2,1)}, u32[]{:S(2)}) copy-start(bf16[1,256,2048]{2,1,0:T(8,128)(2,1)} %param.23) | copy-start | bytes 3145732
  7.3 314.8 %all-gather.8.cloned.1.call-start = ((), (), s32[]{:S(2)}) async-start(), calls=%async_computation.8 | async-start | bytes 8650752 | tf_op jit(solution)/shard_map/all_gather | solution.py:101
  8.0 350.5 %all-gather.10.cloned.1.call-start = ((), (), s32[]{:S(2)}) async-start(), calls=%async_computation.9 | async-start | bytes 8650752 | tf_op jit(solution)/shard_map/all_gather | solution.py:106
  8.8 122.5 %copy-start.30 = (bf16[64,128]{1,0:T(8,128)(2,1)S(1)}, bf16[64,128]{1,0:T(8,128)(2,1)}, u32[]{:S(2)}) copy-start(bf16[64,128]{1,0:T(8,128)(2,1)} %param.30) | copy-start | bytes 49156
  8.8 372.4 %all-gather.12.cloned.1.call-start = ((), (), s32[]{:S(2)}) async-start(), calls=%async_computation.10 | async-start | bytes 34603008 | tf_op jit(solution)/shard_map/all_gather | solution.py:110
  9.5 567.9 %all-gather.14.cloned.1.call-start = ((), (), s32[]{:S(2)}) async-start(), calls=%async_computation.11 | async-start | bytes 34603008 | tf_op jit(solution)/shard_map/all_gather | solution.py:112
  10.1 698.1 %reduce-scatter.11.cloned.1.call-start = ((), (), s32[]{:S(2)}) async-start(), calls=%async_computation.13 | async-start | bytes 327680 | tf_op jit(solution)/shard_map/reduce_scatter | solution.py:265
  68.2 253.9 %copy-start.25 = (f32[2048]{0:T(1024)}, f32[2048]{0:T(1024)S(1)}, u32[]{:S(2)}) copy-start(f32[2048]{0:T(1024)S(1)} %convert_element_type.163) | copy-start | bytes 24580
  68.3 253.8 %copy-start.23 = (f32[2048]{0:T(1024)}, f32[2048]{0:T(1024)S(1)}, u32[]{:S(2)}) copy-start(f32[2048]{0:T(1024)S(1)} %convert_element_type.162) | copy-start | bytes 24580
  128.7 252.5 %copy-start.20 = (f32[2048]{0:T(1024)}, f32[2048]{0:T(1024)S(1)}, u32[]{:S(2)}) copy-start(f32[2048]{0:T(1024)S(1)} %convert_element_type.174) | copy-start | bytes 24580
  130.9 191.2 %copy-start.28 = (f32[256]{0:T(256)}, f32[256]{0:T(256)S(1)}, u32[]{:S(2)}) copy-start(f32[256]{0:T(256)S(1)} %broadcast_multiply_fusion.5) | copy-start | bytes 3076
  131.3 190.8 %copy-start.32 = (f32[256]{0:T(256)}, f32[256]{0:T(256)S(1)}, u32[]{:S(2)}) copy-start(f32[256]{0:T(256)S(1)} %add_rsqrt_fusion.1) | copy-start | bytes 3076
  131.3 85.3 %copy-start.31 = (bf16[64,128]{1,0:T(8,128)(2,1)S(1)}, bf16[64,128]{1,0:T(8,128)(2,1)}, u32[]{:S(2)}) copy-start(bf16[64,128]{1,0:T(8,128)(2,1)} %param.31) | copy-start | bytes 49156
  321.0 296.5 %copy-start.34 = (f32[256]{0:T(256)}, f32[256]{0:T(256)S(1)}, u32[]{:S(2)}) copy-start(f32[256]{0:T(256)S(1)} %fusion.100) | copy-start | bytes 3076
  367.0 250.4 %copy-start.4 = (f32[256,2048]{1,0:T(8,128)}, f32[256,2048]{1,0:T(8,128)S(1)}, u32[]{:S(2)}) copy-start(f32[256,2048]{1,0:T(8,128)S(1)} %get-tuple-element.267) | copy-start | bytes 6291460
  381.2 196.2 %copy-start.11 = (bf16[1,256,2048]{2,1,0:T(8,128)(2,1)S(1)}, bf16[1,256,2048]{2,1,0:T(8,128)(2,1)}, u32[]{:S(2)}) copy-start(bf16[1,256,2048]{2,1,0:T(8,128)(2,1)} %param.41) | copy-start | bytes 3145732
  628.6 64.3 %copy-start.3 = (bf16[1,256,2048]{2,1,0:T(8,128)(2,1)S(1)}, bf16[1,256,2048]{2,1,0:T(8,128)(2,1)}, u32[]{:S(2)}) copy-start(bf16[1,256,2048]{2,1,0:T(8,128)(2,1)} %param.23) | copy-start | bytes 3145732
  628.6 64.3 %copy-start.24 = (f32[2048]{0:T(1024)S(1)}, f32[2048]{0:T(1024)}, u32[]{:S(2)}) copy-start(f32[2048]{0:T(1024)} %copy-done.23) | copy-start | bytes 24580
  628.6 64.3 %copy-start.26 = (f32[2048]{0:T(1024)S(1)}, f32[2048]{0:T(1024)}, u32[]{:S(2)}) copy-start(f32[2048]{0:T(1024)} %copy-done.25) | copy-start | bytes 24580
  628.6 64.3 %copy-start.29 = (f32[256]{0:T(256)S(1)}, f32[256]{0:T(256)}, u32[]{:S(2)}) copy-start(f32[256]{0:T(256)} %copy-done.28) | copy-start | bytes 3076
  628.6 64.3 %copy-start.33 = (f32[256]{0:T(256)S(1)}, f32[256]{0:T(256)}, u32[]{:S(2)}) copy-start(f32[256]{0:T(256)} %copy-done.32) | copy-start | bytes 3076
  692.8 36.1 reduce-scatter.9.cloned.1.call-start
  694.7 168.1 %all-reduce.21.cloned.1.call-start = ((), (), s32[]{:S(2)}) async-start(), calls=%async_computation.20 | async-start | bytes 181248
  709.6 21.6 copy-start.16
  734.2 259.1 %reduce-scatter.15.cloned.1.call-start = ((), (), s32[]{:S(2)}) async-start(), calls=%async_computation.15 | async-start | bytes 1081344 | tf_op jit(solution)/shard_map/reduce_scatter | solution.py:295
  735.8 392.5 %reduce-scatter.17.cloned.1.call-start = ((), (), s32[]{:S(2)}) async-start(), calls=%async_computation.16 | async-start | bytes 1081344 | tf_op jit(solution)/shard_map/reduce_scatter | solution.py:296
  737.3 760.2 %reduce-scatter.13.cloned.1.call-start = ((), (), s32[]{:S(2)}) async-start(), calls=%async_computation.14 | async-start | bytes 17301504 | tf_op jit(solution)/shard_map/reduce_scatter | solution.py:293
  745.9 1116.8 %reduce-scatter.19.cloned.1.call-start = ((), (), s32[]{:S(2)}) async-start(), calls=%async_computation.17 | async-start | bytes 17301504 | tf_op jit(solution)/shard_map/reduce_scatter | solution.py:298
  757.9 2516.9 %reduce-scatter.21.cloned.1.call-start = ((), (), s32[]{:S(2)}) async-start(), calls=%async_computation.18 | async-start | bytes 69206016 | tf_op jit(solution)/shard_map/reduce_scatter | solution.py:302
  785.1 3903.5 %reduce-scatter.23.cloned.1.call-start = ((), (), s32[]{:S(2)}) async-start(), calls=%async_computation.19 | async-start | bytes 69206016 | tf_op jit(solution)/shard_map/reduce_scatter | solution.py:304
  (45 other events, 218.1 us)
Sparse Core Ops, SparseCore 0:
  11.1 79.7 all-gather.7
  93.8 78.3 all-gather.9
  175.1 206.0 all-gather.11
  384.0 193.3 all-gather.13
  692.9 15.2 reduce-scatter.10
  711.0 17.8 reduce-scatter.8
  735.9 126.8 all-reduce.20
  865.7 127.5 reduce-scatter.14
  996.1 132.1 reduce-scatter.16
  1131.1 366.4 reduce-scatter.12
  1500.5 362.1 reduce-scatter.18
  1865.7 1409.1 reduce-scatter.20
  3277.9 1410.6 reduce-scatter.22
where the time goes:
time: 4710 us; the launch traced here: 4700 us
  waiting for transfers between devices  4060 us (86%)
  blocking collectives  302 us (6%)
  matrix products  242 us (5%)
    reduce_scatter x1, waiting for transfers between devices, local(): lax.psum_scatter(d_w_proj, ('dp', 'seq'), scatter_dimension=0, tiled=True)  1410 us
    reduce_scatter x1, waiting for transfers between devices, local(): lax.psum_scatter(d_w_fc, ('dp', 'seq'), scatter_dimension=0, tiled=True)  1410 us
    reduce_scatter x1, waiting for transfers between devices, local(): lax.psum_scatter(d_w_query, ('dp', 'seq'), scatter_dimension=0, tiled=True)  369 us
    reduce_scatter x1, waiting for transfers between devices, local(): lax.psum_scatter(d_w_out, ('dp', 'seq'), scatter_dimension=0, tiled=True)  365 us
    all_gather x1, waiting for transfers between devices, local(): lax.all_gather(w_proj, ('dp', 'seq'), axis=0, tiled=True)  179 us
    reduce_scatter x1, waiting for transfers between devices, local(): lax.psum_scatter(d_w_value, ('dp', 'seq'), scatter_dimension=0, tiled=True)  135 us
    reduce_scatter x1, waiting for transfers between devices, local(): lax.psum_scatter(d_w_key, ('dp', 'seq'), scatter_dimension=0, tiled=True)  119 us
  transfers between devices with their start and end apart: 13, of which 11 were waited for; matrix products, arithmetic and copies ran while one was open for 4% of the time, Pallas kernels for 0%

commit v1 on v0

v1 whole, which is shorter than its diff:
```python
import math

import jax
import jax.numpy as jnp
from jax import lax
from jax.experimental import pallas as pl
from jax.experimental.pallas import tpu as pltpu
from jax.sharding import PartitionSpec as P

HEADS = 16
HEAD = 128
REPOS = 4
BF = jnp.bfloat16
F32 = jnp.float32

norm_epsilon = 1e-05


def normalize(values, gain, offset):
    centre = jnp.mean(values, axis=-1, keepdims=True)
    shifted = values - centre
    inverse = lax.rsqrt(jnp.mean(shifted * shifted, axis=-1, keepdims=True) + norm_epsilon)
    normed = shifted * inverse
    return (normed * gain + offset, normed, inverse)


def normalize_back(grad_in, normed, inverse, gain):
    scaled = grad_in * gain
    first_mean = jnp.mean(scaled, axis=-1, keepdims=True)
    second_mean = jnp.mean(scaled * normed, axis=-1, keepdims=True)
    grad_values = inverse * (scaled - first_mean - normed * second_mean)
    return (grad_values, jnp.sum(grad_in * normed, axis=0), jnp.sum(grad_in, axis=0))


def gelu_tanh(values):
    return jax.nn.gelu(values, approximate=True)


def after(value, other):
    return lax.optimization_barrier((value, other))[0]


def dot32(left, right):
    return jnp.dot(left, right, preferred_element_type=F32)


def dot_t(left, right):
    return lax.dot_general(left, right, (((1,), (1,)), ((), ())), preferred_element_type=F32)


def t_dot(left, right):
    return lax.dot_general(left, right, (((0,), (0,)), ((), ())), preferred_element_type=F32)


class Ring:
    def __init__(self, dp, seq):
        self.nd, self.ns = dp, seq
        self.me = lax.axis_index("dp")
        self.z = lax.axis_index("seq")
        self.order = list(range(0, dp, 2)) + list(range(1, dp, 2))
        self.owners = [self.me ^ k for k in self.order]

    def swap(self, value, mask):
        return lax.ppermute(value, "dp", [(i, i ^ mask) for i in range(self.nd)])

    def up(self, value, by=1):
        return lax.ppermute(value, "seq", [(i, (i + by) % self.ns) for i in range(self.ns)])

    def back(self, step):
        return lax.rem(self.z - step + self.ns, self.ns)

    def seq_gather(self, block):
        pieces = [block]
        for _ in range(self.ns - 1):
            pieces.append(self.up(pieces[-1]))
        return pieces

    def seq_gather_near(self, block):
        return [block] + [self.up(block, step) for step in range(1, self.ns)]

    def seq_place(self, pieces, axis=0):
        shape = pieces[0].shape
        full = jnp.zeros(shape[:axis] + (self.ns,) + shape[axis:], pieces[0].dtype)
        for step, piece in enumerate(pieces):
            full = lax.dynamic_update_slice_in_dim(
                full, jnp.expand_dims(piece, axis), self.back(step), axis
            )
        return full

    def seq_scatter(self, part):
        total = part(self.back(1))
        for step in range(2, self.ns + 1):
            total = self.up(total.astype(BF)).astype(F32) + part(self.back(step))
        return total

    def seq_scatter_near(self, part):
        total = part(self.z)
        for step in range(1, self.ns):
            owner = lax.rem(self.z + step, self.ns)
            total = total + self.up(part(owner).astype(BF), step).astype(F32)
        return total

    def dp_gather(self, block):
        if self.nd == 8:
            half = block.shape[0] // 2
            over_x = self.swap(block, 2)
            over_y = self.swap(block, 4)
            first = self.swap(over_x[:half], 4)
            second = self.swap(over_y[half:], 2)
            even = [block, over_x, over_y, first, second]
        else:
            pieces = {0: block}
            bit = 2
            while bit < self.nd:
                for k in list(pieces):
                    pieces[k | bit] = self.swap(pieces[k], bit)
                bit *= 2
            even = [pieces[k] for k in range(0, self.nd, 2)]
        even = jnp.concatenate(even, axis=0)
        return even, self.swap(even, 1)

    def dp_scatter(self, even, odd):
        held = even.astype(F32) + self.swap(odd.astype(BF), 1).astype(F32)
        rows = held.shape[0] * 2 // self.nd
        if self.nd == 8:
            half = rows // 2
            low = self.swap(held[3 * rows : 3 * rows + half].astype(BF), 4).astype(F32)
            high = self.swap(held[3 * rows + half :].astype(BF), 2).astype(F32)
            to_x = jnp.concatenate(
                [held[rows : rows + half] + low, held[rows + half : 2 * rows]], axis=0
            )
            to_y = jnp.concatenate(
                [held[2 * rows : 2 * rows + half], held[2 * rows + half : 3 * rows] + high], axis=0
            )
            return (
                held[:rows]
                + self.swap(to_x.astype(BF), 2).astype(F32)
                + self.swap(to_y.astype(BF), 4).astype(F32)
            )
        bit = self.nd // 2
        while bit > 1:
            cut = held.shape[0] // 2
            held = held[:cut] + self.swap(held[cut:].astype(BF), bit).astype(F32)
            bit //= 2
        return held

    def relative(self, value):
        size = value.shape[-1] // self.nd
        return jnp.concatenate(
            [
                lax.dynamic_slice_in_dim(value, owner * size, size, value.ndim - 1)
                for owner in self.owners
            ],
            axis=-1,
        )

    def natural(self, value):
        size = value.shape[-1] // self.nd
        at = []
        for place in range(self.nd):
            mask = self.me ^ place
            at.append(lax.shift_right_logical(mask, 1) + (mask & 1) * (self.nd // 2))
        return jnp.concatenate(
            [lax.dynamic_slice_in_dim(value, a * size, size, value.ndim - 1) for a in at], axis=-1
        )


LOG2E = 1.4426950408889634


def attend_kernel(info, query, key, value_t, valid, out, log_total, *, heads, scale):
    keys = key.shape[0]
    rows = query.shape[0]
    place = lax.broadcasted_iota(jnp.int32, (keys, rows), 1) + info[0]
    allowed = lax.broadcasted_iota(jnp.int32, (keys, rows), 0) <= place
    for h in range(heads):
        cols = slice(h * HEAD, (h + 1) * HEAD)
        scores = dot_t(key[...], query[:, cols]) * (scale * LOG2E)
        scores = jnp.where(allowed, scores, -1e30)
        top = jnp.max(scores, axis=0, keepdims=True)
        expo = jnp.exp2(scores - top)
        total = jnp.sum(expo, axis=0, keepdims=True)
        mixed = dot32(value_t[...], expo.astype(BF)) * (1.0 / total)
        out[:, cols] = (jnp.transpose(mixed) * valid[...]).astype(BF)
        log_total[h] = top + jnp.log2(total)


def attend(info, query, key, value_t, valid, pairs, scale):
    rows, width = query.shape
    keys = key.shape[0]
    heads = HEADS // pairs
    step = heads * HEAD
    whole = lambda k, info: (0, 0)
    return pl.pallas_call(
        lambda *refs: attend_kernel(*refs, heads=heads, scale=scale),
        grid_spec=pltpu.PrefetchScalarGridSpec(
            num_scalar_prefetch=1,
            grid=(pairs,),
            in_specs=[
                pl.BlockSpec((rows, step), lambda k, info: (0, info[1 + k])),
                pl.BlockSpec((keys, HEAD), whole),
                pl.BlockSpec((HEAD, keys), whole),
                pl.BlockSpec((rows, 1), whole),
            ],
            out_specs=[
                pl.BlockSpec((rows, step), lambda k, info: (0, k)),
                pl.BlockSpec((heads, 1, rows), lambda k, info: (k, 0, 0)),
            ],
        ),
        out_shape=[
            jax.ShapeDtypeStruct((rows, width), BF),
            jax.ShapeDtypeStruct((HEADS, 1, rows), F32),
        ],
        compiler_params=pltpu.CompilerParams(vmem_limit_bytes=48 * 1024 * 1024),
        cost_estimate=pl.CostEstimate(
            flops=4 * rows * width * keys,
            bytes_accessed=4 * rows * width,
            transcendentals=rows * HEADS * keys,
        ),
    )(info, query, key, value_t, valid)


def attend_back_kernel(
    info, query, grad, log_total, key, key_t, value, out, key_grad, value_grad, *, heads, scale
):
    keys = key.shape[0]
    rows = query.shape[0]
    place = lax.broadcasted_iota(jnp.int32, (keys, rows), 1) + info[0]
    allowed = lax.broadcasted_iota(jnp.int32, (keys, rows), 0) <= place

    @pl.when(pl.program_id(0) == 0)
    def _():
        key_grad[...] = jnp.zeros_like(key_grad)
        value_grad[...] = jnp.zeros_like(value_grad)

    for h in range(heads):
        cols = slice(h * HEAD, (h + 1) * HEAD)
        scores = dot_t(key[...], query[:, cols]) * (scale * LOG2E)
        scores = jnp.where(allowed, scores, -1e30)
        probs = jnp.exp2(scores - log_total[h])
        dprobs = dot_t(value[...], grad[:, cols])
        delta = jnp.sum(probs * dprobs, axis=0, keepdims=True)
        dscores = (probs * (dprobs - delta)).astype(BF)
        value_grad[...] += dot32(probs.astype(BF), grad[:, cols])
        key_grad[...] += dot32(dscores, query[:, cols]) * scale
        back = dot32(key_t[...], dscores) * scale
        out[:, cols] = jnp.transpose(back).astype(BF)


def attend_back(info, query, grad, log_total, key, key_t, value, pairs, scale):
    rows, width = query.shape
    keys = key.shape[0]
    heads = HEADS // pairs
    step = heads * HEAD
    whole = lambda k, info: (0, 0)
    natural = lambda k, info: (0, info[1 + k])
    return pl.pallas_call(
        lambda *refs: attend_back_kernel(*refs, heads=heads, scale=scale),
        grid_spec=pltpu.PrefetchScalarGridSpec(
            num_scalar_prefetch=1,
            grid=(pairs,),
            in_specs=[
                pl.BlockSpec((rows, step), natural),
                pl.BlockSpec((rows, step), lambda k, info: (0, k)),
                pl.BlockSpec((heads, 1, rows), lambda k, info: (k, 0, 0)),
                pl.BlockSpec((keys, HEAD), whole),
                pl.BlockSpec((HEAD, keys), whole),
                pl.BlockSpec((keys, HEAD), whole),
            ],
            out_specs=[
                pl.BlockSpec((rows, step), natural),
                pl.BlockSpec((keys, HEAD), whole),
                pl.BlockSpec((keys, HEAD), whole),
            ],
        ),
        out_shape=[
            jax.ShapeDtypeStruct((rows, width), BF),
            jax.ShapeDtypeStruct((keys, HEAD), F32),
            jax.ShapeDtypeStruct((keys, HEAD), F32),
        ],
        compiler_params=pltpu.CompilerParams(vmem_limit_bytes=48 * 1024 * 1024),
        cost_estimate=pl.CostEstimate(
            flops=10 * rows * width * keys,
            bytes_accessed=6 * rows * width,
            transcendentals=rows * HEADS * keys,
        ),
    )(info, query, grad, log_total, key, key_t, value)


def local(
    dp,
    seq,
    tokens,
    lengths,
    repos,
    ln1_gain,
    ln1_bias,
    w_query,
    b_query,
    w_key,
    w_value,
    b_value,
    w_out,
    b_out,
    ln2_gain,
    ln2_bias,
    w_fc,
    b_fc,
    w_proj,
    b_proj,
    grad_out,
):
    ring = Ring(dp, seq)
    me, z = ring.me, ring.z
    windows, span, width = tokens.shape
    rows = windows * span
    own = w_query.shape[0]
    block = own * seq
    hidden = w_fc.shape[1]
    part = hidden // dp
    piece = part // seq
    scale = 1.0 / math.sqrt(HEAD)
    kv_end = width + 2 * HEAD
    pairs = dp
    all_rows = dp * rows
    half_rows = all_rows // 2

    size_hi = lax.div(lengths, jnp.int32(64))
    columns = [
        ln1_gain[:, None],
        ln1_bias[:, None],
        b_query[:, None],
        b_out[:, None],
        ln2_gain[:, None],
        ln2_bias[:, None],
        b_proj[:, None],
        jnp.pad(b_value, (0, own - b_value.shape[0]))[:, None],
        jnp.broadcast_to(size_hi.astype(BF), (own,))[:, None],
        jnp.broadcast_to((lengths - 64 * size_hi).astype(BF), (own,))[:, None],
        jnp.broadcast_to(repos.astype(BF), (own,))[:, None],
        jnp.transpose(b_fc.reshape(-1, own)),
    ]
    n_plain = 11
    n_fc = b_fc.shape[0] // own
    vector_block = jnp.concatenate(columns, axis=1)
    vector_block = jnp.pad(vector_block, ((0, 0), (0, HEAD - vector_block.shape[1])))
    w_qkv = jnp.concatenate([w_query, w_key, w_value, vector_block], axis=1)

    qkv_z = ring.seq_gather(w_qkv)
    raw_even, raw_odd = ring.dp_gather(grad_out.reshape(rows, width))
    fc_turned = lax.all_to_all(
        w_fc.reshape(own, dp, part), "dp", split_axis=1, concat_axis=0, tiled=False
    ).reshape(dp * own, part)
    qkv_block = after(ring.seq_place(qkv_z).reshape(block, -1), raw_even)
    qkv_even, qkv_odd = ring.dp_gather(qkv_block)
    out_z = ring.seq_gather(after(w_out, qkv_z[-1]))
    out_block = after(ring.seq_place(out_z).reshape(block, -1), qkv_even)
    out_even, out_odd = ring.dp_gather(out_block)
    fc_z = ring.seq_gather(after(fc_turned, out_z[-1]))
    fc_all = ring.seq_place([p.reshape(dp, own, part) for p in fc_z], axis=1).reshape(width, part)
    proj_z = ring.seq_gather(after(w_proj, fc_z[-1]))
    proj_all = ring.seq_place(proj_z).reshape(part, width)

    vectors = jnp.transpose(
        jnp.concatenate([qkv_even[:, kv_end:], qkv_odd[:, kv_end:]], axis=0)
    ).astype(F32)
    g1, o1 = vectors[0], vectors[1]
    straight = ring.natural(vectors[:n_plain])
    bq, bo, g2, o2, bp = (straight[n] for n in range(2, 7))
    bv = straight[7].reshape(dp * seq, own)[:, : b_value.shape[0]].reshape(-1)
    heads_of = lambda n: straight[n].reshape(dp, block)[:, 0]
    all_lengths = heads_of(8) * 64.0 + heads_of(9)
    all_repos = heads_of(10)
    bf_own = jnp.transpose(
        vectors[n_plain : n_plain + n_fc, :block].reshape(n_fc, seq, own), (1, 0, 2)
    ).reshape(part)

    first_place = z * span
    places = first_place + jnp.arange(span, dtype=jnp.int32)
    same = (all_repos[None, :] == all_repos[:, None]).astype(F32)
    weights = jnp.sum(all_lengths) / (REPOS * jnp.sum(same * all_lengths[None, :], axis=1))
    rel_lengths = jnp.stack([all_lengths[o] for o in ring.owners])
    rel_weights = jnp.stack([weights[o] for o in ring.owners])
    all_valid = (places[None, :].astype(F32) < rel_lengths[:, None]).astype(F32)
    row_scale = (all_valid * rel_weights[:, None]).reshape(all_rows, 1)
    valid_rows = all_valid[0].reshape(rows, 1)

    two_even = (raw_even.astype(F32) * row_scale[:half_rows]).astype(BF)
    two_odd = (raw_odd.astype(F32) * row_scale[half_rows:]).astype(BF)
    two_all = jnp.concatenate([two_even, two_odd], axis=0)
    grad_top = grad_out.reshape(rows, width).astype(F32) * row_scale[:rows]
    d_b_proj = jnp.sum(grad_top.astype(BF).astype(F32), axis=0)

    token_rows = tokens.reshape(rows, width)
    normed1_out, normed1, inverse1 = normalize(ring.relative(token_rows).astype(F32), g1, o1)
    attn_in = normed1_out.astype(BF)
    cut = width // 2
    qkv = dot32(attn_in[:, :cut], qkv_even) + dot32(attn_in[:, cut:], qkv_odd)
    query_low = (qkv[:, :width] + bq).astype(BF)
    kv_low = jnp.concatenate(
        [qkv[:, width : width + HEAD], qkv[:, width + HEAD : kv_end] + bv], axis=1
    ).astype(BF)
    kv_all = ring.seq_place(ring.seq_gather_near(kv_low)).reshape(seq * span, 2 * HEAD)
    key_all, value_all = kv_all[:, :HEAD], kv_all[:, HEAD:]
    info = jnp.stack([first_place] + ring.owners)
    attn_low, log_total = attend(
        info, query_low, key_all, jnp.transpose(value_all), valid_rows, pairs, scale
    )
    hidden_one = (
        token_rows.astype(F32)
        + dot32(attn_low[:, :cut], out_even)
        + dot32(attn_low[:, cut:], out_odd)
        + bo
    )

    normed2_out, normed2, inverse2 = normalize(hidden_one, g2, o2)
    mlp_even, mlp_odd = ring.dp_gather(normed2_out.astype(BF))
    mlp_all = jnp.concatenate([mlp_even, mlp_odd], axis=0)
    pre_act = dot32(mlp_all, fc_all) + bf_own
    act_low = gelu_tanh(pre_act).astype(BF)
    d_w_proj = ring.seq_scatter(
        lambda owner: t_dot(
            lax.dynamic_slice(act_low, (0, owner * piece), (all_rows, piece)), two_all
        )
    )
    grad_act = dot_t(two_all, proj_all)
    gelu_pull = jax.vjp(gelu_tanh, pre_act)[1]
    grad_pre = gelu_pull(grad_act)[0].astype(BF)
    d_b_fc = jnp.sum(grad_pre.astype(F32), axis=0)
    grad_mlp_odd = dot_t(grad_pre[half_rows:], fc_all).astype(BF)
    grad_mlp_even = dot_t(grad_pre[:half_rows], fc_all)
    grad_mlp_in = ring.dp_scatter(grad_mlp_even, grad_mlp_odd)
    branch_odd = dot32(act_low[half_rows:], after(proj_all, grad_mlp_in)).astype(BF)
    branch_even = dot32(act_low[:half_rows], proj_all)
    branch_two = ring.dp_scatter(branch_even, branch_odd)
    output = (hidden_one + branch_two + bp).astype(BF).reshape(windows, span, width)
    d_fc = t_dot(mlp_all, after(grad_pre, d_w_proj)).reshape(dp, seq, own, part)
    fc_share = ring.seq_scatter(
        lambda owner: lax.dynamic_slice_in_dim(d_fc, owner, 1, 1).reshape(dp, own, part)
    )
    d_w_fc = (
        lax.all_to_all(fc_share.astype(BF), "dp", split_axis=0, concat_axis=1, tiled=False)
        .reshape(own, hidden)
        .astype(F32)
    )

    grad_norm2, d_g2, d_o2 = normalize_back(grad_mlp_in, normed2, inverse2, g2)
    grad_mid = grad_top + grad_norm2
    grad_one = grad_mid.astype(BF)
    d_b_out = jnp.sum(grad_one.astype(F32), axis=0)

    def scatter_rows(even, odd):
        share = ring.dp_scatter(even, odd)
        return ring.seq_scatter(lambda owner: lax.dynamic_slice_in_dim(share, owner * own, own, 0))

    d_w_out = scatter_rows(
        t_dot(attn_low[:, :cut], grad_one), t_dot(attn_low[:, cut:], grad_one).astype(BF)
    )
    grad_att = jnp.concatenate([dot_t(grad_one, out_even), dot_t(grad_one, out_odd)], axis=1)
    grad_att = (grad_att * valid_rows).astype(BF)
    query_grad, key_grad, value_grad = attend_back(
        info, query_low, grad_att, log_total, key_all, jnp.transpose(key_all), value_all, pairs, scale
    )
    kv_grads = jnp.concatenate([key_grad, value_grad], axis=1).reshape(seq, rows, 2 * HEAD)
    kv_grad = ring.seq_scatter_near(
        lambda owner: lax.dynamic_slice_in_dim(kv_grads, owner, 1, 0)[0]
    ).astype(BF)
    qkv_grad = jnp.concatenate([query_grad, kv_grad], axis=1)
    grad_attn_in = jnp.concatenate(
        [dot_t(qkv_grad, qkv_even[:, :kv_end]), dot_t(qkv_grad, qkv_odd[:, :kv_end])], axis=1
    )
    grad_norm1, d_g1, d_o1 = normalize_back(grad_attn_in, normed1, inverse1, g1)
    grad_tokens = (grad_mid + ring.natural(grad_norm1)).astype(BF).reshape(windows, span, width)
    d_b_query = jnp.sum(query_grad.astype(F32), axis=0)
    d_b_value = jnp.sum(kv_grad[:, HEAD:].astype(F32), axis=0)

    d_bv = jnp.pad(
        d_b_value.reshape(dp * seq, -1), ((0, 0), (0, own - b_value.shape[0]))
    ).reshape(-1)
    straight = jnp.stack([d_b_query, d_b_out, d_g2, d_o2, d_b_proj, d_bv])
    d_bf = jnp.pad(
        jnp.transpose(d_b_fc.reshape(seq, n_fc, own), (1, 0, 2)).reshape(n_fc, block),
        ((0, 0), (0, width - block)),
    )
    vector_grads = jnp.concatenate([d_g1[None], d_o1[None], ring.relative(straight), d_bf], axis=0)
    vector_grads = jnp.transpose(jnp.pad(vector_grads, ((0, HEAD - 8 - n_fc), (0, 0))))
    d_qkv = scatter_rows(
        jnp.concatenate([t_dot(attn_in[:, :cut], qkv_grad), vector_grads[:cut]], axis=1),
        jnp.concatenate(
            [t_dot(attn_in[:, cut:], qkv_grad).astype(BF), vector_grads[cut:].astype(BF)], axis=1
        ),
    )
    small = jnp.transpose(d_qkv[:, kv_end : kv_end + 8 + n_fc])
    return (
        output,
        grad_tokens,
        small[0],
        small[1],
        d_qkv[:, :width],
        small[2],
        d_qkv[:, width : width + HEAD],
        d_qkv[:, width + HEAD : kv_end],
        small[7, : b_value.shape[0]],
        d_w_out,
        small[3],
        small[4],
        small[5],
        d_w_fc,
        small[8:].reshape(-1),
        d_w_proj,
        small[6],
    )


def solution(mesh):
    dp, seq = mesh.shape["dp"], mesh.shape["seq"]
    both = P(("dp", "seq"))
    rows = P(("dp", "seq"), None)
    token = P("dp", "seq", None)

    def run(*args):
        return local(dp, seq, *args)

    return jax.shard_map(
        run,
        mesh=mesh,
        in_specs=(
            token,
            P("dp"),
            P("dp"),
            both,
            both,
            rows,
            both,
            rows,
            rows,
            both,
            rows,
            both,
            both,
            both,
            rows,
            both,
            rows,
            both,
            token,
        ),
        out_specs=(
            token,
            token,
            both,
            both,
            rows,
            both,
            rows,
            rows,
            both,
            rows,
            both,
            both,
            both,
            rows,
            both,
            rows,
            both,
        ),
        check_vma=False,
    )
```

time: 4710 us -> 823 us (0.17)
  waiting for transfers between devices: 4060 us -> 351 us
  blocking collectives: 302 us -> 0 us
  matrix products: 242 us -> 152 us
  starting transfers between devices: 1.1 us -> 88.4 us
  local copies, waits for them, and re-layouts: 36.7 us -> 106 us
    reduce_scatter x8 -> x0, waiting for transfers between devices: 3840 us -> none  [the longest x1 1410 us: local(): lax.psum_scatter(d_w_proj, ('dp', 'seq'), scatter_dimension=0, tiled=True)]
    ppermute x0 -> x70, waiting for transfers between devices: none -> 339 us  [the longest x30 213 us: up(): lax.ppermute(value, 'seq', [(i, (i + by) % self.ns) for i in range(self.n...]
    all_gather x5 -> x0, blocking collectives: 247 us -> none  [the longest x1 81.3 us: local(): lax.all_gather(w_value, ('dp', 'seq'), axis=0, tiled=True)]
    all_gather x4 -> x0, waiting for transfers between devices: 193 us -> none  [the longest x1 179 us: local(): lax.all_gather(w_proj, ('dp', 'seq'), axis=0, tiled=True)]
    dot_general x46 -> x23, matrix products: 242 us -> 152 us  [the longest x7 54.9 us: dot_t(): lax.dot_general(left, right, (((1,), (1,)), ((), ())), preferred_element_...]
    ppermute x0 -> x70, starting transfers between devices: none -> 75.6 us  [the longest x40 51.6 us: swap(): return lax.ppermute(value, 'dp', [(i, i ^ mask) for i in range(self.nd)])]
  transfers between devices with their start and end apart: 13 -> 72, of which waited for: 11 -> 40; matrix products, arithmetic and copies ran while one was open for 4% -> 32% of each run, Pallas kernels for 0% -> 4%
where the time goes in v1:
time: 823 us; the launch traced here: 806 us
  waiting for transfers between devices  351 us (43%)
  matrix products  152 us (18%)
  local copies, waits for them, and re-layouts  106 us (13%)
  starting transfers between devices  88.4 us (11%)
  other arithmetic  71.5 us (9%)
  Pallas kernels  32.4 us (4%)
    ppermute x30, waiting for transfers between devices, up(): lax.ppermute(value, 'seq', [(i, (i + by) % self.ns) for i in range(self.n...  213 us
    ppermute x40, waiting for transfers between devices, swap(): return lax.ppermute(value, 'dp', [(i, i ^ mask) for i in range(self.nd)])  127 us
    dot_general x7, matrix products, dot_t(): lax.dot_general(left, right, (((1,), (1,)), ((), ())), preferred_element_...  54.9 us
    ppermute x40, starting transfers between devices, swap(): return lax.ppermute(value, 'dp', [(i, i ^ mask) for i in range(self.nd)])  51.6 us
    dot_general x9, matrix products, t_dot(): lax.dot_general(left, right, (((0,), (0,)), ((), ())), preferred_element_...  51.1 us
    dot_general x7, matrix products, dot32(): return jnp.dot(left, right, preferred_element_type=F32)  46.3 us
    unnamed x186, local copies, waits for them, and re-layouts  45.7 us
    ppermute x30, starting transfers between devices, up(): lax.ppermute(value, 'seq', [(i, (i + by) % self.ns) for i in range(self.n...  24 us
  transfers between devices with their start and end apart: 72, of which 40 were waited for; matrix products, arithmetic and copies ran while one was open for 32% of the time, Pallas kernels for 4%

profile of v1, /device:TPU:9, one launch (start us, length us, event | category | flops | bytes accessed | tf_op | source)
XLA Modules:
  0.0 806.4 jit_solution(2734375185572229128)
XLA Ops:
  46.3 8.4 %all-to-all-start = ((bf16[1,64,8,1024]{3,1,0,2:T(8,128)(2,1)}), bf16[1,64,8,1024]{3,1,0,2:T(8,128)(2,1)S(1)}, u32[]{:S(2)}, u32[]{:S(2)}) async-start(bf16[1,64,8,1024]{3,1,0,2:T(8,128)(2,1)} %copy.139), calls=%async_computation | async-start | bytes 2097152 | tf_op jit(solution)/shard_map/all_to_all | solution.py:351
  55.8 11.0 %collective-permute-done.8 = bf16[256,2432]{1,0:T(8,128)(2,1)S(1)} collective-permute-done((bf16[256,2432]{1,0:T(8,128)(2,1)S(1)}, bf16[256,2432]{1,0:T(8,128)(2,1)S(1)}, u32[]{:S(2)}, u32[]{:S(2)}) %collective-permute-start.8) | collective-permute-done | bytes 1245216 | tf_op jit(solution)/shard_map/ppermute | solution.py:64
  73.8 17.5 %collective-permute-done.9 = bf16[128,2432]{1,0:T(8,128)(2,1)S(1)} collective-permute-done((bf16[128,2432]{1,0:T(8,128)(2,1)S(1)}, bf16[128,2432]{1,0:T(8,128)(2,1)S(1)}, u32[]{:S(2)}, u32[]{:S(2)}) %collective-permute-start.9) | collective-permute-done | bytes 622624 | tf_op jit(solution)/shard_map/ppermute | solution.py:64
  101.7 6.7 collective-permute-done.16
  121.1 21.8 %collective-permute-done.28 = bf16[512,1024]{1,0:T(8,128)(2,1)} collective-permute-done((bf16[512,1024]{1,0:T(8,128)(2,1)S(1)}, bf16[512,1024]{1,0:T(8,128)(2,1)}, u32[]{:S(2)}, u32[]{:S(2)}) %collective-permute-start.28) | collective-permute-done | bytes 1048608 | tf_op jit(solution)/shard_map/ppermute | solution.py:67
  148.2 18.9 %collective-permute-done.29 = bf16[512,1024]{1,0:T(8,128)(2,1)} collective-permute-done((bf16[512,1024]{1,0:T(8,128)(2,1)}, bf16[512,1024]{1,0:T(8,128)(2,1)}, u32[]{:S(2)}, u32[]{:S(2)}) %collective-permute-start.29) | collective-permute-done | bytes 1048608 | tf_op jit(solution)/shard_map/ppermute | solution.py:67
  177.6 12.6 %collective-permute-done.30 = bf16[512,1024]{1,0:T(8,128)(2,1)S(1)} collective-permute-done((bf16[512,1024]{1,0:T(8,128)(2,1)}, bf16[512,1024]{1,0:T(8,128)(2,1)S(1)}, u32[]{:S(2)}, u32[]{:S(2)}) %collective-permute-start.30) | collective-permute-done | bytes 1048608 | tf_op jit(solution)/shard_map/ppermute | solution.py:67
  231.8 14.5 %shard_map.314 = (bf16[256,2048]{1,0:T(8,128)(2,1)S(1)}, f32[16,1,256]{2,1,0:T(1,128)S(1)}) custom-call(s32[9]{0:T(128)S(1)} %stack.63.refs_0_, bf16[256,2048]{1,0:T(8,128)(2,1)S(1)} %fusion.37.refs_1_, bf16[1024,128]{1,0:T(8,128)(2,1)S(1)} %get-tuple-element.119.refs_2_.refs_4_, bf16[128,1024]{1,0:T(8,128)(2,1)S(1)} %copy.137.refs_3_, ...), custom_call_target="tpu_custom_call" | custom-call | flops 2147483648 | bytes 2097152 | tf_op jit(solution)/shard_map/pallas_call | solution.py:194
  262.2 17.4 %collective-permute-done.24 = bf16[256,2048]{1,0:T(8,128)(2,1)S(1)} collective-permute-done((bf16[256,2048]{1,0:T(8,128)(2,1)S(1)}, bf16[256,2048]{1,0:T(8,128)(2,1)S(1)}, u32[]{:S(2)}, u32[]{:S(2)}) %collective-permute-start.24) | collective-permute-done | bytes 1048608 | tf_op jit(solution)/shard_map/ppermute | solution.py:64
  283.8 8.0 collective-permute-done.25
  301.3 22.4 %collective-permute-done.33 = bf16[256,2048]{1,0:T(8,128)(2,1)S(1)} collective-permute-done((bf16[256,2048]{1,0:T(8,128)(2,1)S(1)}, bf16[256,2048]{1,0:T(8,128)(2,1)S(1)}, u32[]{:S(2)}, u32[]{:S(2)}) %collective-permute-start.33) | collective-permute-done | bytes 1048608 | tf_op jit(solution)/shard_map/ppermute | solution.py:67
  348.1 13.4 %multiply_convert_fusion.2 = (bf16[2048,1024]{1,0:T(8,128)(2,1)}, f32[2048,1024]{1,0:T(8,128)}) fusion(f32[1024]{0:T(1024)S(1)} %add.564, bf16[2048,2048]{1,0:T(8,128)(2,1)S(1)} %constant_dynamic-update-slice_fusion.28, bf16[2048,1024]{1,0:T(8,128)(2,1)S(1)} %bitcast.243), kind=kOutput, calls=%fused_computation.17 | convolution fusion | flops 8610906112 | bytes 25169920 | tf_op jit(solution)/shard_map/dot_general | solution.py:44
  361.4 20.6 %convert_reduce_fusion = (f32[1024]{0:T(1024)S(1)}, bf16[2048,1024]{1,0:T(8,128)(2,1)}) fusion(f32[2048,1024]{1,0:T(8,128)} %get-tuple-element.158, f32[1024]{0:T(1024)S(1)} %add.564, bf16[1024,2048]{1,0:T(8,128)(2,1)} %bitcast.238, bf16[1024,2048]{1,0:T(8,128)(2,1)} %multiply_convert_fusion, bf16[1024,2048]{1,0:T(8,128)(2,1)} %multiply_convert_fusion.1), kind=kOutput, calls=%fused_computation.12 | convolution fusion | flops 8654945280 | bytes 25174016 | tf_op jit(solution)/shard_map/dot_general | solution.py:48
  382.0 9.3 %convolution_convert_fusion.3 = bf16[1024,2048]{1,0:T(8,128)(2,1)} fusion(bf16[2048,1024]{1,0:T(8,128)(2,1)} %bitcast.241, bf16[2048,1024]{1,0:T(8,128)(2,1)} %get-tuple-element.40), kind=kOutput, calls=%fused_computation.27 | convolution fusion | flops 4297064448 | bytes 10485760 | tf_op jit(solution)/shard_map/dot_general | solution.py:48
  392.7 7.1 collective-permute-done.35
  399.8 8.7 %fusion.110 = (bf16[1024,2048]{1,0:T(8,128)(2,1)S(1)}, f32[1024,2048]{1,0:T(8,128)S(1)}) fusion(bf16[1024,2048]{1,0:T(8,128)(2,1)} %collective-permute-done.35, bf16[2048,1024]{1,0:T(8,128)(2,1)} %bitcast.242, bf16[2048,1024]{1,0:T(8,128)(2,1)} %get-tuple-element.40), kind=kOutput, calls=%fused_computation.329 | convolution fusion | flops 4301258752 | bytes 23068672 | tf_op jit(solution)/shard_map/dot_general | solution.py:48
  426.5 18.7 %collective-permute-done.64 = bf16[256,2048]{1,0:T(8,128)(2,1)} collective-permute-done((bf16[256,2048]{1,0:T(8,128)(2,1)}, bf16[256,2048]{1,0:T(8,128)(2,1)}, u32[]{:S(2)}, u32[]{:S(2)}) %collective-permute-start.64) | collective-permute-done | bytes 1048608 | tf_op jit(solution)/shard_map/ppermute | solution.py:67
  463.7 13.5 %collective-permute-done.65 = bf16[256,2048]{1,0:T(8,128)(2,1)S(1)} collective-permute-done((bf16[256,2048]{1,0:T(8,128)(2,1)S(1)}, bf16[256,2048]{1,0:T(8,128)(2,1)S(1)}, u32[]{:S(2)}, u32[]{:S(2)}) %collective-permute-start.65) | collective-permute-done | bytes 1048608 | tf_op jit(solution)/shard_map/ppermute | solution.py:67
  480.7 24.5 %collective-permute-done.66 = bf16[256,2048]{1,0:T(8,128)(2,1)S(1)} collective-permute-done((bf16[256,2048]{1,0:T(8,128)(2,1)}, bf16[256,2048]{1,0:T(8,128)(2,1)S(1)}, u32[]{:S(2)}, u32[]{:S(2)}) %collective-permute-start.66) | collective-permute-done | bytes 1048608 | tf_op jit(solution)/shard_map/ppermute | solution.py:67
  505.2 7.5 convert_add_fusion.3
  512.6 11.8 %fusion.116 = f32[2048,1024]{1,0:T(8,128)S(1)} fusion(bf16[2048,2048]{1,0:T(8,128)(2,1)} %copy-done.50, bf16[2048,1024]{1,0:T(8,128)(2,1)S(1)} %copy-done.65), kind=kOutput, calls=%fused_computation.336 | convolution fusion | flops 8589934592 | bytes 20971520 | tf_op jit(solution)/shard_map/dot_general | solution.py:52
  524.9 10.9 %fusion.111 = (bf16[1024,2048]{1,0:T(8,128)(2,1)}, f32[1024,2048]{1,0:T(8,128)S(1)}) fusion(bf16[1024,2048]{1,0:T(8,128)(2,1)} %collective-permute-done.40, bf16[1024,2048]{1,0:T(8,128)(2,1)S(1)} %bitcast.240, bf16[2048,1024]{1,0:T(8,128)(2,1)} %get-tuple-element.157), kind=kOutput, calls=%fused_computation.330 | convolution fusion | flops 4301258752 | bytes 23068672 | tf_op jit(solution)/shard_map/dot_general | solution.py:44
  540.4 7.8 collective-permute-done.67
  554.7 17.7 %collective-permute-done.68 = bf16[8,64,1024]{2,1,0:T(8,128)(2,1)} collective-permute-done((bf16[8,64,1024]{2,1,0:T(8,128)(2,1)}, bf16[8,64,1024]{2,1,0:T(8,128)(2,1)}, u32[]{:S(2)}, u32[]{:S(2)}) %collective-permute-start.68) | collective-permute-done | bytes 1048608 | tf_op jit(solution)/shard_map/ppermute | solution.py:67
  591.6 17.9 %shard_map.315 = (bf16[256,2048]{1,0:T(8,128)(2,1)S(1)}, f32[1024,128]{1,0:T(8,128)S(1)}, f32[1024,128]{1,0:T(8,128)S(1)}) custom-call(s32[9]{0:T(128)S(1)} %copy-done.7, bf16[256,2048]{1,0:T(8,128)(2,1)S(1)} %copy-done.3, bf16[256,2048]{1,0:T(8,128)(2,1)S(1)} %fusion.38.refs_2_, f32[16,1,256]{2,1,0:T(1,128)S(1)} %get-tuple-element.36.refs_3_, ...), custom_call_target="tpu_custom_call" | custom-call | flops 5368709120 | bytes 3145728 | tf_op jit(solution)/shard_map/pallas_call | solution.py:257
  653.6 11.9 %all-to-all-done.1 = bf16[8,64,1,1024]{3,1,2,0:T(8,128)(2,1)} async-done(((bf16[8,64,1,1024]{3,1,2,0:T(8,128)(2,1)}), bf16[8,64,1,1024]{3,1,2,0:T(8,128)(2,1)}, u32[]{:S(2)}, u32[]{:S(2)}) %all-to-all-start.1) | async-done | bytes 1048608 | tf_op jit(solution)/shard_map/all_to_all | solution.py:442
  680.4 6.8 fusion.112
  690.9 11.8 %fusion.99 = (bf16[1024,2432]{1,0:T(8,128)(2,1)}, f32[1024,2432]{1,0:T(8,128)}) fusion(bf16[1024,2432]{1,0:T(8,128)(2,1)} %collective-permute-done.48, f32[1024,128]{1,0:T(8,128)S(1)} %slice-done, f32[1024,2304]{1,0:T(8,128)} %fusion.73), kind=kLoop, calls=%fused_computation.319 | loop fusion | flops 9961472 | bytes 29884416 | tf_op jit(solution)/shard_map/convert.21
  709.9 9.1 %collective-permute-done.49 = bf16[128,2432]{1,0:T(8,128)(2,1)S(1)} collective-permute-done((bf16[128,2432]{1,0:T(8,128)(2,1)S(1)}, bf16[128,2432]{1,0:T(8,128)(2,1)S(1)}, u32[]{:S(2)}, u32[]{:S(2)}) %collective-permute-start.49) | collective-permute-done | bytes 622624 | tf_op jit(solution)/shard_map/ppermute | solution.py:64
  724.8 16.7 %collective-permute-done.60 = bf16[256,2048]{1,0:T(8,128)(2,1)S(1)} collective-permute-done((bf16[256,2048]{1,0:T(8,128)(2,1)S(1)}, bf16[256,2048]{1,0:T(8,128)(2,1)S(1)}, u32[]{:S(2)}, u32[]{:S(2)}) %collective-permute-start.60) | collective-permute-done | bytes 1048608 | tf_op jit(solution)/shard_map/ppermute | solution.py:64
  745.7 22.4 %collective-permute-done.52 = bf16[256,2432]{1,0:T(8,128)(2,1)S(1)} collective-permute-done((bf16[256,2432]{1,0:T(8,128)(2,1)S(1)}, bf16[256,2432]{1,0:T(8,128)(2,1)S(1)}, u32[]{:S(2)}, u32[]{:S(2)}) %collective-permute-start.52) | collective-permute-done | bytes 1245216 | tf_op jit(solution)/shard_map/ppermute | solution.py:64
  783.3 6.4 collective-permute-done.54
  (500 shorter events, 368.1 us)
Async XLA Ops:
  0.7 31.4 %collective-permute-start.4 = (bf16[256,2048]{1,0:T(8,128)(2,1)}, bf16[256,2048]{1,0:T(8,128)(2,1)S(1)}, u32[]{:S(2)}, u32[]{:S(2)}) collective-permute-start(bf16[256,2048]{1,0:T(8,128)(2,1)} %bitcast.234), channel_id=1, source_target_pairs={{0,16},{4,20},{8,24},{12,28},{16,0},{20,4},{24,8},{28,12},{1,17},{... | collective-permute-start | bytes 3145736 | tf_op jit(solution)/shard_map/ppermute | solution.py:64
  2.0 23.9 %collective-permute-start.3 = (bf16[256,2048]{1,0:T(8,128)(2,1)}, bf16[256,2048]{1,0:T(8,128)(2,1)S(1)}, u32[]{:S(2)}, u32[]{:S(2)}) collective-permute-start(bf16[256,2048]{1,0:T(8,128)(2,1)} %bitcast.235), channel_id=1, source_target_pairs={{0,8},{4,12},{8,0},{12,4},{16,24},{20,28},{24,16},{28,20},{1,9},{5... | collective-permute-start | bytes 3145736 | tf_op jit(solution)/shard_map/ppermute | solution.py:64
  42.8 24.1 %collective-permute-start.8 = (bf16[256,2432]{1,0:T(8,128)(2,1)S(1)}, bf16[256,2432]{1,0:T(8,128)(2,1)S(1)}, u32[]{:S(2)}, u32[]{:S(2)}) collective-permute-start(bf16[256,2432]{1,0:T(8,128)(2,1)S(1)} %bitcast.231), channel_id=1, source_target_pairs={{0,16},{4,20},{8,24},{12,28},{16,0},{20,4},{24,8},{28,12},{1,17},{... | collective-permute-start | bytes 3735560 | tf_op jit(solution)/shard_map/ppermute | solution.py:64
  43.0 24.9 %collective-permute-start.7 = (bf16[256,2432]{1,0:T(8,128)(2,1)S(1)}, bf16[256,2432]{1,0:T(8,128)(2,1)}, u32[]{:S(2)}, u32[]{:S(2)}) collective-permute-start(bf16[256,2432]{1,0:T(8,128)(2,1)S(1)} %bitcast.232), channel_id=1, source_target_pairs={{0,8},{4,12},{8,0},{12,4},{16,24},{20,28},{24,16},{28,20},{1,9},{5... | collective-permute-start | bytes 3735560 | tf_op jit(solution)/shard_map/ppermute | solution.py:64
  46.3 65.0 %all-to-all-start = ((bf16[1,64,8,1024]{3,1,0,2:T(8,128)(2,1)}), bf16[1,64,8,1024]{3,1,0,2:T(8,128)(2,1)S(1)}, u32[]{:S(2)}, u32[]{:S(2)}) async-start(bf16[1,64,8,1024]{3,1,0,2:T(8,128)(2,1)} %copy.139), calls=%async_computation | async-start | bytes 2097152 | tf_op jit(solution)/shard_map/all_to_all | solution.py:351
  54.7 44.2 %collective-permute-start.15 = (bf16[64,2048]{1,0:T(8,128)(2,1)}, bf16[64,2048]{1,0:T(8,128)(2,1)}, u32[]{:S(2)}, u32[]{:S(2)}) collective-permute-start(bf16[64,2048]{1,0:T(8,128)(2,1)} %param.29), channel_id=1, source_target_pairs={{0,1},{1,2},{2,3},{3,0},{4,5},{5,6},{6,7},{7,4},{8,9},{9,10},{10,1... | collective-permute-start | bytes 786440 | tf_op jit(solution)/shard_map/ppermute | solution.py:67
  66.9 25.5 %collective-permute-start.10 = (bf16[128,2432]{1,0:T(8,128)(2,1)S(1)}, bf16[128,2432]{1,0:T(8,128)(2,1)S(1)}, u32[]{:S(2)}, u32[]{:S(2)}) collective-permute-start(bf16[128,2432]{1,0:T(8,128)(2,1)S(1)} %slice.391), channel_id=1, source_target_pairs={{0,8},{4,12},{8,0},{12,4},{16,24},{20,28},{24,16},{28,20},{1,9},{5... | collective-permute-start | bytes 1867784 | tf_op jit(solution)/shard_map/ppermute | solution.py:64
  93.3 102.9 %collective-permute-start.11 = (bf16[1024,2432]{1,0:T(8,128)(2,1)}, bf16[1024,2432]{1,0:T(8,128)(2,1)}, u32[]{:S(2)}, u32[]{:S(2)}) collective-permute-start(bf16[1024,2432]{1,0:T(8,128)(2,1)} %constant_dynamic-update-slice_fusion.5), channel_id=1, source_target_pairs={{0,4},{4,0},{8,12},{12,8},{16,20},{20,16},{24,28},{28,24},{1,5},{5... | collective-permute-start | bytes 14942216 | tf_op jit(solution)/shard_map/ppermute | solution.py:64
  118.1 24.8 %collective-permute-start.28 = (bf16[512,1024]{1,0:T(8,128)(2,1)S(1)}, bf16[512,1024]{1,0:T(8,128)(2,1)}, u32[]{:S(2)}, u32[]{:S(2)}) collective-permute-start(bf16[512,1024]{1,0:T(8,128)(2,1)S(1)} %bitcast.236), channel_id=1, source_target_pairs={{0,1},{1,2},{2,3},{3,0},{4,5},{5,6},{6,7},{7,4},{8,9},{9,10},{10,1... | collective-permute-start | bytes 3145736 | tf_op jit(solution)/shard_map/ppermute | solution.py:67
  142.9 24.2 %collective-permute-start.29 = (bf16[512,1024]{1,0:T(8,128)(2,1)}, bf16[512,1024]{1,0:T(8,128)(2,1)}, u32[]{:S(2)}, u32[]{:S(2)}) collective-permute-start(bf16[512,1024]{1,0:T(8,128)(2,1)} %collective-permute-done.28), channel_id=1, source_target_pairs={{0,1},{1,2},{2,3},{3,0},{4,5},{5,6},{6,7},{7,4},{8,9},{9,10},{10,1... | collective-permute-start | bytes 3145736 | tf_op jit(solution)/shard_map/ppermute | solution.py:67
  146.4 24.2 %collective-permute-start.19 = (bf16[256,2048]{1,0:T(8,128)(2,1)S(1)}, bf16[256,2048]{1,0:T(8,128)(2,1)}, u32[]{:S(2)}, u32[]{:S(2)}) collective-permute-start(bf16[256,2048]{1,0:T(8,128)(2,1)S(1)} %bitcast.246), channel_id=1, source_target_pairs={{0,16},{4,20},{8,24},{12,28},{16,0},{20,4},{24,8},{28,12},{1,17},{... | collective-permute-start | bytes 3145736 | tf_op jit(solution)/shard_map/ppermute | solution.py:64
  190.3 71.8 %collective-permute-start.31 = (bf16[256,2048]{1,0:T(8,128)(2,1)}, bf16[256,2048]{1,0:T(8,128)(2,1)}, u32[]{:S(2)}, u32[]{:S(2)}) collective-permute-start(bf16[256,2048]{1,0:T(8,128)(2,1)} %param.35), channel_id=1, source_target_pairs={{0,1},{1,2},{2,3},{3,0},{4,5},{5,6},{6,7},{7,4},{8,9},{9,10},{10,1... | collective-permute-start | bytes 3145736 | tf_op jit(solution)/shard_map/ppermute | solution.py:67
  192.0 54.4 %collective-permute-start.22 = (bf16[1024,2048]{1,0:T(8,128)(2,1)}, bf16[1024,2048]{1,0:T(8,128)(2,1)}, u32[]{:S(2)}, u32[]{:S(2)}) collective-permute-start(bf16[1024,2048]{1,0:T(8,128)(2,1)} %constant_dynamic-update-slice_fusion.18), channel_id=1, source_target_pairs={{0,4},{4,0},{8,12},{12,8},{16,20},{20,16},{24,28},{28,24},{1,5},{5... | collective-permute-start | bytes 12582920 | tf_op jit(solution)/shard_map/ppermute | solution.py:64
  256.1 24.2 %collective-permute-start.23 = (bf16[256,2048]{1,0:T(8,128)(2,1)S(1)}, bf16[256,2048]{1,0:T(8,128)(2,1)S(1)}, u32[]{:S(2)}, u32[]{:S(2)}) collective-permute-start(bf16[256,2048]{1,0:T(8,128)(2,1)S(1)} %get-tuple-element.72), channel_id=1, source_target_pairs={{0,8},{4,12},{8,0},{12,4},{16,24},{20,28},{24,16},{28,20},{1,9},{5... | collective-permute-start | bytes 3145736 | tf_op jit(solution)/shard_map/ppermute | solution.py:64
  257.3 82.1 %collective-permute-start.34 = (bf16[1024,2048]{1,0:T(8,128)(2,1)}, bf16[1024,2048]{1,0:T(8,128)(2,1)}, u32[]{:S(2)}, u32[]{:S(2)}) collective-permute-start(bf16[1024,2048]{1,0:T(8,128)(2,1)} %constant_dynamic-update-slice_fusion), channel_id=1, source_target_pairs={{0,4},{4,0},{8,12},{12,8},{16,20},{20,16},{24,28},{28,24},{1,5},{5... | collective-permute-start | bytes 12582920 | tf_op jit(solution)/shard_map/ppermute | solution.py:64
  262.0 36.5 %collective-permute-start.32 = (bf16[256,2048]{1,0:T(8,128)(2,1)}, bf16[256,2048]{1,0:T(8,128)(2,1)S(1)}, u32[]{:S(2)}, u32[]{:S(2)}) collective-permute-start(bf16[256,2048]{1,0:T(8,128)(2,1)} %collective-permute-done.31), channel_id=1, source_target_pairs={{0,1},{1,2},{2,3},{3,0},{4,5},{5,6},{6,7},{7,4},{8,9},{9,10},{10,1... | collective-permute-start | bytes 3145736 | tf_op jit(solution)/shard_map/ppermute | solution.py:67
  293.7 50.9 %collective-permute-start.27 = (bf16[1024,2048]{1,0:T(8,128)(2,1)}, bf16[1024,2048]{1,0:T(8,128)(2,1)}, u32[]{:S(2)}, u32[]{:S(2)}) collective-permute-start(bf16[1024,2048]{1,0:T(8,128)(2,1)} %get-tuple-element.120), channel_id=1, source_target_pairs={{0,4},{4,0},{8,12},{12,8},{16,20},{20,16},{24,28},{28,24},{1,5},{5... | collective-permute-start | bytes 12582920 | tf_op jit(solution)/shard_map/ppermute | solution.py:64
  298.5 25.3 %collective-permute-start.33 = (bf16[256,2048]{1,0:T(8,128)(2,1)S(1)}, bf16[256,2048]{1,0:T(8,128)(2,1)S(1)}, u32[]{:S(2)}, u32[]{:S(2)}) collective-permute-start(bf16[256,2048]{1,0:T(8,128)(2,1)S(1)} %collective-permute-done.32), channel_id=1, source_target_pairs={{0,1},{1,2},{2,3},{3,0},{4,5},{5,6},{6,7},{7,4},{8,9},{9,10},{10,1... | collective-permute-start | bytes 3145736 | tf_op jit(solution)/shard_map/ppermute | solution.py:67
  418.4 26.8 %collective-permute-start.64 = (bf16[256,2048]{1,0:T(8,128)(2,1)}, bf16[256,2048]{1,0:T(8,128)(2,1)}, u32[]{:S(2)}, u32[]{:S(2)}) collective-permute-start(bf16[256,2048]{1,0:T(8,128)(2,1)} %convolution_convert_fusion.4), channel_id=1, source_target_pairs={{0,1},{1,2},{2,3},{3,0},{4,5},{5,6},{6,7},{7,4},{8,9},{9,10},{10,1... | collective-permute-start | bytes 3145736 | tf_op jit(solution)/shard_map/ppermute | solution.py:67
  423.9 28.1 %collective-permute-start.39 = (bf16[256,2048]{1,0:T(8,128)(2,1)}, bf16[256,2048]{1,0:T(8,128)(2,1)S(1)}, u32[]{:S(2)}, u32[]{:S(2)}) collective-permute-start(bf16[256,2048]{1,0:T(8,128)(2,1)} %pad_maximum_fusion.7), channel_id=1, source_target_pairs={{0,16},{4,20},{8,24},{12,28},{16,0},{20,4},{24,8},{28,12},{1,17},{... | collective-permute-start | bytes 3145736 | tf_op jit(solution)/shard_map/ppermute | solution.py:64
  425.6 26.5 %collective-permute-start.37 = (bf16[256,2048]{1,0:T(8,128)(2,1)}, bf16[256,2048]{1,0:T(8,128)(2,1)}, u32[]{:S(2)}, u32[]{:S(2)}) collective-permute-start(bf16[256,2048]{1,0:T(8,128)(2,1)} %pad_maximum_fusion.6), channel_id=1, source_target_pairs={{0,8},{4,12},{8,0},{12,4},{16,24},{20,28},{24,16},{28,20},{1,9},{5... | collective-permute-start | bytes 3145736 | tf_op jit(solution)/shard_map/ppermute | solution.py:64
  451.6 25.7 %collective-permute-start.65 = (bf16[256,2048]{1,0:T(8,128)(2,1)S(1)}, bf16[256,2048]{1,0:T(8,128)(2,1)S(1)}, u32[]{:S(2)}, u32[]{:S(2)}) collective-permute-start(bf16[256,2048]{1,0:T(8,128)(2,1)S(1)} %add_convert_fusion.1), channel_id=1, source_target_pairs={{0,1},{1,2},{2,3},{3,0},{4,5},{5,6},{6,7},{7,4},{8,9},{9,10},{10,1... | collective-permute-start | bytes 3145736 | tf_op jit(solution)/shard_map/ppermute | solution.py:67
  462.8 62.0 %collective-permute-start.40 = (bf16[1024,2048]{1,0:T(8,128)(2,1)}, bf16[1024,2048]{1,0:T(8,128)(2,1)}, u32[]{:S(2)}, u32[]{:S(2)}) collective-permute-start(bf16[1024,2048]{1,0:T(8,128)(2,1)} %convolution_convert_fusion.2), channel_id=1, source_target_pairs={{0,4},{4,0},{8,12},{12,8},{16,20},{20,16},{24,28},{28,24},{1,5},{5... | collective-permute-start | bytes 12582920 | tf_op jit(solution)/shard_map/ppermute | solution.py:64
  480.7 24.5 %collective-permute-start.66 = (bf16[256,2048]{1,0:T(8,128)(2,1)}, bf16[256,2048]{1,0:T(8,128)(2,1)S(1)}, u32[]{:S(2)}, u32[]{:S(2)}) collective-permute-start(bf16[256,2048]{1,0:T(8,128)(2,1)} %add_convert_fusion), channel_id=1, source_target_pairs={{0,1},{1,2},{2,3},{3,0},{4,5},{5,6},{6,7},{7,4},{8,9},{9,10},{10,1... | collective-permute-start | bytes 3145736 | tf_op jit(solution)/shard_map/ppermute | solution.py:67
  575.6 70.3 %collective-permute-start.69 = (bf16[8,64,1024]{2,1,0:T(8,128)(2,1)}, bf16[8,64,1024]{2,1,0:T(8,128)(2,1)}, u32[]{:S(2)}, u32[]{:S(2)}) collective-permute-start(bf16[8,64,1024]{2,1,0:T(8,128)(2,1)} %fusion.40), channel_id=1, source_target_pairs={{0,1},{1,2},{2,3},{3,0},{4,5},{5,6},{6,7},{7,4},{8,9},{9,10},{10,1... | collective-permute-start | bytes 3145736 | tf_op jit(solution)/shard_map/ppermute | solution.py:67
  616.4 64.0 %collective-permute-start.56 = (bf16[1024,2048]{1,0:T(8,128)(2,1)}, bf16[1024,2048]{1,0:T(8,128)(2,1)}, u32[]{:S(2)}, u32[]{:S(2)}) collective-permute-start(bf16[1024,2048]{1,0:T(8,128)(2,1)} %convolution_convert_fusion.1), channel_id=1, source_target_pairs={{0,4},{4,0},{8,12},{12,8},{16,20},{20,16},{24,28},{28,24},{1,5},{5... | collective-permute-start | bytes 12582920 | tf_op jit(solution)/shard_map/ppermute | solution.py:64
  641.7 49.2 %collective-permute-start.48 = (bf16[1024,2432]{1,0:T(8,128)(2,1)}, bf16[1024,2432]{1,0:T(8,128)(2,1)}, u32[]{:S(2)}, u32[]{:S(2)}) collective-permute-start(bf16[1024,2432]{1,0:T(8,128)(2,1)} %pad_maximum_fusion.1), channel_id=1, source_target_pairs={{0,4},{4,0},{8,12},{12,8},{16,20},{20,16},{24,28},{28,24},{1,5},{5... | collective-permute-start | bytes 14942216 | tf_op jit(solution)/shard_map/ppermute | solution.py:64
  708.3 33.1 %collective-permute-start.60 = (bf16[256,2048]{1,0:T(8,128)(2,1)S(1)}, bf16[256,2048]{1,0:T(8,128)(2,1)S(1)}, u32[]{:S(2)}, u32[]{:S(2)}) collective-permute-start(bf16[256,2048]{1,0:T(8,128)(2,1)S(1)} %pad_maximum_fusion.12), channel_id=1, source_target_pairs={{0,16},{4,20},{8,24},{12,28},{16,0},{20,4},{24,8},{28,12},{1,17},{... | collective-permute-start | bytes 3145736 | tf_op jit(solution)/shard_map/ppermute | solution.py:64
  709.6 33.2 %collective-permute-start.58 = (bf16[256,2048]{1,0:T(8,128)(2,1)S(1)}, bf16[256,2048]{1,0:T(8,128)(2,1)S(1)}, u32[]{:S(2)}, u32[]{:S(2)}) collective-permute-start(bf16[256,2048]{1,0:T(8,128)(2,1)S(1)} %pad_maximum_fusion.11), channel_id=1, source_target_pairs={{0,8},{4,12},{8,0},{12,4},{16,24},{20,28},{24,16},{28,20},{1,9},{5... | collective-permute-start | bytes 3145736 | tf_op jit(solution)/shard_map/ppermute | solution.py:64
  720.7 47.5 %collective-permute-start.52 = (bf16[256,2432]{1,0:T(8,128)(2,1)S(1)}, bf16[256,2432]{1,0:T(8,128)(2,1)S(1)}, u32[]{:S(2)}, u32[]{:S(2)}) collective-permute-start(bf16[256,2432]{1,0:T(8,128)(2,1)S(1)} %pad_maximum_fusion.4), channel_id=1, source_target_pairs={{0,16},{4,20},{8,24},{12,28},{16,0},{20,4},{24,8},{28,12},{1,17},{... | collective-permute-start | bytes 3735560 | tf_op jit(solution)/shard_map/ppermute | solution.py:64
  721.1 48.4 %collective-permute-start.50 = (bf16[256,2432]{1,0:T(8,128)(2,1)S(1)}, bf16[256,2432]{1,0:T(8,128)(2,1)S(1)}, u32[]{:S(2)}, u32[]{:S(2)}) collective-permute-start(bf16[256,2432]{1,0:T(8,128)(2,1)S(1)} %pad_maximum_fusion.3), channel_id=1, source_target_pairs={{0,8},{4,12},{8,0},{12,4},{16,24},{20,28},{24,16},{28,20},{1,9},{5... | collective-permute-start | bytes 3735560 | tf_op jit(solution)/shard_map/ppermute | solution.py:64
  744.9 25.8 %collective-permute-start.61 = (bf16[64,2048]{1,0:T(8,128)(2,1)S(1)}, bf16[64,2048]{1,0:T(8,128)(2,1)S(1)}, u32[]{:S(2)}, u32[]{:S(2)}) collective-permute-start(bf16[64,2048]{1,0:T(8,128)(2,1)S(1)} %dynamic-slice_convert_fusion.1), channel_id=1, source_target_pairs={{0,1},{1,2},{2,3},{3,0},{4,5},{5,6},{6,7},{7,4},{8,9},{9,10},{10,1... | collective-permute-start | bytes 786440 | tf_op jit(solution)/shard_map/ppermute | solution.py:67
  (110 other events, 1824.1 us)

commit v2 on v1

v2 whole, which is shorter than its diff:
```python
import math

import jax
import jax.numpy as jnp
from jax import lax
from jax.experimental import pallas as pl
from jax.experimental.pallas import tpu as pltpu
from jax.sharding import PartitionSpec as P

HEADS = 16
HEAD = 128
REPOS = 4
BF = jnp.bfloat16
F32 = jnp.float32

norm_epsilon = 1e-05


def normed(values):
    centre = jnp.mean(values, axis=-1, keepdims=True)
    shifted = values - centre
    inverse = lax.rsqrt(jnp.mean(shifted * shifted, axis=-1, keepdims=True) + norm_epsilon)
    return shifted * inverse, inverse


def dot32(left, right):
    return jnp.dot(left, right, preferred_element_type=F32)


def dot_t(left, right):
    return lax.dot_general(left, right, (((1,), (1,)), ((), ())), preferred_element_type=F32)


def t_dot(left, right):
    return lax.dot_general(left, right, (((0,), (0,)), ((), ())), preferred_element_type=F32)


class Ring:
    def __init__(self, dp, seq):
        self.nd, self.ns = dp, seq
        self.me = lax.axis_index("dp")
        self.z = lax.axis_index("seq")
        self.order = list(range(0, dp, 2)) + list(range(1, dp, 2))
        self.owners = [self.me ^ k for k in self.order]

    def swap(self, value, mask):
        return lax.ppermute(value, "dp", [(i, i ^ mask) for i in range(self.nd)])

    def up(self, value, by=1):
        return lax.ppermute(value, "seq", [(i, (i + by) % self.ns) for i in range(self.ns)])

    def back(self, step):
        return lax.rem(self.z - step + self.ns, self.ns)

    def seq_gather_near(self, block):
        return [block] + [self.up(block, step) for step in range(1, self.ns)]

    def seq_place(self, pieces, axis=0):
        shape = pieces[0].shape
        full = jnp.zeros(shape[:axis] + (self.ns,) + shape[axis:], pieces[0].dtype)
        for step, piece in enumerate(pieces):
            full = lax.dynamic_update_slice_in_dim(
                full, jnp.expand_dims(piece, axis), self.back(step), axis
            )
        return full

    def seq_scatter_near(self, part):
        total = part(self.z)
        for step in range(1, self.ns):
            owner = lax.rem(self.z + step, self.ns)
            total = total + self.up(part(owner).astype(BF), step).astype(F32)
        return total

    def cross(self, block):
        if self.nd == 8:
            return self.swap(block, 2), self.swap(block, 4)
        return ()

    def first(self, block, near):
        if self.nd == 8:
            three = (block,) + tuple(near)
            return three + tuple(self.swap(piece, 1) for piece in three)
        return ()

    def corner(self, block, near):
        if self.nd == 8:
            half = block.shape[0] // 2
            return self.swap(near[0][:half], 4), self.swap(near[1][half:], 2)
        pieces = {0: block}
        bit = 2
        while bit < self.nd:
            for k in list(pieces):
                pieces[k | bit] = self.swap(pieces[k], bit)
            bit *= 2
        return tuple(pieces[k] for k in range(0, self.nd, 2))

    def second(self, far):
        far = jnp.concatenate(far, axis=0)
        return far, self.swap(far, 1)

    def pieces(self, first, second):
        if self.nd == 8:
            return first[:3] + second[:1] + first[3:] + second[1:]
        return second

    def other(self, value):
        return self.swap(value, 1)

    def corner_sums(self, even, other):
        if self.nd != 8:
            return ()
        rows = even.shape[0] // 4
        at = 3 * rows
        half = rows // 2
        held = even[at:].astype(F32) + other[at:].astype(F32)
        return held[:half].astype(BF), held[half:].astype(BF)

    def send_corner(self, sums):
        if self.nd != 8:
            return ()
        return self.swap(sums[0], 4), self.swap(sums[1], 2)

    def cross_sums(self, even, other, far):
        if self.nd == 8:
            rows = even.shape[0] // 4
            half = rows // 2

            def held(start, size):
                return even[start : start + size].astype(F32) + other[start : start + size].astype(
                    F32
                )

            low, high = far
            to_x = jnp.concatenate(
                [
                    (held(rows, half) + low.astype(F32)).astype(BF),
                    held(rows + half, half).astype(BF),
                ],
                axis=0,
            )
            to_y = jnp.concatenate(
                [
                    held(2 * rows, half).astype(BF),
                    (held(2 * rows + half, half) + high.astype(F32)).astype(BF),
                ],
                axis=0,
            )
            return to_x, to_y
        held = even.astype(F32) + other.astype(F32)
        bit = self.nd // 2
        while bit > 2:
            cut = held.shape[0] // 2
            held = held[:cut] + self.swap(held[cut:].astype(BF), bit).astype(F32)
            bit //= 2
        return held.astype(BF), jnp.zeros_like(even[: even.shape[0] // (self.nd // 2)])

    def send_cross(self, sums):
        if self.nd == 8:
            return self.swap(sums[0], 2), self.swap(sums[1], 4)
        cut = sums[0].shape[0] // 2
        return self.swap(sums[0][cut:], 2), sums[0][:cut]

    def ends(self, even, other, near):
        if self.nd == 8:
            return even, other, near[0], near[1]
        nothing = jnp.zeros_like(near[0])
        return near[0], near[1], nothing, nothing

    def scatter_end(self, even, other, near):
        rows = even.shape[0] * 2 // self.nd
        return sum(part[:rows].astype(F32) for part in self.ends(even, other, near))


LOG2E = 1.4426950408889634


def attend_kernel(info, query, key, value_t, valid, out, log_total, *, heads, scale):
    keys = key.shape[0]
    rows = query.shape[0]
    place = lax.broadcasted_iota(jnp.int32, (keys, rows), 1) + info[0]
    allowed = lax.broadcasted_iota(jnp.int32, (keys, rows), 0) <= place
    for h in range(heads):
        cols = slice(h * HEAD, (h + 1) * HEAD)
        scores = dot_t(key[...], query[:, cols]) * (scale * LOG2E)
        scores = jnp.where(allowed, scores, -1e30)
        top = jnp.max(scores, axis=0, keepdims=True)
        expo = jnp.exp2(scores - top)
        total = jnp.sum(expo, axis=0, keepdims=True)
        mixed = dot32(value_t[...], expo.astype(BF)) * (1.0 / total)
        out[:, cols] = (jnp.transpose(mixed) * valid[...]).astype(BF)
        log_total[h] = top + jnp.log2(total)


def attend(info, query, key, value_t, valid, pairs, scale):
    rows, width = query.shape
    keys = key.shape[0]
    heads = HEADS // pairs
    step = heads * HEAD
    whole = lambda k, info: (0, 0)
    return pl.pallas_call(
        lambda *refs: attend_kernel(*refs, heads=heads, scale=scale),
        grid_spec=pltpu.PrefetchScalarGridSpec(
            num_scalar_prefetch=1,
            grid=(pairs,),
            in_specs=[
                pl.BlockSpec((rows, step), lambda k, info: (0, info[1 + k])),
                pl.BlockSpec((keys, HEAD), whole),
                pl.BlockSpec((HEAD, keys), whole),
                pl.BlockSpec((rows, 1), whole),
            ],
            out_specs=[
                pl.BlockSpec((rows, step), lambda k, info: (0, k)),
                pl.BlockSpec((heads, 1, rows), lambda k, info: (k, 0, 0)),
            ],
        ),
        out_shape=[
            jax.ShapeDtypeStruct((rows, width), BF),
            jax.ShapeDtypeStruct((HEADS, 1, rows), F32),
        ],
        compiler_params=pltpu.CompilerParams(vmem_limit_bytes=48 * 1024 * 1024),
        cost_estimate=cost(),
    )(info, query, key, value_t, valid)


def attend_back_kernel(
    info, query, grad, log_total, key, key_t, value, out, key_grad, value_grad, *, heads, scale
):
    keys = key.shape[0]
    rows = query.shape[0]
    place = lax.broadcasted_iota(jnp.int32, (keys, rows), 1) + info[0]
    allowed = lax.broadcasted_iota(jnp.int32, (keys, rows), 0) <= place

    @pl.when(pl.program_id(0) == 0)
    def _():
        key_grad[...] = jnp.zeros_like(key_grad)
        value_grad[...] = jnp.zeros_like(value_grad)

    for h in range(heads):
        cols = slice(h * HEAD, (h + 1) * HEAD)
        scores = dot_t(key[...], query[:, cols]) * (scale * LOG2E)
        scores = jnp.where(allowed, scores, -1e30)
        probs = jnp.exp2(scores - log_total[h])
        dprobs = dot_t(value[...], grad[:, cols])
        delta = jnp.sum(probs * dprobs, axis=0, keepdims=True)
        dscores = (probs * (dprobs - delta)).astype(BF)
        value_grad[...] += dot32(probs.astype(BF), grad[:, cols])
        key_grad[...] += dot32(dscores, query[:, cols]) * scale
        back = dot32(key_t[...], dscores) * scale
        out[:, cols] = jnp.transpose(back).astype(BF)


def attend_back(info, query, grad, log_total, key, key_t, value, pairs, scale):
    rows, width = query.shape
    keys = key.shape[0]
    heads = HEADS // pairs
    step = heads * HEAD
    whole = lambda k, info: (0, 0)
    natural = lambda k, info: (0, info[1 + k])
    return pl.pallas_call(
        lambda *refs: attend_back_kernel(*refs, heads=heads, scale=scale),
        grid_spec=pltpu.PrefetchScalarGridSpec(
            num_scalar_prefetch=1,
            grid=(pairs,),
            in_specs=[
                pl.BlockSpec((rows, step), natural),
                pl.BlockSpec((rows, step), lambda k, info: (0, k)),
                pl.BlockSpec((heads, 1, rows), lambda k, info: (k, 0, 0)),
                pl.BlockSpec((keys, HEAD), whole),
                pl.BlockSpec((HEAD, keys), whole),
                pl.BlockSpec((keys, HEAD), whole),
            ],
            out_specs=[
                pl.BlockSpec((rows, step), natural),
                pl.BlockSpec((keys, HEAD), whole),
                pl.BlockSpec((keys, HEAD), whole),
            ],
        ),
        out_shape=[
            jax.ShapeDtypeStruct((rows, width), BF),
            jax.ShapeDtypeStruct((keys, HEAD), F32),
            jax.ShapeDtypeStruct((keys, HEAD), F32),
        ],
        compiler_params=pltpu.CompilerParams(vmem_limit_bytes=48 * 1024 * 1024),
        cost_estimate=cost(),
    )(info, query, grad, log_total, key, key_t, value)


def fetches(gathered, weight, sems):
    return [
        pltpu.make_async_copy(gathered.at[n], weight.at[:, n], sems.at[n])
        for n in range(gathered.shape[0])
    ]


def row_copies(pieces, full, sems):
    copies = []
    at = 0
    for n, piece in enumerate(pieces):
        size = piece.shape[0]
        copies.append((at, pltpu.make_async_copy(piece, full.at[pl.ds(at, size)], sems.at[n])))
        at += size
    return copies


ROOT = math.sqrt(2.0 / math.pi)
CUBIC = 0.044715


def row_tile(rows):
    return math.gcd(rows, 512)


def by_row(i, *_):
    return (i, 0)


def by_column(i, *_):
    return (0, i)


def fixed(i, *_):
    return (0, 0)


IN_VMEM = pl.BlockSpec(memory_space=pltpu.VMEM)
IN_SMEM = pl.BlockSpec(memory_space=pltpu.SMEM)
ANYWHERE = pl.BlockSpec(memory_space=pl.ANY)


PARAMS = pltpu.CompilerParams(vmem_limit_bytes=54 * 1024 * 1024)


def cost(*_):
    return pl.CostEstimate(flops=1024, bytes_accessed=1024, transcendentals=0)


def columns_of(info, n, size):
    return pl.ds(pl.multiple_of(info[1 + n] * size, HEAD), size)


N_VECTORS = 16


def stack_rows(*lines):
    width = lines[0].shape[1]
    at = lax.broadcasted_iota(jnp.int32, (8, width), 0)
    rows = jnp.zeros((8, width), F32)
    for n, line in enumerate(lines):
        rows = jnp.where(at == n, line, rows)
    return rows


def vmem(shape, dtype):
    return pltpu.VMEM(shape, dtype)


def enter_call(info, tokens, pieces, dp, own, n_value):
    rows, width = tokens.shape
    block = width // dp
    wide = pieces[0].shape[1]
    kv_end = wide - HEAD
    count = len(pieces)

    def kernel(info, tokens, *refs):
        attn, query, kv, rel, nat, weight, sems = refs[count:]
        copies = row_copies(refs[:count], weight, sems)
        for _, copy in copies:
            copy.start()
        x = tokens[...].astype(F32)
        centre = jnp.mean(x, axis=-1, keepdims=True)
        x = x - centre
        inverse = lax.rsqrt(jnp.mean(x * x, axis=-1, keepdims=True) + norm_epsilon)
        for _, copy in copies:
            copy.wait()
        for n in range(dp):
            mine = slice(n * block, (n + 1) * block)
            place = columns_of(info, n, block)
            vectors = jnp.transpose(weight[mine, kv_end:].astype(F32))[:N_VECTORS]
            rel[:, mine] = vectors
            nat[:, place] = vectors
            x = tokens[:, place].astype(F32)
            attn[:, mine] = ((x - centre) * inverse * vectors[0:1] + vectors[1:2]).astype(BF)
        at = lax.broadcasted_iota(jnp.int32, (width, HEAD), 0)
        d = lax.broadcasted_iota(jnp.int32, (width, HEAD), 1)
        chosen = (at == lax.div(d, n_value) * own + lax.rem(d, n_value)).astype(BF)
        offset = dot32(nat[...].astype(BF), chosen)[7:8]
        both = dot32(attn[...], weight[:, width:kv_end])
        kv[:, :HEAD] = both[:, :HEAD].astype(BF)
        kv[:, HEAD:] = (both[:, HEAD:] + offset).astype(BF)
        for at in range(0, width, 512):
            mine = slice(at, at + 512)
            query[:, mine] = (dot32(attn[...], weight[:, mine]) + nat[2:3, mine]).astype(BF)

    return pl.pallas_call(
        kernel,
        name="enter",
        in_specs=[IN_SMEM, IN_VMEM] + [ANYWHERE] * count,
        out_specs=[IN_VMEM] * 5,
        scratch_shapes=[vmem((width, wide), BF), pltpu.SemaphoreType.DMA((count,))],
        out_shape=[
            jax.ShapeDtypeStruct((rows, width), BF),
            jax.ShapeDtypeStruct((rows, width), BF),
            jax.ShapeDtypeStruct((rows, 2 * HEAD), BF),
            jax.ShapeDtypeStruct((N_VECTORS, width), F32),
            jax.ShapeDtypeStruct((N_VECTORS, width), F32),
        ],
        compiler_params=PARAMS,
        cost_estimate=cost(2 * rows * width * kv_end, tokens, *pieces),
    )(info, tokens, *pieces)


def leave_call(attn, pieces, tokens, nat):
    rows, width = tokens.shape
    count = len(pieces)

    def kernel(attn, tokens, nat, *refs):
        hidden, mlp, weight, sems = refs[count:]
        copies = row_copies(refs[:count], weight, sems)
        for _, copy in copies:
            copy.start()
        for _, copy in copies:
            copy.wait()
        for at in range(0, width, 512):
            mine = slice(at, at + 512)
            hidden[:, mine] = (
                dot32(attn[...], weight[:, mine]) + tokens[:, mine].astype(F32) + nat[3:4, mine]
            )
        mlp[...] = (normed(hidden[...])[0] * nat[4:5] + nat[5:6]).astype(BF)

    return pl.pallas_call(
        kernel,
        name="leave",
        in_specs=[IN_VMEM] * 3 + [ANYWHERE] * count,
        out_specs=[IN_VMEM] * 2,
        scratch_shapes=[vmem((width, width), BF), pltpu.SemaphoreType.DMA((count,))],
        out_shape=[
            jax.ShapeDtypeStruct((rows, width), F32),
            jax.ShapeDtypeStruct((rows, width), BF),
        ],
        compiler_params=PARAMS,
        cost_estimate=cost(2 * rows * width * width, tokens, *pieces),
    )(attn, tokens, nat, *pieces)


def middle_call(grads, hidden, top, row_scale, valid, nat, pieces):
    rows, width = hidden.shape
    count = len(pieces)

    def kernel(g0, g1, g2, g3, hidden, top, scale, valid, nat, *refs):
        mid, one, sums, att, weight, sems = refs[count:]
        copies = row_copies(refs[:count], weight, sems)
        for _, copy in copies:
            copy.start()
        grad = (
            g0[...].astype(F32) + g1[...].astype(F32) + g2[...].astype(F32) + g3[...].astype(F32)
        )
        norm, inverse = normed(hidden[...])
        scaled = grad * nat[4:5]
        first = jnp.mean(scaled, axis=-1, keepdims=True)
        second = jnp.mean(scaled * norm, axis=-1, keepdims=True)
        grad_top = top[...].astype(F32) * scale[...]
        total = grad_top + inverse * (scaled - first - norm * second)
        mid[...] = total
        low = total.astype(BF)
        one[...] = low
        sums[...] = stack_rows(
            jnp.sum(low.astype(F32), axis=0, keepdims=True),
            jnp.sum(grad * norm, axis=0, keepdims=True),
            jnp.sum(grad, axis=0, keepdims=True),
            jnp.sum(grad_top.astype(BF).astype(F32), axis=0, keepdims=True),
        )
        for _, copy in copies:
            copy.wait()
        for at in range(0, width, 512):
            mine = slice(at, at + 512)
            att[:, mine] = (dot_t(one[...], weight[mine, :]) * valid[...]).astype(BF)

    return pl.pallas_call(
        kernel,
        name="middle",
        grid=(1,),
        in_specs=[pl.BlockSpec((rows, width), fixed)] * 4
        + [IN_VMEM] * 5
        + [ANYWHERE] * count,
        out_specs=[IN_VMEM] * 4,
        scratch_shapes=[vmem((width, width), BF), pltpu.SemaphoreType.DMA((count,))],
        out_shape=[
            jax.ShapeDtypeStruct((rows, width), F32),
            jax.ShapeDtypeStruct((rows, width), BF),
            jax.ShapeDtypeStruct((8, width), F32),
            jax.ShapeDtypeStruct((rows, width), BF),
        ],
        compiler_params=PARAMS,
        cost_estimate=cost(2 * rows * width * width, hidden, hidden, *pieces),
    )(*grads, hidden, top, row_scale, valid, nat, *pieces)


def last_call(
    info, query_grad, kv_grad, pieces, tokens, attn, rel, mid, sums, d_bf, dp, own, n_value
):
    rows, width = tokens.shape
    block = width // dp
    wide = pieces[0].shape[1]
    count = len(pieces)

    def kernel(info, query, kv, tokens, attn, rel, mid, sums, d_bf, *refs):
        out, small, weight, back, norm, line, sems = refs[count:]
        copies = row_copies(refs[:count], weight, sems)
        for _, copy in copies:
            copy.start()
        value, inverse = normed(tokens[...].astype(F32))
        norm[...] = value
        d_query = jnp.sum(query[...].astype(F32), axis=0, keepdims=True)
        d_value = jnp.sum(kv[:, HEAD:].astype(F32), axis=0, keepdims=True)
        d = lax.broadcasted_iota(jnp.int32, (HEAD, width), 0)
        at = lax.broadcasted_iota(jnp.int32, (HEAD, width), 1)
        chosen = (at == lax.div(d, n_value) * own + lax.rem(d, n_value)).astype(F32)
        spread = jnp.dot(
            jnp.broadcast_to(d_value, (8, HEAD)),
            chosen,
            preferred_element_type=F32,
            precision=lax.Precision.HIGHEST,
        )[:1]
        line[...] = stack_rows(d_query, spread)
        for _, copy in copies:
            copy.wait()
        first = jnp.zeros((rows, 1), F32)
        second = jnp.zeros((rows, 1), F32)
        for n in range(dp):
            mine = slice(n * block, (n + 1) * block)
            grad = dot_t(query[...], weight[mine, :width]) + dot_t(
                kv[...], weight[mine, width : width + 2 * HEAD]
            )
            back[:, mine] = grad
            scaled = grad * rel[0:1, mine]
            first += jnp.sum(scaled, axis=-1, keepdims=True)
            second += jnp.sum(scaled * norm[:, columns_of(info, n, block)], axis=-1, keepdims=True)
        first = first / width
        second = second / width
        for n in range(dp):
            place = columns_of(info, n, block)
            mine = slice(n * block, (n + 1) * block)
            value = norm[:, place]
            grad = back[:, mine]
            scaled = grad * rel[0:1, mine]
            out[:, place] = (mid[:, place] + inverse * (scaled - first - value * second)).astype(BF)
            top = stack_rows(
                jnp.sum(grad * value, axis=0, keepdims=True),
                jnp.sum(grad, axis=0, keepdims=True),
            )
            small[mine, : 2 * HEAD] = t_dot(attn[:, mine], kv[...]).astype(BF)
            low = d_bf[...] if n == 0 else jnp.zeros_like(d_bf[...])
            rows_out = jnp.concatenate(
                [top, sums[:, place], line[:, place], low, jnp.zeros((HEAD - 32, block), F32)]
            )
            small[mine, 2 * HEAD :] = jnp.transpose(rows_out).astype(BF)

    return pl.pallas_call(
        kernel,
        name="last",
        in_specs=[IN_SMEM] + [IN_VMEM] * 8 + [ANYWHERE] * count,
        out_specs=[IN_VMEM] * 2,
        scratch_shapes=[
            vmem((width, wide), BF),
            vmem((rows, width), F32),
            vmem((rows, width), F32),
            vmem((8, width), F32),
            pltpu.SemaphoreType.DMA((count,)),
        ],
        out_shape=[
            jax.ShapeDtypeStruct((rows, width), BF),
            jax.ShapeDtypeStruct((width, 3 * HEAD), BF),
        ],
        compiler_params=PARAMS,
        cost_estimate=cost(2 * rows * width * wide, tokens, mid, *pieces),
    )(info, query_grad, kv_grad, tokens, attn, rel, mid, sums, d_bf, *pieces)


def start_at_first(step, tile, copies):
    @pl.when(step == 0)
    def _():
        for _, copy in copies:
            copy.start()

    for at, copy in copies:
        pl.when(step == at // tile)(copy.wait)


def grad_act_call(pieces, row_scale, weight):
    rows, width = row_scale.shape[0], weight.shape[1]
    part = weight.shape[0]
    tile = row_tile(rows)
    count = len(pieces)

    def kernel(scale, weight, *refs):
        two, out, full, sems = refs[count:]
        step = pl.program_id(0)
        start_at_first(step, tile, row_copies(refs[:count], full, sems))
        raw = full[pl.ds(pl.multiple_of(step * tile, tile), tile), :]
        low = (raw.astype(F32) * scale[...]).astype(BF)
        two[...] = low
        out[...] = dot_t(low, weight[...]).astype(BF)

    return pl.pallas_call(
        kernel,
        name="grad_act",
        grid=(rows // tile,),
        in_specs=[pl.BlockSpec((tile, 1), by_row), pl.BlockSpec((part, width), fixed)]
        + [ANYWHERE] * count,
        out_specs=[pl.BlockSpec((tile, width), by_row), pl.BlockSpec((tile, part), by_row)],
        out_shape=[
            jax.ShapeDtypeStruct((rows, width), BF),
            jax.ShapeDtypeStruct((rows, part), BF),
        ],
        scratch_shapes=[vmem((rows, width), BF), pltpu.SemaphoreType.DMA((count,))],
        compiler_params=PARAMS,
        cost_estimate=cost(2 * rows * width * part, weight, *pieces, *pieces),
    )(row_scale, weight, *pieces)


def feed_call(pieces, offset, grad_act, gathered):
    rows = grad_act.shape[0]
    tile = row_tile(rows)
    count = len(pieces)
    seq, groups, own, part = gathered.shape
    width = seq * groups * own

    def kernel(offset, back, gathered, *refs):
        whole, act, pre, total, weight, full, sems, more = refs[count:]
        step = pl.program_id(0)

        @pl.when(step == 0)
        def _():
            for copy in fetches(gathered, weight, sems):
                copy.start()
            total[...] = jnp.zeros_like(total)

        start_at_first(step, tile, row_copies(refs[:count], full, more))

        @pl.when(step == 0)
        def _():
            for copy in fetches(gathered, weight, sems):
                copy.wait()

        rows_in = full[pl.ds(pl.multiple_of(step * tile, tile), tile), :]
        whole[...] = rows_in
        for at in range(0, part, 256):
            mine = slice(at, at + 256)
            v = dot32(rows_in, weight[:, :, :, mine].reshape(width, 256)) + offset[:, mine]
            square = v * v
            t = jnp.tanh(ROOT * v * (1.0 + CUBIC * square))
            up = 0.5 + 0.5 * t
            act[:, mine] = (v * up).astype(BF)
            slope = up + (0.5 * ROOT) * v * (1.0 - t * t) * (1.0 + (3.0 * CUBIC) * square)
            grad = (back[:, mine].astype(F32) * slope).astype(BF)
            pre[:, mine] = grad
            total[:, mine] += jnp.sum(grad.astype(F32), axis=0, keepdims=True)

    return pl.pallas_call(
        kernel,
        name="feed",
        grid=(rows // tile,),
        in_specs=[pl.BlockSpec((1, part), fixed), pl.BlockSpec((tile, part), by_row), ANYWHERE]
        + [ANYWHERE] * count,
        out_specs=[
            pl.BlockSpec((tile, width), by_row),
            pl.BlockSpec((tile, part), by_row),
            pl.BlockSpec((tile, part), by_row),
            pl.BlockSpec((1, part), fixed),
        ],
        out_shape=[
            jax.ShapeDtypeStruct((rows, width), BF),
            jax.ShapeDtypeStruct((rows, part), BF),
            jax.ShapeDtypeStruct((rows, part), BF),
            jax.ShapeDtypeStruct((1, part), F32),
        ],
        scratch_shapes=[
            vmem((groups, seq, own, part), BF),
            vmem((rows, width), BF),
            pltpu.SemaphoreType.DMA((seq,)),
            pltpu.SemaphoreType.DMA((count,)),
        ],
        compiler_params=PARAMS,
        cost_estimate=cost(2 * rows * width * part, gathered, grad_act, *pieces, *pieces),
    )(offset, grad_act, gathered, *pieces)


def grad_mlp_call(value, second_half, gathered):
    rows, part = value.shape[0] // 2, value.shape[1]
    tile = row_tile(rows)
    seq, groups, own, _ = gathered.shape
    width = seq * groups * own
    skip = rows // tile if second_half else 0

    def kernel(value, gathered, out, weight, sems):
        @pl.when(pl.program_id(0) == 0)
        def _():
            copies = fetches(gathered, weight, sems)
            for copy in copies:
                copy.start()
            for copy in copies:
                copy.wait()

        out[...] = dot_t(value[...], weight[...].reshape(width, part)).astype(BF)

    return pl.pallas_call(
        kernel,
        name="grad_mlp",
        grid=(rows // tile,),
        in_specs=[pl.BlockSpec((tile, part), lambda i: (i + skip, 0)), ANYWHERE],
        out_specs=pl.BlockSpec((tile, width), by_row),
        out_shape=jax.ShapeDtypeStruct((rows, width), BF),
        scratch_shapes=[vmem((groups, seq, own, part), BF), pltpu.SemaphoreType.DMA((seq,))],
        compiler_params=PARAMS,
        cost_estimate=cost(2 * rows * width * part, value, gathered),
    )(value, gathered)


def branch_call(value, second_half, weight):
    rows, part = value.shape[0] // 2, value.shape[1]
    width = weight.shape[1]
    tile = row_tile(rows)
    skip = rows // tile if second_half else 0

    def kernel(value, weight, out):
        out[...] = dot32(value[...], weight[...]).astype(BF)

    return pl.pallas_call(
        kernel,
        name="branch",
        grid=(rows // tile,),
        in_specs=[
            pl.BlockSpec((tile, part), lambda i: (i + skip, 0)),
            pl.BlockSpec((part, width), fixed),
        ],
        out_specs=pl.BlockSpec((tile, width), by_row),
        out_shape=jax.ShapeDtypeStruct((rows, width), BF),
        compiler_params=PARAMS,
        cost_estimate=cost(2 * rows * width * part, value, weight),
    )(value, weight)


def d_rows_call(left, second_half, right, dp):
    rows, width = right.shape
    blocks = dp // 2
    size = left.shape[1] // dp
    skip = blocks if second_half else 0

    def kernel(left, right, out):
        out[...] = t_dot(left[...], right[...]).astype(BF)

    return pl.pallas_call(
        kernel,
        name="d_rows",
        grid=(blocks,),
        in_specs=[
            pl.BlockSpec((rows, size), lambda i: (0, i + skip)),
            pl.BlockSpec((rows, width), fixed),
        ],
        out_specs=pl.BlockSpec((size, width), by_row),
        out_shape=jax.ShapeDtypeStruct((size * blocks, width), BF),
        compiler_params=PARAMS,
        cost_estimate=cost(),
    )(left, right)


def d_proj_call(act, two, seq):
    rows, part = act.shape
    width = two.shape[1]
    tile = max(part // seq, HEAD)

    def kernel(act, two, out):
        out[...] = t_dot(act[...], two[...]).astype(BF)

    return pl.pallas_call(
        kernel,
        name="d_proj",
        grid=(part // tile,),
        in_specs=[pl.BlockSpec((rows, tile), by_column), pl.BlockSpec((rows, width), fixed)],
        out_specs=pl.BlockSpec((tile, width), by_row),
        out_shape=jax.ShapeDtypeStruct((part, width), BF),
        compiler_params=PARAMS,
        cost_estimate=cost(2 * rows * width * part, act, two),
    )(act, two)


def d_fc_call(mlp, grad_pre, dp, seq):
    rows, width = mlp.shape
    part = grad_pre.shape[1]
    own = width // (dp * seq)
    tile = width // dp

    def kernel(mlp, grad, out):
        out[...] = t_dot(mlp[...], grad[...]).astype(BF).reshape(seq, 1, own, part)

    return pl.pallas_call(
        kernel,
        name="d_fc",
        grid=(dp,),
        in_specs=[pl.BlockSpec((rows, tile), by_column), pl.BlockSpec((rows, part), fixed)],
        out_specs=pl.BlockSpec((seq, 1, own, part), lambda i: (0, i, 0, 0)),
        out_shape=jax.ShapeDtypeStruct((seq, dp, own, part), BF),
        compiler_params=PARAMS,
        cost_estimate=cost(2 * rows * width * part, mlp, grad_pre),
    )(mlp, grad_pre)


def local(
    dp,
    seq,
    tokens,
    lengths,
    repos,
    ln1_gain,
    ln1_bias,
    w_query,
    b_query,
    w_key,
    w_value,
    b_value,
    w_out,
    b_out,
    ln2_gain,
    ln2_bias,
    w_fc,
    b_fc,
    w_proj,
    b_proj,
    grad_out,
):
    ring = Ring(dp, seq)
    me, z = ring.me, ring.z
    windows, span, width = tokens.shape
    rows = windows * span
    own = w_query.shape[0]
    block = own * seq
    hidden = w_fc.shape[1]
    part = hidden // dp
    piece = part // seq
    scale = 1.0 / math.sqrt(HEAD)
    kv_end = width + 2 * HEAD
    pairs = dp
    all_rows = dp * rows

    size_hi = lax.div(lengths, jnp.int32(64))
    columns = [
        ln1_gain[:, None],
        ln1_bias[:, None],
        b_query[:, None],
        b_out[:, None],
        ln2_gain[:, None],
        ln2_bias[:, None],
        b_proj[:, None],
        jnp.pad(b_value, (0, own - b_value.shape[0]))[:, None],
        jnp.broadcast_to(size_hi.astype(BF), (own,))[:, None],
        jnp.broadcast_to((lengths - 64 * size_hi).astype(BF), (own,))[:, None],
        jnp.broadcast_to(repos.astype(BF), (own,))[:, None],
        jnp.transpose(b_fc.reshape(-1, own)),
    ]
    n_plain = 11
    n_fc = b_fc.shape[0] // own
    vector_block = jnp.concatenate(columns, axis=1)
    vector_block = jnp.pad(vector_block, ((0, 0), (0, HEAD - vector_block.shape[1])))
    w_qkv = jnp.concatenate([w_query, w_key, w_value, vector_block], axis=1)

    token = jnp.zeros((), F32)

    def tick(*values):
        nonlocal token
        values, token = lax.optimization_barrier((values, token))
        return values

    first_place = z * span
    info = jnp.stack([first_place] + ring.owners)
    token_rows = tokens.reshape(rows, width)
    raw = grad_out.reshape(rows, width)
    n_value = b_value.shape[0]
    raw_near = ring.cross(raw)
    qkv_z = ring.seq_gather_near(w_qkv)
    qkv_z, w_out, raw, raw_near = tick(qkv_z, w_out, raw, raw_near)

    qkv_block = ring.seq_place(qkv_z).reshape(block, -1)
    qkv_near = ring.cross(qkv_block)
    out_z = ring.seq_gather_near(w_out)
    qkv_block, qkv_near, out_z, w_proj = tick(qkv_block, qkv_near, out_z, w_proj)
    proj_all = lax.all_gather(w_proj, "seq", axis=0, tiled=True)

    qkv_far = ring.corner(qkv_block, qkv_near)
    qkv_first = ring.first(qkv_block, qkv_near)
    out_block = ring.seq_place(out_z).reshape(block, -1)
    qkv_far, out_block, qkv_first = tick(qkv_far, out_block, qkv_first)

    qkv_second = ring.second(qkv_far)
    out_near = ring.cross(out_block)
    qkv_second, qkv_first = tick(qkv_second, qkv_first)
    qkv_all = ring.pieces(qkv_first, qkv_second)
    attn_in, query_low, kv_low, rel, nat = enter_call(info, token_rows, qkv_all, dp, own, n_value)
    kv_low, attn_in, query_low, rel, w_fc = tick(kv_low, attn_in, query_low, rel, w_fc)
    kv_z = ring.seq_gather_near(kv_low)
    fc_turned = lax.all_to_all(
        w_fc.reshape(own, dp, part), "dp", split_axis=1, concat_axis=0, tiled=False
    )

    all_lengths = (rel[8] * 64.0 + rel[9]).reshape(dp, block)[:, :1]
    all_repos = rel[10].reshape(dp, block)[:, :1]
    same = (all_repos == all_repos.reshape(1, dp)).astype(F32)
    weights = jnp.sum(all_lengths) / (
        REPOS * jnp.sum(same * all_lengths.reshape(1, dp), axis=1, keepdims=True)
    )
    places = (first_place + jnp.arange(span, dtype=jnp.int32)).astype(F32)
    all_valid = (places[None, :] < all_lengths).astype(F32)
    row_scale = (all_valid * weights).reshape(all_rows, 1)
    valid_rows = all_valid[0].reshape(rows, 1)
    bf_own = jnp.transpose(
        rel[n_plain : n_plain + n_fc, :block].reshape(n_fc, seq, own), (1, 0, 2)
    ).reshape(1, part)
    own_scale = row_scale[:rows]
    kv_z, raw, out_block, out_near, row_scale, own_scale, bf_own, fc_turned = tick(
        kv_z, raw, out_block, out_near, row_scale, own_scale, bf_own, fc_turned
    )
    fc_all = lax.all_gather(fc_turned.reshape(dp, own, part), "seq", axis=0, tiled=False)

    out_far = ring.corner(out_block, out_near)
    out_first = ring.first(out_block, out_near)
    kv_all = ring.seq_place(kv_z).reshape(seq * span, 2 * HEAD)
    key_all, value_all = kv_all[:, :HEAD], kv_all[:, HEAD:]
    attn_low, log_total = attend(
        info, query_low, key_all, jnp.transpose(value_all), valid_rows, pairs, scale
    )
    attn_low, raw, out_far, out_first = tick(attn_low, raw, out_far, out_first)
    out_second = ring.second(out_far)
    out_second, attn_low = tick(out_second, attn_low)
    raw_far = ring.corner(raw, raw_near)
    raw_first = ring.first(raw, raw_near)
    out_all = ring.pieces(out_first, out_second)
    hidden_one, mlp_own = leave_call(attn_low, out_all, token_rows, nat)
    mlp_own, raw_far, raw_first = tick(mlp_own, raw_far, raw_first)

    mlp_near = ring.cross(mlp_own)
    raw_second = ring.second(raw_far)
    raw_second, proj_all = tick(raw_second, proj_all)
    two_all, grad_act = grad_act_call(ring.pieces(raw_first, raw_second), row_scale, proj_all)
    mlp_own, two_all, grad_act, mlp_near = tick(mlp_own, two_all, grad_act, mlp_near)
    mlp_far = ring.corner(mlp_own, mlp_near)
    mlp_first = ring.first(mlp_own, mlp_near)
    mlp_far, mlp_first, fc_all = tick(mlp_far, mlp_first, fc_all)
    mlp_second = ring.second(mlp_far)
    mlp_second, fc_all = tick(mlp_second, fc_all)
    mlp_all, act_low, grad_pre, d_b_fc = feed_call(
        ring.pieces(mlp_first, mlp_second), bf_own, grad_act, fc_all
    )
    odd = grad_mlp_call(grad_pre, True, fc_all)
    odd, grad_pre = tick(odd, grad_pre)
    other = ring.other(odd)
    even = grad_mlp_call(grad_pre, False, fc_all)
    even, other = tick(even, other)
    corner = ring.corner_sums(even, other)
    corner, act_low = tick(corner, act_low)
    far = ring.send_corner(corner)
    branch_odd = branch_call(act_low, True, proj_all)
    far, branch_odd, act_low, grad_pre = tick(far, branch_odd, act_low, grad_pre)
    cross = ring.cross_sums(even, other, far)
    cross, act_low, grad_pre, branch_odd = tick(cross, act_low, grad_pre, branch_odd)
    near = ring.send_cross(cross)
    branch_other = ring.other(branch_odd)
    branch_even = branch_call(act_low, False, proj_all)
    d_fc = d_fc_call(mlp_all, grad_pre, dp, seq)
    near, branch_even, branch_other, d_fc = tick(near, branch_even, branch_other, d_fc)
    fc_share = lax.psum_scatter(d_fc, "seq", scatter_dimension=0, tiled=False)
    corner = ring.corner_sums(branch_even, branch_other)
    corner, near = tick(corner, near)

    branch_far = ring.send_corner(corner)
    d_bf = jnp.transpose(d_b_fc.reshape(seq, n_fc, own), (1, 0, 2)).reshape(n_fc, block)
    d_bf = jnp.pad(d_bf, ((0, 8 - n_fc), (0, 0)))
    grad_mid, grad_one, sums, grad_att = middle_call(
        ring.ends(even, other, near), hidden_one, raw, own_scale, valid_rows, nat, out_all
    )
    grad_att, grad_one, branch_far = tick(grad_att, grad_one, branch_far)
    cross = ring.cross_sums(branch_even, branch_other, branch_far)
    cross, grad_att = tick(cross, grad_att)
    branch_near = ring.send_cross(cross)
    query_grad, key_grad, value_grad = attend_back(
        info, query_low, grad_att, log_total, key_all, jnp.transpose(key_all), value_all, pairs, scale
    )
    d_q_odd = d_rows_call(attn_in, True, query_grad, dp)
    kv_grads = jnp.concatenate([key_grad, value_grad], axis=1).reshape(seq, rows, 2 * HEAD)
    kv_mine = lax.dynamic_slice_in_dim(kv_grads, z, 1, 0)[0]
    kv_sends = [
        lax.dynamic_slice_in_dim(kv_grads, lax.rem(z + step, seq), 1, 0)[0].astype(BF)
        for step in range(1, seq)
    ]
    query_grad, kv_mine, kv_sends, grad_one, d_q_odd, branch_near = tick(
        query_grad, kv_mine, kv_sends, grad_one, d_q_odd, branch_near
    )
    d_q_other = ring.other(d_q_odd)
    kv_parts = [ring.up(part, step + 1) for step, part in enumerate(kv_sends)]
    d_q_even = d_rows_call(attn_in, False, query_grad, dp)
    d_out_odd = d_rows_call(attn_low, True, grad_one, dp)
    d_q_other, d_q_even, d_out_odd, grad_one = tick(d_q_other, d_q_even, d_out_odd, grad_one)
    corner = ring.corner_sums(d_q_even, d_q_other)
    corner, act_low = tick(corner, act_low)
    q_far = ring.send_corner(corner)
    d_proj = d_proj_call(act_low, two_all, seq)
    q_far, d_proj, kv_parts, d_out_odd, grad_one, fc_share = tick(
        q_far, d_proj, kv_parts, d_out_odd, grad_one, fc_share
    )
    proj_share = lax.psum_scatter(d_proj, "seq", scatter_dimension=0, tiled=True)
    cross = ring.cross_sums(d_q_even, d_q_other, q_far)
    kv_grad = (kv_mine + sum(part.astype(F32) for part in kv_parts)).astype(BF)
    cross, kv_grad, d_out_odd, grad_one = tick(cross, kv_grad, d_out_odd, grad_one)
    q_near = ring.send_cross(cross)
    d_out_other = ring.other(d_out_odd)
    d_out_even = d_rows_call(attn_low, False, grad_one, dp)
    grad_rows, small = last_call(
        info,
        query_grad,
        kv_grad,
        qkv_all,
        token_rows,
        attn_in,
        rel,
        grad_mid,
        sums,
        d_bf,
        dp,
        own,
        n_value,
    )
    grad_tokens = grad_rows.reshape(windows, span, width)
    cut = width // 2
    out_corner = ring.corner_sums(d_out_even, d_out_other)
    small_odd = small[cut:]
    q_near, small, small_odd, out_corner = tick(q_near, small, small_odd, out_corner)
    out_far_back = ring.send_corner(out_corner)
    small_other = ring.other(small_odd)
    q_share = ring.scatter_end(d_q_even, d_q_other, q_near)
    branch_two = ring.scatter_end(branch_even, branch_other, branch_near)
    output = (hidden_one + branch_two + nat[6:7]).astype(BF).reshape(windows, span, width)
    out_far_back, q_share, small_other, output = tick(out_far_back, q_share, small_other, output)
    small_corner = ring.corner_sums(small[:cut], small_other)
    cross = ring.cross_sums(d_out_even, d_out_other, out_far_back)
    cross, small_corner, q_share = tick(cross, small_corner, q_share)
    small_far = ring.send_corner(small_corner)
    small_far, proj_share = tick(small_far, proj_share)
    out_near_back = ring.send_cross(cross)
    small_cross = ring.cross_sums(small[:cut], small_other, small_far)
    small_near = ring.send_cross(small_cross)
    d_w_query = ring.seq_scatter_near(
        lambda owner: lax.dynamic_slice_in_dim(q_share, owner * own, own, 0)
    )
    out_near_back, small_near, d_w_query, fc_share = tick(
        out_near_back, small_near, d_w_query, fc_share
    )
    out_share = ring.scatter_end(d_out_even, d_out_other, out_near_back)
    d_w_out = ring.seq_scatter_near(
        lambda owner: lax.dynamic_slice_in_dim(out_share, owner * own, own, 0)
    )
    small_share = ring.scatter_end(small[:cut], small_other, small_near)
    d_small = ring.seq_scatter_near(
        lambda owner: lax.dynamic_slice_in_dim(small_share, owner * own, own, 0)
    )
    d_w_proj = proj_share.astype(F32)
    d_w_fc = (
        lax.all_to_all(fc_share, "dp", split_axis=0, concat_axis=1, tiled=False)
        .reshape(own, hidden)
        .astype(F32)
    )
    vectors = jnp.transpose(d_small[:, 2 * HEAD :])
    return (
        output,
        grad_tokens,
        vectors[0],
        vectors[1],
        d_w_query,
        vectors[16],
        d_small[:, :HEAD],
        d_small[:, HEAD : 2 * HEAD],
        vectors[17, : b_value.shape[0]],
        d_w_out,
        vectors[8],
        vectors[9],
        vectors[10],
        d_w_fc,
        vectors[24 : 24 + n_fc].reshape(-1),
        d_w_proj,
        vectors[11],
    )


def solution(mesh):
    dp, seq = mesh.shape["dp"], mesh.shape["seq"]
    both = P(("dp", "seq"))
    rows = P(("dp", "seq"), None)
    token = P("dp", "seq", None)

    def run(*args):
        return local(dp, seq, *args)

    return jax.shard_map(
        run,
        mesh=mesh,
        in_specs=(
            token,
            P("dp"),
            P("dp"),
            both,
            both,
            rows,
            both,
            rows,
            rows,
            both,
            rows,
            both,
            both,
            both,
            rows,
            both,
            rows,
            both,
            token,
        ),
        out_specs=(
            token,
            token,
            both,
            both,
            rows,
            both,
            rows,
            rows,
            both,
            rows,
            both,
            both,
            both,
            rows,
            both,
            rows,
            both,
        ),
        check_vma=False,
    )
```

time: 823 us -> 586 us (0.71)
  waiting for transfers between devices: 351 us -> 182 us
  Pallas kernels: 32.4 us -> 198 us
  matrix products: 152 us -> 0 us
  local copies, waits for them, and re-layouts: 106 us -> 51.2 us
  other arithmetic: 71.5 us -> 49.4 us
  between operations: 4.33 us -> 16.6 us
  starting transfers between devices: 88.4 us -> 79.3 us
    pallas_call x0 -> x16, Pallas kernels: none -> 165 us  [the longest x1 22.1 us: feed_call(): pl.pallas_call(kernel, name='feed', grid=(rows // tile,), in_specs=[pl.Bl...]
    dot_general x23 -> x0, matrix products: 152 us -> none  [the longest x7 54.9 us: dot_t(): lax.dot_general(left, right, (((1,), (1,)), ((), ())), preferred_element_...]
    ppermute x30 -> x21, waiting for transfers between devices: 213 us -> 79.3 us  [up(): lax.ppermute(value, 'seq', [(i, (i + by) % self.ns) for i in range(self.n...]
    ppermute x40 -> x57, waiting for transfers between devices: 127 us -> 58.6 us  [swap(): return lax.ppermute(value, 'dp', [(i, i ^ mask) for i in range(self.nd)])]
    reduce_scatter x0 -> x2, waiting for transfers between devices: none -> 33.1 us  [the longest x1 33.1 us: local(): lax.psum_scatter(d_proj, 'seq', scatter_dimension=0, tiled=True)]
    unnamed x186 -> x92, local copies, waits for them, and re-layouts: 45.7 us -> 16 us
    reduce_sum x9 -> x1, other arithmetic: 12.2 us -> 0.18 us  [local(): jnp.sum(same * all_lengths.reshape(1, dp), axis=1, keepdims=True)]
    all_to_all x1, waiting for transfers between devices: 11.9 us -> 0.01 us  [local(): lax.all_to_all(fc_share, 'dp', split_axis=0, concat_axis=1, tiled=False)]
  transfers between devices with their start and end apart: 72 -> 84, of which waited for: 40 -> 30; matrix products, arithmetic and copies ran while one was open for 32% -> 14% of each run, Pallas kernels for 4% -> 29%
where the time goes in v2:
time: 586 us; the launch traced here: 577 us
  Pallas kernels  198 us (34%)
  waiting for transfers between devices  182 us (31%)
  starting transfers between devices  79.3 us (14%)
  local copies, waits for them, and re-layouts  51.2 us (9%)
  other arithmetic  49.4 us (8%)
  between operations  16.6 us (3%)
    ppermute x21, waiting for transfers between devices, up(): lax.ppermute(value, 'seq', [(i, (i + by) % self.ns) for i in range(self.n...  79.3 us
    ppermute x57, waiting for transfers between devices, swap(): return lax.ppermute(value, 'dp', [(i, i ^ mask) for i in range(self.nd)])  58.6 us
    ppermute x57, starting transfers between devices, swap(): return lax.ppermute(value, 'dp', [(i, i ^ mask) for i in range(self.nd)])  47.6 us
    reduce_scatter x1, waiting for transfers between devices, local(): lax.psum_scatter(d_proj, 'seq', scatter_dimension=0, tiled=True)  33.1 us
    pallas_call x1, Pallas kernels, feed_call(): pl.pallas_call(kernel, name='feed', grid=(rows // tile,), in_specs=[pl.Bl...  22.1 us
    pallas_call x4, Pallas kernels, d_rows_call(): pl.pallas_call(kernel, name='d_rows', grid=(blocks,), in_specs=[pl.BlockS...  20.6 us
    ppermute x21, starting transfers between devices, up(): lax.ppermute(value, 'seq', [(i, (i + by) % self.ns) for i in range(self.n...  20 us
    pallas_call x2, Pallas kernels, grad_mlp_call(): pl.pallas_call(kernel, name='grad_mlp', grid=(rows // tile,), in_specs=[p...  19.6 us
  transfers between devices with their start and end apart: 84, of which 30 were waited for; matrix products, arithmetic and copies ran while one was open for 14% of the time, Pallas kernels for 29%

profile of v2, /device:TPU:9, one launch (start us, length us, event | category | flops | bytes accessed | tf_op | source)
XLA Modules:
  0.0 576.9 jit_solution(7318816923825018989)
XLA Ops:
  22.2 19.0 %collective-permute-done.1 = bf16[64,2432]{1,0:T(8,128)(2,1)S(1)} collective-permute-done((bf16[64,2432]{1,0:T(8,128)(2,1)S(1)}, bf16[64,2432]{1,0:T(8,128)(2,1)S(1)}, u32[]{:S(2)}, u32[]{:S(2)}) %collective-permute-start.1) | collective-permute-done | bytes 311328 | tf_op jit(solution)/shard_map/ppermute | solution.py:50
  48.0 5.4 collective-permute-done.7
  53.3 14.9 %collective-permute-done.8 = bf16[64,2048]{1,0:T(8,128)(2,1)S(1)} collective-permute-done((bf16[64,2048]{1,0:T(8,128)(2,1)S(1)}, bf16[64,2048]{1,0:T(8,128)(2,1)S(1)}, u32[]{:S(2)}, u32[]{:S(2)}) %collective-permute-start.8) | collective-permute-done | bytes 262176 | tf_op jit(solution)/shard_map/ppermute | solution.py:50
  69.9 4.7 collective-permute-done.5.refs_1_
  81.3 12.6 %collective-permute-done.10 = bf16[128,2432]{1,0:T(8,128)(2,1)S(1)} collective-permute-done((bf16[128,2432]{1,0:T(8,128)(2,1)S(1)}, bf16[128,2432]{1,0:T(8,128)(2,1)S(1)}, u32[]{:S(2)}, u32[]{:S(2)}) %collective-permute-start.10) | collective-permute-done | bytes 622624 | tf_op jit(solution)/shard_map/ppermute | solution.py:47
  100.3 9.3 %enter.1 = (bf16[256,2048]{1,0:T(8,128)(2,1)}, bf16[256,2048]{1,0:T(8,128)(2,1)}, bf16[256,256]{1,0:T(8,128)(2,1)}, f32[16,2048]{1,0:T(8,128)}, f32[16,2048]{1,0:T(8,128)}) custom-call(s32[9]{0:T(128)} %stack.39.info.refs_0_, bf16[256,2048]{1,0:T(8,128)(2,1)} %bitcast.128, bf16[256,2432]{1,0:T(8,128)(2,1)} %bitcast.121, ...), custom_call_target="tpu_custom_call" | custom-call | flops 1024 | bytes 1024 | tf_op jit(solution)/shard_map/enter/pallas_call | solution.py:394
  123.6 12.0 %collective-permute-done.17 = bf16[256,256]{1,0:T(8,128)(2,1)S(1)} collective-permute-done((bf16[256,256]{1,0:T(8,128)(2,1)}, bf16[256,256]{1,0:T(8,128)(2,1)S(1)}, u32[]{:S(2)}, u32[]{:S(2)}) %collective-permute-start.17) | collective-permute-done | bytes 131104 | tf_op jit(solution)/shard_map/ppermute | solution.py:50
  148.8 14.9 %shard_map.314 = (bf16[256,2048]{1,0:T(8,128)(2,1)S(1)}, f32[16,1,256]{2,1,0:T(1,128)S(1)}) custom-call(s32[9]{0:T(128)S(1)} %copy-done.5, bf16[256,2048]{1,0:T(8,128)(2,1)S(1)} %copy-done.2, bf16[1024,128]{1,0:T(8,128)(2,1)S(1)} %get-tuple-element.508.refs_2_.refs_4_, bf16[128,1024]{1,0:T(8,128)(2,1)S(1)} %copy.99.refs_3_, f32[256,1]{1,0:T(8,128)S(1)} %copy.100.refs_4_.valid), custom_call_target="tpu_custom_call" | custom-call | flops 1024 | bytes 1024 | tf_op jit(solution)/shard_map/pallas_call | solution.py:200
  171.3 9.7 %leave.1 = (f32[256,2048]{1,0:T(8,128)}, bf16[256,2048]{1,0:T(8,128)(2,1)}) custom-call(bf16[256,2048]{1,0:T(8,128)(2,1)} %copy-done.1, bf16[256,2048]{1,0:T(8,128)(2,1)} %bitcast.129, f32[16,2048]{1,0:T(8,128)} %get-tuple-element.297.nat, bf16[256,2048]{1,0:T(8,128)(2,1)} %bitcast.126, bf16[256,2048]{1,0:T(8,128)(2,1)} %collective-permute-done.19.refs_1_, ...), custom_call_target="tpu_custom_call" | custom-call | flops 1024 | bytes 1024 | tf_op jit(solution)/shard_map/leave/pallas_call | solution.py:430
  191.0 15.3 %grad_act.1 = (bf16[2048,2048]{1,0:T(8,128)(2,1)}, bf16[2048,1024]{1,0:T(8,128)(2,1)}) custom-call(f32[2048,1]{1,0:T(8,128)} %copy.101.scale, bf16[1024,2048]{1,0:T(8,128)(2,1)} %all-gather.4.cloned.1.call-done.weight, bf16[256,2048]{1,0:T(8,128)(2,1)} %bitcast.135, bf16[256,2048]{1,0:T(8,128)(2,1)} %copy-done.24, ...), custom_call_target="tpu_custom_call" | custom-call | flops 1024 | bytes 1024 | tf_op jit(solution)/shard_map/grad_act/pallas_call | solution.py:604
  206.3 6.9 %collective-permute-done.33.refs_1_ = bf16[256,2048]{1,0:T(8,128)(2,1)S(1)} collective-permute-done((bf16[256,2048]{1,0:T(8,128)(2,1)}, bf16[256,2048]{1,0:T(8,128)(2,1)S(1)}, u32[]{:S(2)}, u32[]{:S(2)}) %collective-permute-start.33) | collective-permute-done | bytes 1048608 | tf_op jit(solution)/shard_map/ppermute | solution.py:47
  218.4 11.7 %collective-permute-done.35 = bf16[128,2048]{1,0:T(8,128)(2,1)S(1)} collective-permute-done((bf16[128,2048]{1,0:T(8,128)(2,1)S(1)}, bf16[128,2048]{1,0:T(8,128)(2,1)S(1)}, u32[]{:S(2)}, u32[]{:S(2)}) %collective-permute-start.35) | collective-permute-done | bytes 524320 | tf_op jit(solution)/shard_map/ppermute | solution.py:47
  232.7 11.3 %all-gather.6.cloned.1.call-done = bf16[32,64,1024]{2,1,0:T(8,128)(2,1)} async-done(((bf16[8,64,1024]{2,1,0:T(8,128)(2,1)}), bf16[32,64,1024]{2,1,0:T(8,128)(2,1)}) %all-gather.6.cloned.1.call-update) | async-done | bytes 4194320 | tf_op jit(solution)/shard_map/all_gather | solution.py:921
  250.0 22.1 %feed.1 = (bf16[2048,2048]{1,0:T(8,128)(2,1)}, bf16[2048,1024]{1,0:T(8,128)(2,1)}, bf16[2048,1024]{1,0:T(8,128)(2,1)}, f32[1,1024]{1,0:T(1,128)}) custom-call(f32[1,1024]{1,0:T(1,128)} %reshape.161.offset, bf16[2048,1024]{1,0:T(8,128)(2,1)} %get-tuple-element.329.back, bf16[4,8,64,1024]{3,2,1,0:T(8,128)(2,1)} %bitcast.115, ...), custom_call_target="tpu_custom_call" | custom-call | flops 1024 | bytes 1024 | tf_op jit(solution)/shard_map/feed/pallas_call | solution.py:659
  272.1 10.1 %grad_mlp.2 = bf16[1024,2048]{1,0:T(8,128)(2,1)} custom-call(bf16[2048,1024]{1,0:T(8,128)(2,1)} %get-tuple-element.372.value.grad, bf16[4,8,64,1024]{3,2,1,0:T(8,128)(2,1)} %bitcast.116), custom_call_target="tpu_custom_call" | custom-call | flops 1024 | bytes 1024 | tf_op jit(solution)/shard_map/grad_mlp/pallas_call | solution.py:706
  282.7 9.6 %grad_mlp.3.g0 = bf16[1024,2048]{1,0:T(8,128)(2,1)} custom-call(bf16[2048,1024]{1,0:T(8,128)(2,1)} %get-tuple-element.372.value.grad, bf16[4,8,64,1024]{3,2,1,0:T(8,128)(2,1)} %bitcast.117), custom_call_target="tpu_custom_call" | custom-call | flops 1024 | bytes 1024 | tf_op jit(solution)/shard_map/grad_mlp/pallas_call | solution.py:706
  297.4 8.5 %branch.2 = bf16[1024,2048]{1,0:T(8,128)(2,1)} custom-call(bf16[2048,1024]{1,0:T(8,128)(2,1)} %get-tuple-element.404.value.act, bf16[1024,2048]{1,0:T(8,128)(2,1)} %all-gather.4.cloned.1.call-done.weight), custom_call_target="tpu_custom_call" | custom-call | flops 1024 | bytes 1024 | tf_op jit(solution)/shard_map/branch/pallas_call | solution.py:728
  316.3 8.6 %branch.3 = bf16[1024,2048]{1,0:T(8,128)(2,1)} custom-call(bf16[2048,1024]{1,0:T(8,128)(2,1)} %get-tuple-element.404.value.act, bf16[1024,2048]{1,0:T(8,128)(2,1)} %all-gather.4.cloned.1.call-done.weight), custom_call_target="tpu_custom_call" | custom-call | flops 1024 | bytes 1024 | tf_op jit(solution)/shard_map/branch/pallas_call | solution.py:728
  324.8 14.1 %d_fc.1 = bf16[4,8,64,1024]{3,2,1,0:T(8,128)(2,1)} custom-call(bf16[2048,2048]{1,0:T(8,128)(2,1)} %get-tuple-element.371.mlp, bf16[2048,1024]{1,0:T(8,128)(2,1)} %get-tuple-element.372.value.grad), custom_call_target="tpu_custom_call" | custom-call | flops 1024 | bytes 1024 | tf_op jit(solution)/shard_map/d_fc/pallas_call | solution.py:796
  346.3 11.1 %middle.1 = (f32[256,2048]{1,0:T(8,128)}, bf16[256,2048]{1,0:T(8,128)(2,1)}, f32[8,2048]{1,0:T(8,128)}, bf16[256,2048]{1,0:T(8,128)(2,1)}) custom-call(bf16[1024,2048]{1,0:T(8,128)(2,1)} %grad_mlp.3.g0, bf16[1024,2048]{1,0:T(8,128)(2,1)} %copy-done.9, bf16[256,2048]{1,0:T(8,128)(2,1)} %copy-done.27, bf16[256,2048]{1,0:T(8,128)(2,1)} %collective-permute-done.45.g3, ...), custom_call_target="tpu_custom_call" | custom-call | flops 1024 | bytes 1024 | tf_op jit(solution)/shard_map/middle/pallas_call | solution.py:478
  364.4 17.8 %shard_map.315 = (bf16[256,2048]{1,0:T(8,128)(2,1)S(1)}, f32[1024,128]{1,0:T(8,128)S(1)}, f32[1024,128]{1,0:T(8,128)S(1)}) custom-call(s32[9]{0:T(128)S(1)} %copy-done.5, bf16[256,2048]{1,0:T(8,128)(2,1)S(1)} %copy-done.2, bf16[256,2048]{1,0:T(8,128)(2,1)S(1)} %copy-done.4, f32[16,1,256]{2,1,0:T(1,128)S(1)} %get-tuple-element.389.refs_3_, ...), custom_call_target="tpu_custom_call" | custom-call | flops 1024 | bytes 1024 | tf_op jit(solution)/shard_map/pallas_call | solution.py:259
  383.2 5.1 d_rows.4
  390.9 5.2 d_rows.6
  396.0 5.1 d_rows.5
  409.2 14.3 %d_proj.1 = bf16[1024,2048]{1,0:T(8,128)(2,1)} custom-call(bf16[2048,1024]{1,0:T(8,128)(2,1)} %get-tuple-element.404.value.act, bf16[2048,2048]{1,0:T(8,128)(2,1)} %get-tuple-element.405.two), custom_call_target="tpu_custom_call" | custom-call | flops 1024 | bytes 1024 | tf_op jit(solution)/shard_map/d_proj/pallas_call | solution.py:775
  437.2 5.3 d_rows.7
  442.5 12.1 %last.1 = (bf16[256,2048]{1,0:T(8,128)(2,1)}, bf16[2048,384]{1,0:T(8,128)(2,1)}) custom-call(s32[9]{0:T(128)} %stack.39.info.refs_0_, bf16[256,2048]{1,0:T(8,128)(2,1)} %copy-done, bf16[256,256]{1,0:T(8,128)(2,1)} %add_convert_fusion.22.kv, bf16[256,2048]{1,0:T(8,128)(2,1)} %bitcast.130, bf16[256,2048]{1,0:T(8,128)(2,1)} %get-tuple-element.394.left.attn, ...), custom_call_target="tpu_custom_call" | custom-call | flops 1024 | bytes 1024 | tf_op jit(solution)/shard_map/last/pallas_call | solution.py:558
  466.9 9.7 %collective-permute-done.60 = bf16[128,2048]{1,0:T(8,128)(2,1)S(1)} collective-permute-done((bf16[128,2048]{1,0:T(8,128)(2,1)S(1)}, bf16[128,2048]{1,0:T(8,128)(2,1)S(1)}, u32[]{:S(2)}, u32[]{:S(2)}) %collective-permute-start.60) | collective-permute-done | bytes 524320 | tf_op jit(solution)/shard_map/ppermute | solution.py:47
  489.6 33.1 %reduce-scatter.5.cloned.1.call-done = bf16[256,2048]{1,0:T(8,128)(2,1)} async-done(((bf16[1024,2048]{1,0:T(8,128)(2,1)}), bf16[256,2048]{1,0:T(8,128)(2,1)}) %reduce-scatter.5.cloned.1.call-update) | async-done | bytes 1048592 | tf_op jit(solution)/shard_map/reduce_scatter | solution.py:1008
  542.3 6.8 %all-to-all-start.1 = ((bf16[8,64,1,1024]{3,1,2,0:T(8,128)(2,1)}), bf16[8,64,1,1024]{3,1,2,0:T(8,128)(2,1)S(1)}, u32[]{:S(2)}, u32[]{:S(2)}) async-start(bf16[8,64,1,1024]{3,1,2,0:T(8,128)(2,1)} %bitcast.143), calls=%async_computation.3 | async-start | bytes 2097152 | tf_op jit(solution)/shard_map/all_to_all | solution.py:1065
  553.0 7.4 %collective-permute-done.76 = bf16[64,2048]{1,0:T(8,128)(2,1)} collective-permute-done((bf16[64,2048]{1,0:T(8,128)(2,1)}, bf16[64,2048]{1,0:T(8,128)(2,1)}, u32[]{:S(2)}, u32[]{:S(2)}) %collective-permute-start.76) | collective-permute-done | bytes 262176 | tf_op jit(solution)/shard_map/ppermute | solution.py:50
  560.4 5.8 %collective-permute-done.77 = bf16[64,2048]{1,0:T(8,128)(2,1)} collective-permute-done((bf16[64,2048]{1,0:T(8,128)(2,1)}, bf16[64,2048]{1,0:T(8,128)(2,1)}, u32[]{:S(2)}, u32[]{:S(2)}) %collective-permute-start.77) | collective-permute-done | bytes 262176 | tf_op jit(solution)/shard_map/ppermute | solution.py:50
  (362 shorter events, 201.1 us)
Async XLA Ops:
  7.2 183.8 %all-gather.4.cloned.1.call-start = ((), (), s32[]{:S(2)}) async-start(), calls=%async_computation.4 | async-start | bytes 5242880 | tf_op jit(solution)/shard_map/all_gather | solution.py:886
  7.2 37.5 %collective-permute-start.3 = (bf16[256,2048]{1,0:T(8,128)(2,1)}, bf16[256,2048]{1,0:T(8,128)(2,1)S(1)}, u32[]{:S(2)}, u32[]{:S(2)}) collective-permute-start(bf16[256,2048]{1,0:T(8,128)(2,1)} %bitcast.133), channel_id=1, source_target_pairs={{0,8},{4,12},{8,0},{12,4},{16,24},{20,28},{24,16},{28,20},{1,9},{5... | collective-permute-start | bytes 3145736 | tf_op jit(solution)/shard_map/ppermute | solution.py:47
  8.5 37.2 %collective-permute-start.4 = (bf16[256,2048]{1,0:T(8,128)(2,1)}, bf16[256,2048]{1,0:T(8,128)(2,1)}, u32[]{:S(2)}, u32[]{:S(2)}) collective-permute-start(bf16[256,2048]{1,0:T(8,128)(2,1)} %bitcast.134), channel_id=1, source_target_pairs={{0,16},{4,20},{8,24},{12,28},{16,0},{20,4},{24,8},{28,12},{1,17},{... | collective-permute-start | bytes 3145736 | tf_op jit(solution)/shard_map/ppermute | solution.py:47
  15.8 25.4 %collective-permute-start.1 = (bf16[64,2432]{1,0:T(8,128)(2,1)S(1)}, bf16[64,2432]{1,0:T(8,128)(2,1)S(1)}, u32[]{:S(2)}, u32[]{:S(2)}) collective-permute-start(bf16[64,2432]{1,0:T(8,128)(2,1)S(1)} %fusion.2), channel_id=1, source_target_pairs={{0,2},{1,3},{2,0},{3,1},{4,6},{5,7},{6,4},{7,5},{8,10},{9,11},{10,... | collective-permute-start | bytes 933896 | tf_op jit(solution)/shard_map/ppermute | solution.py:50
  16.9 27.8 %collective-permute-start.2 = (bf16[64,2432]{1,0:T(8,128)(2,1)S(1)}, bf16[64,2432]{1,0:T(8,128)(2,1)S(1)}, u32[]{:S(2)}, u32[]{:S(2)}) collective-permute-start(bf16[64,2432]{1,0:T(8,128)(2,1)S(1)} %fusion.2), channel_id=1, source_target_pairs={{0,3},{1,0},{2,1},{3,2},{4,7},{5,4},{6,5},{7,6},{8,11},{9,8},{10,9... | collective-permute-start | bytes 933896 | tf_op jit(solution)/shard_map/ppermute | solution.py:50
  45.9 28.6 %collective-permute-start.5 = (bf16[256,2432]{1,0:T(8,128)(2,1)S(1)}, bf16[256,2432]{1,0:T(8,128)(2,1)}, u32[]{:S(2)}, u32[]{:S(2)}) collective-permute-start(bf16[256,2432]{1,0:T(8,128)(2,1)S(1)} %bitcast.118), channel_id=1, source_target_pairs={{0,8},{4,12},{8,0},{12,4},{16,24},{20,28},{24,16},{28,20},{1,9},{5... | collective-permute-start | bytes 3735560 | tf_op jit(solution)/shard_map/ppermute | solution.py:47
  46.3 28.3 %collective-permute-start.6 = (bf16[256,2432]{1,0:T(8,128)(2,1)S(1)}, bf16[256,2432]{1,0:T(8,128)(2,1)}, u32[]{:S(2)}, u32[]{:S(2)}) collective-permute-start(bf16[256,2432]{1,0:T(8,128)(2,1)S(1)} %bitcast.119), channel_id=1, source_target_pairs={{0,16},{4,20},{8,24},{12,28},{16,0},{20,4},{24,8},{28,12},{1,17},{... | collective-permute-start | bytes 3735560 | tf_op jit(solution)/shard_map/ppermute | solution.py:47
  46.5 23.4 %collective-permute-start.9 = (bf16[64,2048]{1,0:T(8,128)(2,1)S(1)}, bf16[64,2048]{1,0:T(8,128)(2,1)S(1)}, u32[]{:S(2)}, u32[]{:S(2)}) collective-permute-start(bf16[64,2048]{1,0:T(8,128)(2,1)S(1)} %copy-done.37), channel_id=1, source_target_pairs={{0,3},{1,0},{2,1},{3,2},{4,7},{5,4},{6,5},{7,6},{8,11},{9,8},{10,9... | collective-permute-start | bytes 786440 | tf_op jit(solution)/shard_map/ppermute | solution.py:50
  97.9 25.5 %collective-permute-start.19 = (bf16[256,2048]{1,0:T(8,128)(2,1)S(1)}, bf16[256,2048]{1,0:T(8,128)(2,1)}, u32[]{:S(2)}, u32[]{:S(2)}) collective-permute-start(bf16[256,2048]{1,0:T(8,128)(2,1)S(1)} %bitcast.123), channel_id=1, source_target_pairs={{0,8},{4,12},{8,0},{12,4},{16,24},{20,28},{24,16},{28,20},{1,9},{5... | collective-permute-start | bytes 3145736 | tf_op jit(solution)/shard_map/ppermute | solution.py:47
  99.1 24.5 %collective-permute-start.20 = (bf16[256,2048]{1,0:T(8,128)(2,1)S(1)}, bf16[256,2048]{1,0:T(8,128)(2,1)}, u32[]{:S(2)}, u32[]{:S(2)}) collective-permute-start(bf16[256,2048]{1,0:T(8,128)(2,1)S(1)} %bitcast.124), channel_id=1, source_target_pairs={{0,16},{4,20},{8,24},{12,28},{16,0},{20,4},{24,8},{28,12},{1,17},{... | collective-permute-start | bytes 3145736 | tf_op jit(solution)/shard_map/ppermute | solution.py:47
  109.7 25.8 %collective-permute-start.17 = (bf16[256,256]{1,0:T(8,128)(2,1)}, bf16[256,256]{1,0:T(8,128)(2,1)S(1)}, u32[]{:S(2)}, u32[]{:S(2)}) collective-permute-start(bf16[256,256]{1,0:T(8,128)(2,1)} %get-tuple-element.282), channel_id=1, source_target_pairs={{0,2},{1,3},{2,0},{3,1},{4,6},{5,7},{6,4},{7,5},{8,10},{9,11},{10,... | collective-permute-start | bytes 393224 | tf_op jit(solution)/shard_map/ppermute | solution.py:50
  109.8 27.7 %collective-permute-start.18 = (bf16[256,256]{1,0:T(8,128)(2,1)}, bf16[256,256]{1,0:T(8,128)(2,1)S(1)}, u32[]{:S(2)}, u32[]{:S(2)}) collective-permute-start(bf16[256,256]{1,0:T(8,128)(2,1)} %get-tuple-element.282), channel_id=1, source_target_pairs={{0,3},{1,0},{2,1},{3,2},{4,7},{5,4},{6,5},{7,6},{8,11},{9,8},{10,9... | collective-permute-start | bytes 393224 | tf_op jit(solution)/shard_map/ppermute | solution.py:50
  120.9 123.0 %all-gather.6.cloned.1.call-start = ((), (), s32[]{:S(2)}) async-start(), calls=%async_computation.7 | async-start | bytes 5242880 | tf_op jit(solution)/shard_map/all_gather | solution.py:921
  138.6 288.7 %reduce-scatter.3.cloned.1.call-start = ((), (), s32[]{:S(2)}) async-start(), calls=%async_computation.5 | async-start | bytes 5242880 | tf_op jit(solution)/shard_map/reduce_scatter | solution.py:969
  188.1 25.0 %collective-permute-start.33 = (bf16[256,2048]{1,0:T(8,128)(2,1)}, bf16[256,2048]{1,0:T(8,128)(2,1)S(1)}, u32[]{:S(2)}, u32[]{:S(2)}) collective-permute-start(bf16[256,2048]{1,0:T(8,128)(2,1)} %get-tuple-element.340.refs_0_), channel_id=1, source_target_pairs={{0,8},{4,12},{8,0},{12,4},{16,24},{20,28},{24,16},{28,20},{1,9},{5... | collective-permute-start | bytes 3145736 | tf_op jit(solution)/shard_map/ppermute | solution.py:47
  188.9 24.7 %collective-permute-start.34 = (bf16[256,2048]{1,0:T(8,128)(2,1)}, bf16[256,2048]{1,0:T(8,128)(2,1)}, u32[]{:S(2)}, u32[]{:S(2)}) collective-permute-start(bf16[256,2048]{1,0:T(8,128)(2,1)} %get-tuple-element.340.refs_0_), channel_id=1, source_target_pairs={{0,16},{4,20},{8,24},{12,28},{16,0},{20,4},{24,8},{28,12},{1,17},{... | collective-permute-start | bytes 3145736 | tf_op jit(solution)/shard_map/ppermute | solution.py:47
  313.7 27.1 %collective-permute-start.46 = (bf16[1024,2048]{1,0:T(8,128)(2,1)}, bf16[1024,2048]{1,0:T(8,128)(2,1)}, u32[]{:S(2)}, u32[]{:S(2)}) collective-permute-start(bf16[1024,2048]{1,0:T(8,128)(2,1)} %branch.2), channel_id=1, source_target_pairs={{0,4},{4,0},{8,12},{12,8},{16,20},{20,16},{24,28},{28,24},{1,5},{5... | collective-permute-start | bytes 12582920 | tf_op jit(solution)/shard_map/ppermute | solution.py:47
  314.8 25.1 %collective-permute-start.44 = (bf16[256,2048]{1,0:T(8,128)(2,1)}, bf16[256,2048]{1,0:T(8,128)(2,1)S(1)}, u32[]{:S(2)}, u32[]{:S(2)}) collective-permute-start(bf16[256,2048]{1,0:T(8,128)(2,1)} %get-tuple-element.367), channel_id=1, source_target_pairs={{0,8},{4,12},{8,0},{12,4},{16,24},{20,28},{24,16},{28,20},{1,9},{5... | collective-permute-start | bytes 3145736 | tf_op jit(solution)/shard_map/ppermute | solution.py:47
  316.0 24.8 %collective-permute-start.45 = (bf16[256,2048]{1,0:T(8,128)(2,1)}, bf16[256,2048]{1,0:T(8,128)(2,1)}, u32[]{:S(2)}, u32[]{:S(2)}) collective-permute-start(bf16[256,2048]{1,0:T(8,128)(2,1)} %get-tuple-element.368), channel_id=1, source_target_pairs={{0,16},{4,20},{8,24},{12,28},{16,0},{20,4},{24,8},{28,12},{1,17},{... | collective-permute-start | bytes 3145736 | tf_op jit(solution)/shard_map/ppermute | solution.py:47
  341.0 181.7 %reduce-scatter.5.cloned.1.call-start = ((), (), s32[]{:S(2)}) async-start(), calls=%async_computation.6 | async-start | bytes 5242880 | tf_op jit(solution)/shard_map/reduce_scatter | solution.py:1008
  362.2 26.2 %collective-permute-start.49 = (bf16[256,2048]{1,0:T(8,128)(2,1)}, bf16[256,2048]{1,0:T(8,128)(2,1)}, u32[]{:S(2)}, u32[]{:S(2)}) collective-permute-start(bf16[256,2048]{1,0:T(8,128)(2,1)} %pad_maximum_fusion.2), channel_id=1, source_target_pairs={{0,8},{4,12},{8,0},{12,4},{16,24},{20,28},{24,16},{28,20},{1,9},{5... | collective-permute-start | bytes 3145736 | tf_op jit(solution)/shard_map/ppermute | solution.py:47
  363.1 25.4 %collective-permute-start.50 = (bf16[256,2048]{1,0:T(8,128)(2,1)}, bf16[256,2048]{1,0:T(8,128)(2,1)}, u32[]{:S(2)}, u32[]{:S(2)}) collective-permute-start(bf16[256,2048]{1,0:T(8,128)(2,1)} %pad_maximum_fusion.3), channel_id=1, source_target_pairs={{0,16},{4,20},{8,24},{12,28},{16,0},{20,4},{24,8},{28,12},{1,17},{... | collective-permute-start | bytes 3145736 | tf_op jit(solution)/shard_map/ppermute | solution.py:47
  403.7 23.6 %collective-permute-start.52 = (bf16[128,2048]{1,0:T(8,128)(2,1)S(1)}, bf16[128,2048]{1,0:T(8,128)(2,1)S(1)}, u32[]{:S(2)}, u32[]{:S(2)}) collective-permute-start(bf16[128,2048]{1,0:T(8,128)(2,1)S(1)} %get-tuple-element.402), channel_id=1, source_target_pairs={{0,16},{4,20},{8,24},{12,28},{16,0},{20,4},{24,8},{28,12},{1,17},{... | collective-permute-start | bytes 1572872 | tf_op jit(solution)/shard_map/ppermute | solution.py:47
  431.3 24.6 %collective-permute-start.59 = (bf16[1024,2048]{1,0:T(8,128)(2,1)}, bf16[1024,2048]{1,0:T(8,128)(2,1)}, u32[]{:S(2)}, u32[]{:S(2)}) collective-permute-start(bf16[1024,2048]{1,0:T(8,128)(2,1)} %d_rows.6), channel_id=1, source_target_pairs={{0,4},{4,0},{8,12},{12,8},{16,20},{20,16},{24,28},{28,24},{1,5},{5... | collective-permute-start | bytes 12582920 | tf_op jit(solution)/shard_map/ppermute | solution.py:47
  432.0 25.8 %collective-permute-start.57 = (bf16[256,2048]{1,0:T(8,128)(2,1)S(1)}, bf16[256,2048]{1,0:T(8,128)(2,1)S(1)}, u32[]{:S(2)}, u32[]{:S(2)}) collective-permute-start(bf16[256,2048]{1,0:T(8,128)(2,1)S(1)} %pad_maximum_fusion.5), channel_id=1, source_target_pairs={{0,8},{4,12},{8,0},{12,4},{16,24},{20,28},{24,16},{28,20},{1,9},{5... | collective-permute-start | bytes 3145736 | tf_op jit(solution)/shard_map/ppermute | solution.py:47
  433.2 24.6 %collective-permute-start.58 = (bf16[256,2048]{1,0:T(8,128)(2,1)S(1)}, bf16[256,2048]{1,0:T(8,128)(2,1)}, u32[]{:S(2)}, u32[]{:S(2)}) collective-permute-start(bf16[256,2048]{1,0:T(8,128)(2,1)S(1)} %pad_maximum_fusion.6), channel_id=1, source_target_pairs={{0,16},{4,20},{8,24},{12,28},{16,0},{20,4},{24,8},{28,12},{1,17},{... | collective-permute-start | bytes 3145736 | tf_op jit(solution)/shard_map/ppermute | solution.py:47
  483.1 47.4 %collective-permute-start.63 = (bf16[256,2048]{1,0:T(8,128)(2,1)}, bf16[256,2048]{1,0:T(8,128)(2,1)}, u32[]{:S(2)}, u32[]{:S(2)}) collective-permute-start(bf16[256,2048]{1,0:T(8,128)(2,1)} %pad_maximum_fusion.7), channel_id=1, source_target_pairs={{0,8},{4,12},{8,0},{12,4},{16,24},{20,28},{24,16},{28,20},{1,9},{5... | collective-permute-start | bytes 3145736 | tf_op jit(solution)/shard_map/ppermute | solution.py:47
  484.3 46.2 %collective-permute-start.64 = (bf16[256,2048]{1,0:T(8,128)(2,1)S(1)}, bf16[256,2048]{1,0:T(8,128)(2,1)}, u32[]{:S(2)}, u32[]{:S(2)}) collective-permute-start(bf16[256,2048]{1,0:T(8,128)(2,1)S(1)} %pad_maximum_fusion.8), channel_id=1, source_target_pairs={{0,16},{4,20},{8,24},{12,28},{16,0},{20,4},{24,8},{28,12},{1,17},{... | collective-permute-start | bytes 3145736 | tf_op jit(solution)/shard_map/ppermute | solution.py:47
  486.3 37.9 %collective-permute-start.69 = (bf16[64,2048]{1,0:T(8,128)(2,1)}, bf16[64,2048]{1,0:T(8,128)(2,1)}, u32[]{:S(2)}, u32[]{:S(2)}) collective-permute-start(bf16[64,2048]{1,0:T(8,128)(2,1)} %get-tuple-element.491), channel_id=1, source_target_pairs={{0,1},{1,2},{2,3},{3,0},{4,5},{5,6},{6,7},{7,4},{8,9},{9,10},{10,1... | collective-permute-start | bytes 786440 | tf_op jit(solution)/shard_map/ppermute | solution.py:50
  486.3 39.5 %collective-permute-start.70 = (bf16[64,2048]{1,0:T(8,128)(2,1)}, bf16[64,2048]{1,0:T(8,128)(2,1)}, u32[]{:S(2)}, u32[]{:S(2)}) collective-permute-start(bf16[64,2048]{1,0:T(8,128)(2,1)} %get-tuple-element.493), channel_id=1, source_target_pairs={{0,2},{1,3},{2,0},{3,1},{4,6},{5,7},{6,4},{7,5},{8,10},{9,11},{10,... | collective-permute-start | bytes 786440 | tf_op jit(solution)/shard_map/ppermute | solution.py:50
  488.1 38.8 %collective-permute-start.71 = (bf16[64,2048]{1,0:T(8,128)(2,1)S(1)}, bf16[64,2048]{1,0:T(8,128)(2,1)}, u32[]{:S(2)}, u32[]{:S(2)}) collective-permute-start(bf16[64,2048]{1,0:T(8,128)(2,1)S(1)} %get-tuple-element.492), channel_id=1, source_target_pairs={{0,3},{1,0},{2,1},{3,2},{4,7},{5,4},{6,5},{7,6},{8,11},{9,8},{10,9... | collective-permute-start | bytes 786440 | tf_op jit(solution)/shard_map/ppermute | solution.py:50
  542.3 26.0 %all-to-all-start.1 = ((bf16[8,64,1,1024]{3,1,2,0:T(8,128)(2,1)}), bf16[8,64,1,1024]{3,1,2,0:T(8,128)(2,1)S(1)}, u32[]{:S(2)}, u32[]{:S(2)}) async-start(bf16[8,64,1,1024]{3,1,2,0:T(8,128)(2,1)} %bitcast.143), calls=%async_computation.3 | async-start | bytes 2097152 | tf_op jit(solution)/shard_map/all_to_all | solution.py:1065
  (93 other events, 1099.3 us)
Sparse Core Ops, SparseCore 0:
  74.7 87.2 all-gather.3
  163.6 80.3 all-gather.5
  340.9 85.3 reduce-scatter.2
  428.5 94.0 reduce-scatter.4

commit v3 on v2

--- a/solution.py
+++ b/solution.py
@@ -64,12 +64,20 @@
             )
         return full
 
-    def seq_scatter_near(self, part):
-        total = part(self.z)
-        for step in range(1, self.ns):
-            owner = lax.rem(self.z + step, self.ns)
-            total = total + self.up(part(owner).astype(BF), step).astype(F32)
-        return total
+    def seq_cut(self, share, rows):
+        mine = lax.dynamic_slice_in_dim(share, self.z * rows, rows, 0)
+        sends = [
+            lax.dynamic_slice_in_dim(
+                share, lax.rem(self.z + step, self.ns) * rows, rows, 0
+            ).astype(BF)
+            for step in range(1, self.ns)
+        ]
+        return mine, sends
+
+    def seq_sum(self, mine, sends):
+        for step, part in enumerate(sends):
+            mine = mine + self.up(part, step + 1).astype(F32)
+        return mine
 
     def cross(self, block):
         if self.nd == 8:
@@ -104,15 +112,24 @@
         return second
 
     def other(self, value):
+        if isinstance(value, (list, tuple)):
+            return [self.swap(part, 1) for part in value]
         return self.swap(value, 1)
+
+    def part(self, value, at):
+        arrays = value if isinstance(value, (list, tuple)) else [value]
+        rows = sum(a.shape[0] for a in arrays) * 2 // self.nd
+        start = at * rows
+        for array in arrays:
+            if start < array.shape[0]:
+                return array[start : start + rows]
+            start -= array.shape[0]
 
     def corner_sums(self, even, other):
         if self.nd != 8:
             return ()
-        rows = even.shape[0] // 4
-        at = 3 * rows
-        half = rows // 2
-        held = even[at:].astype(F32) + other[at:].astype(F32)
+        held = self.part(even, 3).astype(F32) + self.part(other, 3).astype(F32)
+        half = held.shape[0] // 2
         return held[:half].astype(BF), held[half:].astype(BF)
 
     def send_corner(self, sums):
@@ -122,43 +139,36 @@
 
     def cross_sums(self, even, other, far):
         if self.nd == 8:
-            rows = even.shape[0] // 4
-            half = rows // 2
-
-            def held(start, size):
-                return even[start : start + size].astype(F32) + other[start : start + size].astype(
-                    F32
-                )
-
             low, high = far
+            half = low.shape[0]
+
+            def held(at, first):
+                rows = slice(first, first + half)
+                return self.part(even, at)[rows].astype(F32) + self.part(other, at)[rows].astype(F32)
+
             to_x = jnp.concatenate(
-                [
-                    (held(rows, half) + low.astype(F32)).astype(BF),
-                    held(rows + half, half).astype(BF),
-                ],
-                axis=0,
+                [(held(1, 0) + low.astype(F32)).astype(BF), held(1, half).astype(BF)], axis=0
             )
             to_y = jnp.concatenate(
-                [
-                    held(2 * rows, half).astype(BF),
-                    (held(2 * rows + half, half) + high.astype(F32)).astype(BF),
-                ],
-                axis=0,
+                [held(2, 0).astype(BF), (held(2, half) + high.astype(F32)).astype(BF)], axis=0
             )
             return to_x, to_y
-        held = even.astype(F32) + other.astype(F32)
-        bit = self.nd // 2
-        while bit > 2:
-            cut = held.shape[0] // 2
-            held = held[:cut] + self.swap(held[cut:].astype(BF), bit).astype(F32)
-            bit //= 2
-        return held.astype(BF), jnp.zeros_like(even[: even.shape[0] // (self.nd // 2)])
+        held = [
+            self.part(even, at).astype(F32) + self.part(other, at).astype(F32)
+            for at in range(self.nd // 2)
+        ]
+        while len(held) > 2:
+            cut = len(held) // 2
+            held = [
+                a + self.swap(b.astype(BF), len(held)).astype(F32)
+                for a, b in zip(held[:cut], held[cut:])
+            ]
+        return held[0].astype(BF), held[1].astype(BF)
 
     def send_cross(self, sums):
         if self.nd == 8:
             return self.swap(sums[0], 2), self.swap(sums[1], 4)
-        cut = sums[0].shape[0] // 2
-        return self.swap(sums[0][cut:], 2), sums[0][:cut]
+        return sums[0], self.swap(sums[1], 2)
 
     def ends(self, even, other, near):
         if self.nd == 8:
@@ -167,8 +177,11 @@
         return near[0], near[1], nothing, nothing
 
     def scatter_end(self, even, other, near):
-        rows = even.shape[0] * 2 // self.nd
-        return sum(part[:rows].astype(F32) for part in self.ends(even, other, near))
+        if self.nd == 8:
+            parts = (self.part(even, 0), self.part(other, 0)) + tuple(near)
+        else:
+            parts = near
+        return sum(part.astype(F32) for part in parts)
 
 
 LOG2E = 1.4426950408889634
@@ -745,11 +758,21 @@
     blocks = dp // 2
     size = left.shape[1] // dp
     skip = blocks if second_half else 0
-
-    def kernel(left, right, out):
-        out[...] = t_dot(left[...], right[...]).astype(BF)
-
-    return pl.pallas_call(
+    count = 2 if second_half else 1
+    each = blocks // count
+
+    def kernel(left, right, *outs):
+        value = t_dot(left[...], right[...]).astype(BF)
+        for n, out in enumerate(outs):
+
+            @pl.when(pl.program_id(0) // each == n)
+            def _(out=out):
+                out[...] = value
+
+    def place(n):
+        return lambda i: (jnp.clip(i - n * each, 0, each - 1), 0)
+
+    outs = pl.pallas_call(
         kernel,
         name="d_rows",
         grid=(blocks,),
@@ -757,11 +780,12 @@
             pl.BlockSpec((rows, size), lambda i: (0, i + skip)),
             pl.BlockSpec((rows, width), fixed),
         ],
-        out_specs=pl.BlockSpec((size, width), by_row),
-        out_shape=jax.ShapeDtypeStruct((size * blocks, width), BF),
+        out_specs=[pl.BlockSpec((size, width), place(n)) for n in range(count)],
+        out_shape=[jax.ShapeDtypeStruct((size * each, width), BF)] * count,
         compiler_params=PARAMS,
         cost_estimate=cost(),
     )(left, right)
+    return outs if second_half else outs[0]
 
 
 def d_proj_call(act, two, seq):
@@ -958,15 +982,17 @@
     corner, act_low = tick(corner, act_low)
     far = ring.send_corner(corner)
     branch_odd = branch_call(act_low, True, proj_all)
-    far, branch_odd, act_low, grad_pre = tick(far, branch_odd, act_low, grad_pre)
+    d_fc = d_fc_call(mlp_all, grad_pre, dp, seq)
+    far, branch_odd, act_low, d_fc = tick(far, branch_odd, act_low, d_fc)
+    fc_share = lax.psum_scatter(d_fc, "seq", scatter_dimension=0, tiled=False)
     cross = ring.cross_sums(even, other, far)
-    cross, act_low, grad_pre, branch_odd = tick(cross, act_low, grad_pre, branch_odd)
+    cross, act_low, branch_odd = tick(cross, act_low, branch_odd)
     near = ring.send_cross(cross)
     branch_other = ring.other(branch_odd)
     branch_even = branch_call(act_low, False, proj_all)
-    d_fc = d_fc_call(mlp_all, grad_pre, dp, seq)
-    near, branch_even, branch_other, d_fc = tick(near, branch_even, branch_other, d_fc)
-    fc_share = lax.psum_scatter(d_fc, "seq", scatter_dimension=0, tiled=False)
+    d_proj = d_proj_call(act_low, two_all, seq)
+    near, branch_even, branch_other, d_proj = tick(near, branch_even, branch_other, d_proj)
+    proj_share = lax.psum_scatter(d_proj, "seq", scatter_dimension=0, tiled=True)
     corner = ring.corner_sums(branch_even, branch_other)
     corner, near = tick(corner, near)
 
@@ -976,42 +1002,32 @@
     grad_mid, grad_one, sums, grad_att = middle_call(
         ring.ends(even, other, near), hidden_one, raw, own_scale, valid_rows, nat, out_all
     )
-    grad_att, grad_one, branch_far = tick(grad_att, grad_one, branch_far)
+    d_out_odd = d_rows_call(attn_low, True, grad_one, dp)
+    grad_att, grad_one, d_out_odd, branch_far = tick(grad_att, grad_one, d_out_odd, branch_far)
     cross = ring.cross_sums(branch_even, branch_other, branch_far)
-    cross, grad_att = tick(cross, grad_att)
+    cross, grad_att, grad_one, d_out_odd = tick(cross, grad_att, grad_one, d_out_odd)
     branch_near = ring.send_cross(cross)
+    d_out_other = ring.other(d_out_odd)
     query_grad, key_grad, value_grad = attend_back(
         info, query_low, grad_att, log_total, key_all, jnp.transpose(key_all), value_all, pairs, scale
     )
+    d_out_even = d_rows_call(attn_low, False, grad_one, dp)
+    kv_grads = jnp.concatenate([key_grad, value_grad], axis=1)
+    kv_mine, kv_sends = ring.seq_cut(kv_grads, rows)
+    query_grad, kv_mine, kv_sends, d_out_even, d_out_other, branch_near, fc_share = tick(
+        query_grad, kv_mine, kv_sends, d_out_even, d_out_other, branch_near, fc_share
+    )
+    corner = ring.corner_sums(d_out_even, d_out_other)
+    corner, query_grad = tick(corner, query_grad)
+    out_far_back = ring.send_corner(corner)
+    kv_grad = ring.seq_sum(kv_mine, kv_sends).astype(BF)
     d_q_odd = d_rows_call(attn_in, True, query_grad, dp)
-    kv_grads = jnp.concatenate([key_grad, value_grad], axis=1).reshape(seq, rows, 2 * HEAD)
-    kv_mine = lax.dynamic_slice_in_dim(kv_grads, z, 1, 0)[0]
-    kv_sends = [
-        lax.dynamic_slice_in_dim(kv_grads, lax.rem(z + step, seq), 1, 0)[0].astype(BF)
-        for step in range(1, seq)
-    ]
-    query_grad, kv_mine, kv_sends, grad_one, d_q_odd, branch_near = tick(
-        query_grad, kv_mine, kv_sends, grad_one, d_q_odd, branch_near
-    )
+    out_far_back, kv_grad, d_q_odd, query_grad = tick(out_far_back, kv_grad, d_q_odd, query_grad)
+    cross = ring.cross_sums(d_out_even, d_out_other, out_far_back)
+    cross, d_q_odd, query_grad, kv_grad = tick(cross, d_q_odd, query_grad, kv_grad)
+    out_near_back = ring.send_cross(cross)
     d_q_other = ring.other(d_q_odd)
-    kv_parts = [ring.up(part, step + 1) for step, part in enumerate(kv_sends)]
     d_q_even = d_rows_call(attn_in, False, query_grad, dp)
-    d_out_odd = d_rows_call(attn_low, True, grad_one, dp)
-    d_q_other, d_q_even, d_out_odd, grad_one = tick(d_q_other, d_q_even, d_out_odd, grad_one)
-    corner = ring.corner_sums(d_q_even, d_q_other)
-    corner, act_low = tick(corner, act_low)
-    q_far = ring.send_corner(corner)
-    d_proj = d_proj_call(act_low, two_all, seq)
-    q_far, d_proj, kv_parts, d_out_odd, grad_one, fc_share = tick(
-        q_far, d_proj, kv_parts, d_out_odd, grad_one, fc_share
-    )
-    proj_share = lax.psum_scatter(d_proj, "seq", scatter_dimension=0, tiled=True)
-    cross = ring.cross_sums(d_q_even, d_q_other, q_far)
-    kv_grad = (kv_mine + sum(part.astype(F32) for part in kv_parts)).astype(BF)
-    cross, kv_grad, d_out_odd, grad_one = tick(cross, kv_grad, d_out_odd, grad_one)
-    q_near = ring.send_cross(cross)
-    d_out_other = ring.other(d_out_odd)
-    d_out_even = d_rows_call(attn_low, False, grad_one, dp)
     grad_rows, small = last_call(
         info,
         query_grad,
@@ -1029,43 +1045,41 @@
     )
     grad_tokens = grad_rows.reshape(windows, span, width)
     cut = width // 2
-    out_corner = ring.corner_sums(d_out_even, d_out_other)
     small_odd = small[cut:]
-    q_near, small, small_odd, out_corner = tick(q_near, small, small_odd, out_corner)
-    out_far_back = ring.send_corner(out_corner)
+    out_near_back, d_q_other, d_q_even, small, small_odd, branch_near = tick(
+        out_near_back, d_q_other, d_q_even, small, small_odd, branch_near
+    )
+    corner = ring.corner_sums(d_q_even, d_q_other)
+    corner, small_odd, out_near_back, branch_near = tick(
+        corner, small_odd, out_near_back, branch_near
+    )
+    q_far = ring.send_corner(corner)
     small_other = ring.other(small_odd)
-    q_share = ring.scatter_end(d_q_even, d_q_other, q_near)
+    out_share = ring.scatter_end(d_out_even, d_out_other, out_near_back)
+    out_mine, out_sends = ring.seq_cut(out_share, own)
     branch_two = ring.scatter_end(branch_even, branch_other, branch_near)
     output = (hidden_one + branch_two + nat[6:7]).astype(BF).reshape(windows, span, width)
-    out_far_back, q_share, small_other, output = tick(out_far_back, q_share, small_other, output)
+    q_far, small_other, out_mine, out_sends, output = tick(
+        q_far, small_other, out_mine, out_sends, output
+    )
+    cross = ring.cross_sums(d_q_even, d_q_other, q_far)
+    cross, small_other, out_sends = tick(cross, small_other, out_sends)
+    q_near = ring.send_cross(cross)
+    d_w_out = ring.seq_sum(out_mine, out_sends)
     small_corner = ring.corner_sums(small[:cut], small_other)
-    cross = ring.cross_sums(d_out_even, d_out_other, out_far_back)
-    cross, small_corner, q_share = tick(cross, small_corner, q_share)
+    q_near, d_w_out, small_corner, proj_share = tick(q_near, d_w_out, small_corner, proj_share)
+    q_share = ring.scatter_end(d_q_even, d_q_other, q_near)
+    q_mine, q_sends = ring.seq_cut(q_share, own)
+    q_mine, q_sends, small_corner = tick(q_mine, q_sends, small_corner)
+    d_w_query = ring.seq_sum(q_mine, q_sends)
     small_far = ring.send_corner(small_corner)
-    small_far, proj_share = tick(small_far, proj_share)
-    out_near_back = ring.send_cross(cross)
-    small_cross = ring.cross_sums(small[:cut], small_other, small_far)
-    small_near = ring.send_cross(small_cross)
-    d_w_query = ring.seq_scatter_near(
-        lambda owner: lax.dynamic_slice_in_dim(q_share, owner * own, own, 0)
-    )
-    out_near_back, small_near, d_w_query, fc_share = tick(
-        out_near_back, small_near, d_w_query, fc_share
-    )
-    out_share = ring.scatter_end(d_out_even, d_out_other, out_near_back)
-    d_w_out = ring.seq_scatter_near(
-        lambda owner: lax.dynamic_slice_in_dim(out_share, owner * own, own, 0)
-    )
+    small_near = ring.send_cross(ring.cross_sums(small[:cut], small_other, small_far))
+    small_near, fc_share = tick(small_near, fc_share)
+    fc_turned_back = lax.all_to_all(fc_share, "dp", split_axis=0, concat_axis=1, tiled=False)
     small_share = ring.scatter_end(small[:cut], small_other, small_near)
-    d_small = ring.seq_scatter_near(
-        lambda owner: lax.dynamic_slice_in_dim(small_share, owner * own, own, 0)
-    )
+    d_small = ring.seq_sum(*ring.seq_cut(small_share, own))
     d_w_proj = proj_share.astype(F32)
-    d_w_fc = (
-        lax.all_to_all(fc_share, "dp", split_axis=0, concat_axis=1, tiled=False)
-        .reshape(own, hidden)
-        .astype(F32)
-    )
+    d_w_fc = fc_turned_back.reshape(own, hidden).astype(F32)
     vectors = jnp.transpose(d_small[:, 2 * HEAD :])
     return (
         output,

time: 586 us -> 574 us (0.980)
  waiting for transfers between devices: 182 us -> 175 us
    reduce_scatter x1, waiting for transfers between devices: 33.1 us -> 0.01 us  [local(): lax.psum_scatter(d_proj, 'seq', scatter_dimension=0, tiled=True)]
    ppermute x21, waiting for transfers between devices: 79.3 us -> 110 us  [up(): lax.ppermute(value, 'seq', [(i, (i + by) % self.ns) for i in range(self.n...]
    ppermute x57 -> x59, waiting for transfers between devices: 58.6 us -> 53.6 us  [swap(): return lax.ppermute(value, 'dp', [(i, i ^ mask) for i in range(self.nd)])]
    ppermute x57 -> x59, starting transfers between devices: 47.6 us -> 48.9 us  [swap(): return lax.ppermute(value, 'dp', [(i, i ^ mask) for i in range(self.nd)])]
    unnamed x92 -> x105, local copies, waits for them, and re-layouts: 16 us -> 15.6 us
  transfers between devices with their start and end apart: 84 -> 86, of which waited for: 30 -> 32; matrix products, arithmetic and copies ran while one was open for 14% -> 12% of each run, Pallas kernels for 29% -> 30%
where the time goes in v3:
time: 574 us; the launch traced here: 565 us
  Pallas kernels  199 us (35%)
  waiting for transfers between devices  175 us (30%)
  starting transfers between devices  78.9 us (14%)
  local copies, waits for them, and re-layouts  51.1 us (9%)
  other arithmetic  43.8 us (8%)
  between operations  16.7 us (3%)
    ppermute x21, waiting for transfers between devices, up(): lax.ppermute(value, 'seq', [(i, (i + by) % self.ns) for i in range(self.n...  110 us
    ppermute x59, waiting for transfers between devices, swap(): return lax.ppermute(value, 'dp', [(i, i ^ mask) for i in range(self.nd)])  53.6 us
    ppermute x59, starting transfers between devices, swap(): return lax.ppermute(value, 'dp', [(i, i ^ mask) for i in range(self.nd)])  48.9 us
    pallas_call x1, Pallas kernels, feed_call(): pl.pallas_call(kernel, name='feed', grid=(rows // tile,), in_specs=[pl.Bl...  22.1 us
    pallas_call x4, Pallas kernels, d_rows_call(): pl.pallas_call(kernel, name='d_rows', grid=(blocks,), in_specs=[pl.BlockS...  22.1 us
    pallas_call x2, Pallas kernels, grad_mlp_call(): pl.pallas_call(kernel, name='grad_mlp', grid=(rows // tile,), in_specs=[p...  19.6 us
    ppermute x21, starting transfers between devices, up(): lax.ppermute(value, 'seq', [(i, (i + by) % self.ns) for i in range(self.n...  18.4 us
    pallas_call x1, Pallas kernels, attend_back(): pl.pallas_call(lambda *refs: attend_back_kernel(*refs, heads=heads, scale...  18 us
  transfers between devices with their start and end apart: 86, of which 32 were waited for; matrix products, arithmetic and copies ran while one was open for 12% of the time, Pallas kernels for 30%

profile of v3, /device:TPU:9, one launch (start us, length us, event | category | flops | bytes accessed | tf_op | source)
XLA Modules:
  0.0 564.5 jit_solution(2471756611923496012)
XLA Ops:
  22.2 19.0 %collective-permute-done.1 = bf16[64,2432]{1,0:T(8,128)(2,1)S(1)} collective-permute-done((bf16[64,2432]{1,0:T(8,128)(2,1)S(1)}, bf16[64,2432]{1,0:T(8,128)(2,1)S(1)}, u32[]{:S(2)}, u32[]{:S(2)}) %collective-permute-start.1) | collective-permute-done | bytes 311328 | tf_op jit(solution)/shard_map/ppermute | solution.py:50
  47.0 5.6 collective-permute-done.7
  52.6 15.0 %collective-permute-done.8 = bf16[64,2048]{1,0:T(8,128)(2,1)S(1)} collective-permute-done((bf16[64,2048]{1,0:T(8,128)(2,1)}, bf16[64,2048]{1,0:T(8,128)(2,1)S(1)}, u32[]{:S(2)}, u32[]{:S(2)}) %collective-permute-start.8) | collective-permute-done | bytes 262176 | tf_op jit(solution)/shard_map/ppermute | solution.py:50
  80.5 12.6 %collective-permute-done.10 = bf16[128,2432]{1,0:T(8,128)(2,1)S(1)} collective-permute-done((bf16[128,2432]{1,0:T(8,128)(2,1)S(1)}, bf16[128,2432]{1,0:T(8,128)(2,1)S(1)}, u32[]{:S(2)}, u32[]{:S(2)}) %collective-permute-start.10) | collective-permute-done | bytes 622624 | tf_op jit(solution)/shard_map/ppermute | solution.py:47
  100.4 9.3 %enter.1 = (bf16[256,2048]{1,0:T(8,128)(2,1)}, bf16[256,2048]{1,0:T(8,128)(2,1)}, bf16[256,256]{1,0:T(8,128)(2,1)}, f32[16,2048]{1,0:T(8,128)}, f32[16,2048]{1,0:T(8,128)}) custom-call(s32[9]{0:T(128)} %stack.39.info.refs_0_, bf16[256,2048]{1,0:T(8,128)(2,1)} %bitcast.119, bf16[256,2432]{1,0:T(8,128)(2,1)} %bitcast.112, ...), custom_call_target="tpu_custom_call" | custom-call | flops 1024 | bytes 1024 | tf_op jit(solution)/shard_map/enter/pallas_call | solution.py:407
  124.2 11.6 %collective-permute-done.17 = bf16[256,256]{1,0:T(8,128)(2,1)S(1)} collective-permute-done((bf16[256,256]{1,0:T(8,128)(2,1)}, bf16[256,256]{1,0:T(8,128)(2,1)S(1)}, u32[]{:S(2)}, u32[]{:S(2)}) %collective-permute-start.17) | collective-permute-done | bytes 131104 | tf_op jit(solution)/shard_map/ppermute | solution.py:50
  147.7 14.9 %shard_map.314 = (bf16[256,2048]{1,0:T(8,128)(2,1)S(1)}, f32[16,1,256]{2,1,0:T(1,128)S(1)}) custom-call(s32[9]{0:T(128)S(1)} %copy-done.5, bf16[256,2048]{1,0:T(8,128)(2,1)S(1)} %copy-done.2, bf16[1024,128]{1,0:T(8,128)(2,1)S(1)} %get-tuple-element.562.refs_2_.refs_4_, bf16[128,1024]{1,0:T(8,128)(2,1)S(1)} %copy.99.refs_3_, f32[256,1]{1,0:T(8,128)S(1)} %copy.100.refs_4_.valid), custom_call_target="tpu_custom_call" | custom-call | flops 1024 | bytes 1024 | tf_op jit(solution)/shard_map/pallas_call | solution.py:213
  170.2 9.7 %leave.1 = (f32[256,2048]{1,0:T(8,128)}, bf16[256,2048]{1,0:T(8,128)(2,1)}) custom-call(bf16[256,2048]{1,0:T(8,128)(2,1)} %copy-done.1, bf16[256,2048]{1,0:T(8,128)(2,1)} %bitcast.120, f32[16,2048]{1,0:T(8,128)} %get-tuple-element.322.nat, bf16[256,2048]{1,0:T(8,128)(2,1)} %bitcast.116, bf16[256,2048]{1,0:T(8,128)(2,1)} %collective-permute-done.19.refs_1_, ...), custom_call_target="tpu_custom_call" | custom-call | flops 1024 | bytes 1024 | tf_op jit(solution)/shard_map/leave/pallas_call | solution.py:443
  189.9 15.3 %grad_act.1 = (bf16[2048,2048]{1,0:T(8,128)(2,1)}, bf16[2048,1024]{1,0:T(8,128)(2,1)}) custom-call(f32[2048,1]{1,0:T(8,128)} %copy.101.scale, bf16[1024,2048]{1,0:T(8,128)(2,1)} %all-gather.4.cloned.1.call-done.weight, bf16[256,2048]{1,0:T(8,128)(2,1)} %bitcast.125, bf16[256,2048]{1,0:T(8,128)(2,1)} %copy-done.24, ...), custom_call_target="tpu_custom_call" | custom-call | flops 1024 | bytes 1024 | tf_op jit(solution)/shard_map/grad_act/pallas_call | solution.py:617
  205.2 6.9 %collective-permute-done.33.refs_1_ = bf16[256,2048]{1,0:T(8,128)(2,1)S(1)} collective-permute-done((bf16[256,2048]{1,0:T(8,128)(2,1)}, bf16[256,2048]{1,0:T(8,128)(2,1)S(1)}, u32[]{:S(2)}, u32[]{:S(2)}) %collective-permute-start.33) | collective-permute-done | bytes 1048608 | tf_op jit(solution)/shard_map/ppermute | solution.py:47
  217.4 11.8 %collective-permute-done.35 = bf16[128,2048]{1,0:T(8,128)(2,1)S(1)} collective-permute-done((bf16[128,2048]{1,0:T(8,128)(2,1)S(1)}, bf16[128,2048]{1,0:T(8,128)(2,1)S(1)}, u32[]{:S(2)}, u32[]{:S(2)}) %collective-permute-start.35) | collective-permute-done | bytes 524320 | tf_op jit(solution)/shard_map/ppermute | solution.py:47
  231.7 11.3 %all-gather.6.cloned.1.call-done = bf16[32,64,1024]{2,1,0:T(8,128)(2,1)} async-done(((bf16[8,64,1024]{2,1,0:T(8,128)(2,1)}), bf16[32,64,1024]{2,1,0:T(8,128)(2,1)}) %all-gather.6.cloned.1.call-update) | async-done | bytes 4194320 | tf_op jit(solution)/shard_map/all_gather | solution.py:945
  249.1 22.1 %feed.1 = (bf16[2048,2048]{1,0:T(8,128)(2,1)}, bf16[2048,1024]{1,0:T(8,128)(2,1)}, bf16[2048,1024]{1,0:T(8,128)(2,1)}, f32[1,1024]{1,0:T(1,128)}) custom-call(f32[1,1024]{1,0:T(1,128)} %reshape.155.offset, bf16[2048,1024]{1,0:T(8,128)(2,1)} %get-tuple-element.354.back, bf16[4,8,64,1024]{3,2,1,0:T(8,128)(2,1)} %bitcast.106, ...), custom_call_target="tpu_custom_call" | custom-call | flops 1024 | bytes 1024 | tf_op jit(solution)/shard_map/feed/pallas_call | solution.py:672
  271.2 10.0 %grad_mlp.2 = bf16[1024,2048]{1,0:T(8,128)(2,1)} custom-call(bf16[2048,1024]{1,0:T(8,128)(2,1)} %get-tuple-element.375.value.grad, bf16[4,8,64,1024]{3,2,1,0:T(8,128)(2,1)} %bitcast.107), custom_call_target="tpu_custom_call" | custom-call | flops 1024 | bytes 1024 | tf_op jit(solution)/shard_map/grad_mlp/pallas_call | solution.py:719
  281.6 9.6 %grad_mlp.3.g0 = bf16[1024,2048]{1,0:T(8,128)(2,1)} custom-call(bf16[2048,1024]{1,0:T(8,128)(2,1)} %get-tuple-element.375.value.grad, bf16[4,8,64,1024]{3,2,1,0:T(8,128)(2,1)} %bitcast.108), custom_call_target="tpu_custom_call" | custom-call | flops 1024 | bytes 1024 | tf_op jit(solution)/shard_map/grad_mlp/pallas_call | solution.py:719
  297.3 14.1 %d_fc.1 = bf16[4,8,64,1024]{3,2,1,0:T(8,128)(2,1)} custom-call(bf16[2048,2048]{1,0:T(8,128)(2,1)} %get-tuple-element.385.mlp, bf16[2048,1024]{1,0:T(8,128)(2,1)} %get-tuple-element.375.value.grad), custom_call_target="tpu_custom_call" | custom-call | flops 1024 | bytes 1024 | tf_op jit(solution)/shard_map/d_fc/pallas_call | solution.py:820
  311.4 8.7 %branch.2 = bf16[1024,2048]{1,0:T(8,128)(2,1)} custom-call(bf16[2048,1024]{1,0:T(8,128)(2,1)} %get-tuple-element.394.value.act, bf16[1024,2048]{1,0:T(8,128)(2,1)} %all-gather.4.cloned.1.call-done.weight), custom_call_target="tpu_custom_call" | custom-call | flops 1024 | bytes 1024 | tf_op jit(solution)/shard_map/branch/pallas_call | solution.py:741
  325.5 8.7 %branch.3 = bf16[1024,2048]{1,0:T(8,128)(2,1)} custom-call(bf16[2048,1024]{1,0:T(8,128)(2,1)} %get-tuple-element.394.value.act, bf16[1024,2048]{1,0:T(8,128)(2,1)} %all-gather.4.cloned.1.call-done.weight), custom_call_target="tpu_custom_call" | custom-call | flops 1024 | bytes 1024 | tf_op jit(solution)/shard_map/branch/pallas_call | solution.py:741
  334.3 14.2 %d_proj.1 = bf16[1024,2048]{1,0:T(8,128)(2,1)} custom-call(bf16[2048,1024]{1,0:T(8,128)(2,1)} %get-tuple-element.394.value.act, bf16[2048,2048]{1,0:T(8,128)(2,1)} %get-tuple-element.396.two), custom_call_target="tpu_custom_call" | custom-call | flops 1024 | bytes 1024 | tf_op jit(solution)/shard_map/d_proj/pallas_call | solution.py:799
  355.5 10.4 %middle.1 = (f32[256,2048]{1,0:T(8,128)}, bf16[256,2048]{1,0:T(8,128)(2,1)}, f32[8,2048]{1,0:T(8,128)}, bf16[256,2048]{1,0:T(8,128)(2,1)}) custom-call(bf16[1024,2048]{1,0:T(8,128)(2,1)} %grad_mlp.3.g0, bf16[1024,2048]{1,0:T(8,128)(2,1)} %copy-done.9, bf16[256,2048]{1,0:T(8,128)(2,1)} %copy-done.30, bf16[256,2048]{1,0:T(8,128)(2,1)} %collective-permute-done.45.g3, ...), custom_call_target="tpu_custom_call" | custom-call | flops 1024 | bytes 1024 | tf_op jit(solution)/shard_map/middle/pallas_call | solution.py:491
  366.0 5.7 %d_rows.4 = (bf16[512,2048]{1,0:T(8,128)(2,1)}, bf16[512,2048]{1,0:T(8,128)(2,1)}) custom-call(bf16[256,2048]{1,0:T(8,128)(2,1)} %copy-done.1, bf16[256,2048]{1,0:T(8,128)(2,1)} %get-tuple-element.423.right), custom_call_target="tpu_custom_call" | custom-call | flops 1024 | bytes 1024 | tf_op jit(solution)/shard_map/d_rows/pallas_call | solution.py:775
  378.7 5.4 d_rows.5
  384.1 18.0 %shard_map.315 = (bf16[256,2048]{1,0:T(8,128)(2,1)S(1)}, f32[1024,128]{1,0:T(8,128)S(1)}, f32[1024,128]{1,0:T(8,128)S(1)}) custom-call(s32[9]{0:T(128)S(1)} %copy-done.5, bf16[256,2048]{1,0:T(8,128)(2,1)S(1)} %copy-done.2, bf16[256,2048]{1,0:T(8,128)(2,1)S(1)} %copy-done.4, f32[16,1,256]{2,1,0:T(1,128)S(1)} %get-tuple-element.419.refs_3_, ...), custom_call_target="tpu_custom_call" | custom-call | flops 1024 | bytes 1024 | tf_op jit(solution)/shard_map/pallas_call | solution.py:272
  412.0 5.7 %d_rows.6 = (bf16[512,2048]{1,0:T(8,128)(2,1)}, bf16[512,2048]{1,0:T(8,128)(2,1)}) custom-call(bf16[256,2048]{1,0:T(8,128)(2,1)} %get-tuple-element.439.left.attn, bf16[256,2048]{1,0:T(8,128)(2,1)} %copy-done), custom_call_target="tpu_custom_call" | custom-call | flops 1024 | bytes 1024 | tf_op jit(solution)/shard_map/d_rows/pallas_call | solution.py:775
  420.7 5.6 collective-permute-done.57
  431.4 6.3 %collective-permute-start.60 = (bf16[512,2048]{1,0:T(8,128)(2,1)}, bf16[512,2048]{1,0:T(8,128)(2,1)}, u32[]{:S(2)}, u32[]{:S(2)}) collective-permute-start(bf16[512,2048]{1,0:T(8,128)(2,1)} %get-tuple-element.451), channel_id=1, source_target_pairs={{0,4},{4,0},{8,12},{12,8},{16,20},{20,16},{24,28},{28,24},{1,5},{5... | collective-permute-start | bytes 6291464 | tf_op jit(solution)/shard_map/ppermute | solution.py:47
  441.6 5.3 d_rows.7
  447.0 12.1 %last.1 = (bf16[256,2048]{1,0:T(8,128)(2,1)}, bf16[2048,384]{1,0:T(8,128)(2,1)}) custom-call(s32[9]{0:T(128)} %stack.39.info.refs_0_, bf16[256,2048]{1,0:T(8,128)(2,1)} %copy-done, bf16[256,256]{1,0:T(8,128)(2,1)} %add_convert_fusion.22.kv, bf16[256,2048]{1,0:T(8,128)(2,1)} %bitcast.121, bf16[256,2048]{1,0:T(8,128)(2,1)} %get-tuple-element.439.left.attn, ...), custom_call_target="tpu_custom_call" | custom-call | flops 1024 | bytes 1024 | tf_op jit(solution)/shard_map/last/pallas_call | solution.py:571
  486.3 19.3 %collective-permute-done.67 = bf16[64,2048]{1,0:T(8,128)(2,1)S(1)} collective-permute-done((bf16[64,2048]{1,0:T(8,128)(2,1)S(1)}, bf16[64,2048]{1,0:T(8,128)(2,1)S(1)}, u32[]{:S(2)}, u32[]{:S(2)}) %collective-permute-start.67) | collective-permute-done | bytes 262176 | tf_op jit(solution)/shard_map/ppermute | solution.py:50
  505.6 5.6 collective-permute-done.68
  528.7 6.1 %all-to-all-start.1 = ((bf16[8,64,1,1024]{3,1,2,0:T(8,128)(2,1)}), bf16[8,64,1,1024]{3,1,2,0:T(8,128)(2,1)S(1)}, u32[]{:S(2)}, u32[]{:S(2)}) async-start(bf16[8,64,1,1024]{3,1,2,0:T(8,128)(2,1)} %bitcast.131), calls=%async_computation.3 | async-start | bytes 2097152 | tf_op jit(solution)/shard_map/all_to_all | solution.py:1078
  538.9 8.2 %collective-permute-done.78 = bf16[64,2048]{1,0:T(8,128)(2,1)} collective-permute-done((bf16[64,2048]{1,0:T(8,128)(2,1)}, bf16[64,2048]{1,0:T(8,128)(2,1)}, u32[]{:S(2)}, u32[]{:S(2)}) %collective-permute-start.78) | collective-permute-done | bytes 262176 | tf_op jit(solution)/shard_map/ppermute | solution.py:50
  (381 shorter events, 203.6 us)
Async XLA Ops:
  7.2 182.7 %all-gather.4.cloned.1.call-start = ((), (), s32[]{:S(2)}) async-start(), calls=%async_computation.4 | async-start | bytes 5242880 | tf_op jit(solution)/shard_map/all_gather | solution.py:910
  7.2 37.4 %collective-permute-start.3 = (bf16[256,2048]{1,0:T(8,128)(2,1)}, bf16[256,2048]{1,0:T(8,128)(2,1)S(1)}, u32[]{:S(2)}, u32[]{:S(2)}) collective-permute-start(bf16[256,2048]{1,0:T(8,128)(2,1)} %bitcast.123), channel_id=1, source_target_pairs={{0,8},{4,12},{8,0},{12,4},{16,24},{20,28},{24,16},{28,20},{1,9},{5... | collective-permute-start | bytes 3145736 | tf_op jit(solution)/shard_map/ppermute | solution.py:47
  8.5 36.2 %collective-permute-start.4 = (bf16[256,2048]{1,0:T(8,128)(2,1)}, bf16[256,2048]{1,0:T(8,128)(2,1)}, u32[]{:S(2)}, u32[]{:S(2)}) collective-permute-start(bf16[256,2048]{1,0:T(8,128)(2,1)} %bitcast.124), channel_id=1, source_target_pairs={{0,16},{4,20},{8,24},{12,28},{16,0},{20,4},{24,8},{28,12},{1,17},{... | collective-permute-start | bytes 3145736 | tf_op jit(solution)/shard_map/ppermute | solution.py:47
  15.8 25.4 %collective-permute-start.1 = (bf16[64,2432]{1,0:T(8,128)(2,1)S(1)}, bf16[64,2432]{1,0:T(8,128)(2,1)S(1)}, u32[]{:S(2)}, u32[]{:S(2)}) collective-permute-start(bf16[64,2432]{1,0:T(8,128)(2,1)S(1)} %fusion.2), channel_id=1, source_target_pairs={{0,2},{1,3},{2,0},{3,1},{4,6},{5,7},{6,4},{7,5},{8,10},{9,11},{10,... | collective-permute-start | bytes 933896 | tf_op jit(solution)/shard_map/ppermute | solution.py:50
  16.9 27.8 %collective-permute-start.2 = (bf16[64,2432]{1,0:T(8,128)(2,1)S(1)}, bf16[64,2432]{1,0:T(8,128)(2,1)S(1)}, u32[]{:S(2)}, u32[]{:S(2)}) collective-permute-start(bf16[64,2432]{1,0:T(8,128)(2,1)S(1)} %fusion.2), channel_id=1, source_target_pairs={{0,3},{1,0},{2,1},{3,2},{4,7},{5,4},{6,5},{7,6},{8,11},{9,8},{10,9... | collective-permute-start | bytes 933896 | tf_op jit(solution)/shard_map/ppermute | solution.py:50
  45.0 28.6 %collective-permute-start.5 = (bf16[256,2432]{1,0:T(8,128)(2,1)S(1)}, bf16[256,2432]{1,0:T(8,128)(2,1)}, u32[]{:S(2)}, u32[]{:S(2)}) collective-permute-start(bf16[256,2432]{1,0:T(8,128)(2,1)S(1)} %bitcast.109), channel_id=1, source_target_pairs={{0,8},{4,12},{8,0},{12,4},{16,24},{20,28},{24,16},{28,20},{1,9},{5... | collective-permute-start | bytes 3735560 | tf_op jit(solution)/shard_map/ppermute | solution.py:47
  45.3 28.3 %collective-permute-start.6 = (bf16[256,2432]{1,0:T(8,128)(2,1)S(1)}, bf16[256,2432]{1,0:T(8,128)(2,1)}, u32[]{:S(2)}, u32[]{:S(2)}) collective-permute-start(bf16[256,2432]{1,0:T(8,128)(2,1)S(1)} %bitcast.110), channel_id=1, source_target_pairs={{0,16},{4,20},{8,24},{12,28},{16,0},{20,4},{24,8},{28,12},{1,17},{... | collective-permute-start | bytes 3735560 | tf_op jit(solution)/shard_map/ppermute | solution.py:47
  96.9 27.3 %collective-permute-start.19 = (bf16[256,2048]{1,0:T(8,128)(2,1)S(1)}, bf16[256,2048]{1,0:T(8,128)(2,1)}, u32[]{:S(2)}, u32[]{:S(2)}) collective-permute-start(bf16[256,2048]{1,0:T(8,128)(2,1)S(1)} %bitcast.114), channel_id=1, source_target_pairs={{0,8},{4,12},{8,0},{12,4},{16,24},{20,28},{24,16},{28,20},{1,9},{5... | collective-permute-start | bytes 3145736 | tf_op jit(solution)/shard_map/ppermute | solution.py:47
  98.1 26.0 %collective-permute-start.20 = (bf16[256,2048]{1,0:T(8,128)(2,1)S(1)}, bf16[256,2048]{1,0:T(8,128)(2,1)}, u32[]{:S(2)}, u32[]{:S(2)}) collective-permute-start(bf16[256,2048]{1,0:T(8,128)(2,1)S(1)} %bitcast.115), channel_id=1, source_target_pairs={{0,16},{4,20},{8,24},{12,28},{16,0},{20,4},{24,8},{28,12},{1,17},{... | collective-permute-start | bytes 3145736 | tf_op jit(solution)/shard_map/ppermute | solution.py:47
  109.8 26.0 %collective-permute-start.17 = (bf16[256,256]{1,0:T(8,128)(2,1)}, bf16[256,256]{1,0:T(8,128)(2,1)S(1)}, u32[]{:S(2)}, u32[]{:S(2)}) collective-permute-start(bf16[256,256]{1,0:T(8,128)(2,1)} %get-tuple-element.307), channel_id=1, source_target_pairs={{0,2},{1,3},{2,0},{3,1},{4,6},{5,7},{6,4},{7,5},{8,10},{9,11},{10,... | collective-permute-start | bytes 393224 | tf_op jit(solution)/shard_map/ppermute | solution.py:50
  109.8 27.7 %collective-permute-start.18 = (bf16[256,256]{1,0:T(8,128)(2,1)}, bf16[256,256]{1,0:T(8,128)(2,1)S(1)}, u32[]{:S(2)}, u32[]{:S(2)}) collective-permute-start(bf16[256,256]{1,0:T(8,128)(2,1)} %get-tuple-element.307), channel_id=1, source_target_pairs={{0,3},{1,0},{2,1},{3,2},{4,7},{5,4},{6,5},{7,6},{8,11},{9,8},{10,9... | collective-permute-start | bytes 393224 | tf_op jit(solution)/shard_map/ppermute | solution.py:50
  121.6 121.4 %all-gather.6.cloned.1.call-start = ((), (), s32[]{:S(2)}) async-start(), calls=%async_computation.7 | async-start | bytes 5242880 | tf_op jit(solution)/shard_map/all_gather | solution.py:945
  137.5 265.8 %reduce-scatter.3.cloned.1.call-start = ((), (), s32[]{:S(2)}) async-start(), calls=%async_computation.5 | async-start | bytes 5242880 | tf_op jit(solution)/shard_map/reduce_scatter | solution.py:987
  187.1 25.0 %collective-permute-start.33 = (bf16[256,2048]{1,0:T(8,128)(2,1)}, bf16[256,2048]{1,0:T(8,128)(2,1)S(1)}, u32[]{:S(2)}, u32[]{:S(2)}) collective-permute-start(bf16[256,2048]{1,0:T(8,128)(2,1)} %get-tuple-element.365.refs_0_), channel_id=1, source_target_pairs={{0,8},{4,12},{8,0},{12,4},{16,24},{20,28},{24,16},{28,20},{1,9},{5... | collective-permute-start | bytes 3145736 | tf_op jit(solution)/shard_map/ppermute | solution.py:47
  187.9 24.7 %collective-permute-start.34 = (bf16[256,2048]{1,0:T(8,128)(2,1)}, bf16[256,2048]{1,0:T(8,128)(2,1)}, u32[]{:S(2)}, u32[]{:S(2)}) collective-permute-start(bf16[256,2048]{1,0:T(8,128)(2,1)} %get-tuple-element.365.refs_0_), channel_id=1, source_target_pairs={{0,16},{4,20},{8,24},{12,28},{16,0},{20,4},{24,8},{28,12},{1,17},{... | collective-permute-start | bytes 3145736 | tf_op jit(solution)/shard_map/ppermute | solution.py:47
  294.7 25.4 %collective-permute-start.42 = (bf16[128,2048]{1,0:T(8,128)(2,1)}, bf16[128,2048]{1,0:T(8,128)(2,1)S(1)}, u32[]{:S(2)}, u32[]{:S(2)}) collective-permute-start(bf16[128,2048]{1,0:T(8,128)(2,1)} %get-tuple-element.382), channel_id=1, source_target_pairs={{0,16},{4,20},{8,24},{12,28},{16,0},{20,4},{24,8},{28,12},{1,17},{... | collective-permute-start | bytes 1572872 | tf_op jit(solution)/shard_map/ppermute | solution.py:47
  324.3 26.0 %collective-permute-start.46 = (bf16[1024,2048]{1,0:T(8,128)(2,1)}, bf16[1024,2048]{1,0:T(8,128)(2,1)}, u32[]{:S(2)}, u32[]{:S(2)}) collective-permute-start(bf16[1024,2048]{1,0:T(8,128)(2,1)} %branch.2), channel_id=1, source_target_pairs={{0,4},{4,0},{8,12},{12,8},{16,20},{20,16},{24,28},{28,24},{1,5},{5... | collective-permute-start | bytes 12582920 | tf_op jit(solution)/shard_map/ppermute | solution.py:47
  325.1 189.3 %reduce-scatter.5.cloned.1.call-start = ((), (), s32[]{:S(2)}) async-start(), calls=%async_computation.6 | async-start | bytes 5242880 | tf_op jit(solution)/shard_map/reduce_scatter | solution.py:995
  325.1 25.2 %collective-permute-start.44 = (bf16[256,2048]{1,0:T(8,128)(2,1)}, bf16[256,2048]{1,0:T(8,128)(2,1)S(1)}, u32[]{:S(2)}, u32[]{:S(2)}) collective-permute-start(bf16[256,2048]{1,0:T(8,128)(2,1)} %get-tuple-element.392), channel_id=1, source_target_pairs={{0,8},{4,12},{8,0},{12,4},{16,24},{20,28},{24,16},{28,20},{1,9},{5... | collective-permute-start | bytes 3145736 | tf_op jit(solution)/shard_map/ppermute | solution.py:47
  325.4 24.9 %collective-permute-start.45 = (bf16[256,2048]{1,0:T(8,128)(2,1)}, bf16[256,2048]{1,0:T(8,128)(2,1)}, u32[]{:S(2)}, u32[]{:S(2)}) collective-permute-start(bf16[256,2048]{1,0:T(8,128)(2,1)} %get-tuple-element.393), channel_id=1, source_target_pairs={{0,16},{4,20},{8,24},{12,28},{16,0},{20,4},{24,8},{28,12},{1,17},{... | collective-permute-start | bytes 3145736 | tf_op jit(solution)/shard_map/ppermute | solution.py:47
  375.5 27.9 %collective-permute-start.49 = (bf16[512,2048]{1,0:T(8,128)(2,1)}, bf16[512,2048]{1,0:T(8,128)(2,1)}, u32[]{:S(2)}, u32[]{:S(2)}) collective-permute-start(bf16[512,2048]{1,0:T(8,128)(2,1)} %get-tuple-element.424), channel_id=1, source_target_pairs={{0,4},{4,0},{8,12},{12,8},{16,20},{20,16},{24,28},{28,24},{1,5},{5... | collective-permute-start | bytes 6291464 | tf_op jit(solution)/shard_map/ppermute | solution.py:47
  377.1 26.2 %collective-permute-start.50 = (bf16[512,2048]{1,0:T(8,128)(2,1)}, bf16[512,2048]{1,0:T(8,128)(2,1)}, u32[]{:S(2)}, u32[]{:S(2)}) collective-permute-start(bf16[512,2048]{1,0:T(8,128)(2,1)} %get-tuple-element.425), channel_id=1, source_target_pairs={{0,4},{4,0},{8,12},{12,8},{16,20},{20,16},{24,28},{28,24},{1,5},{5... | collective-permute-start | bytes 6291464 | tf_op jit(solution)/shard_map/ppermute | solution.py:47
  377.1 26.2 %collective-permute-start.51 = (bf16[256,2048]{1,0:T(8,128)(2,1)}, bf16[256,2048]{1,0:T(8,128)(2,1)}, u32[]{:S(2)}, u32[]{:S(2)}) collective-permute-start(bf16[256,2048]{1,0:T(8,128)(2,1)} %pad_maximum_fusion.2), channel_id=1, source_target_pairs={{0,8},{4,12},{8,0},{12,4},{16,24},{20,28},{24,16},{28,20},{1,9},{5... | collective-permute-start | bytes 3145736 | tf_op jit(solution)/shard_map/ppermute | solution.py:47
  377.4 25.9 %collective-permute-start.52 = (bf16[256,2048]{1,0:T(8,128)(2,1)S(1)}, bf16[256,2048]{1,0:T(8,128)(2,1)}, u32[]{:S(2)}, u32[]{:S(2)}) collective-permute-start(bf16[256,2048]{1,0:T(8,128)(2,1)S(1)} %pad_maximum_fusion.3), channel_id=1, source_target_pairs={{0,16},{4,20},{8,24},{12,28},{16,0},{20,4},{24,8},{28,12},{1,17},{... | collective-permute-start | bytes 3145736 | tf_op jit(solution)/shard_map/ppermute | solution.py:47
  431.4 30.9 %collective-permute-start.60 = (bf16[512,2048]{1,0:T(8,128)(2,1)}, bf16[512,2048]{1,0:T(8,128)(2,1)}, u32[]{:S(2)}, u32[]{:S(2)}) collective-permute-start(bf16[512,2048]{1,0:T(8,128)(2,1)} %get-tuple-element.451), channel_id=1, source_target_pairs={{0,4},{4,0},{8,12},{12,8},{16,20},{20,16},{24,28},{28,24},{1,5},{5... | collective-permute-start | bytes 6291464 | tf_op jit(solution)/shard_map/ppermute | solution.py:47
  437.8 24.5 %collective-permute-start.61 = (bf16[512,2048]{1,0:T(8,128)(2,1)}, bf16[512,2048]{1,0:T(8,128)(2,1)S(1)}, u32[]{:S(2)}, u32[]{:S(2)}) collective-permute-start(bf16[512,2048]{1,0:T(8,128)(2,1)} %get-tuple-element.452), channel_id=1, source_target_pairs={{0,4},{4,0},{8,12},{12,8},{16,20},{20,16},{24,28},{28,24},{1,5},{5... | collective-permute-start | bytes 6291464 | tf_op jit(solution)/shard_map/ppermute | solution.py:47
  482.2 32.2 %collective-permute-start.65 = (bf16[256,2048]{1,0:T(8,128)(2,1)}, bf16[256,2048]{1,0:T(8,128)(2,1)}, u32[]{:S(2)}, u32[]{:S(2)}) collective-permute-start(bf16[256,2048]{1,0:T(8,128)(2,1)} %pad_maximum_fusion.6), channel_id=1, source_target_pairs={{0,8},{4,12},{8,0},{12,4},{16,24},{20,28},{24,16},{28,20},{1,9},{5... | collective-permute-start | bytes 3145736 | tf_op jit(solution)/shard_map/ppermute | solution.py:47
  483.5 30.9 %collective-permute-start.66 = (bf16[256,2048]{1,0:T(8,128)(2,1)S(1)}, bf16[256,2048]{1,0:T(8,128)(2,1)}, u32[]{:S(2)}, u32[]{:S(2)}) collective-permute-start(bf16[256,2048]{1,0:T(8,128)(2,1)S(1)} %pad_maximum_fusion.7), channel_id=1, source_target_pairs={{0,16},{4,20},{8,24},{12,28},{16,0},{20,4},{24,8},{28,12},{1,17},{... | collective-permute-start | bytes 3145736 | tf_op jit(solution)/shard_map/ppermute | solution.py:47
  483.9 27.3 %collective-permute-start.68 = (bf16[64,2048]{1,0:T(8,128)(2,1)S(1)}, bf16[64,2048]{1,0:T(8,128)(2,1)S(1)}, u32[]{:S(2)}, u32[]{:S(2)}) collective-permute-start(bf16[64,2048]{1,0:T(8,128)(2,1)S(1)} %get-tuple-element.490), channel_id=1, source_target_pairs={{0,2},{1,3},{2,0},{3,1},{4,6},{5,7},{6,4},{7,5},{8,10},{9,11},{10,... | collective-permute-start | bytes 786440 | tf_op jit(solution)/shard_map/ppermute | solution.py:50
  483.9 29.6 %collective-permute-start.69 = (bf16[64,2048]{1,0:T(8,128)(2,1)S(1)}, bf16[64,2048]{1,0:T(8,128)(2,1)S(1)}, u32[]{:S(2)}, u32[]{:S(2)}) collective-permute-start(bf16[64,2048]{1,0:T(8,128)(2,1)S(1)} %get-tuple-element.491), channel_id=1, source_target_pairs={{0,3},{1,0},{2,1},{3,2},{4,7},{5,4},{6,5},{7,6},{8,11},{9,8},{10,9... | collective-permute-start | bytes 786440 | tf_op jit(solution)/shard_map/ppermute | solution.py:50
  524.8 26.0 %collective-permute-start.79 = (bf16[64,2048]{1,0:T(8,128)(2,1)S(1)}, bf16[64,2048]{1,0:T(8,128)(2,1)}, u32[]{:S(2)}, u32[]{:S(2)}) collective-permute-start(bf16[64,2048]{1,0:T(8,128)(2,1)S(1)} %get-tuple-element.505), channel_id=1, source_target_pairs={{0,3},{1,0},{2,1},{3,2},{4,7},{5,4},{6,5},{7,6},{8,11},{9,8},{10,9... | collective-permute-start | bytes 786440 | tf_op jit(solution)/shard_map/ppermute | solution.py:50
  528.7 27.1 %all-to-all-start.1 = ((bf16[8,64,1,1024]{3,1,2,0:T(8,128)(2,1)}), bf16[8,64,1,1024]{3,1,2,0:T(8,128)(2,1)S(1)}, u32[]{:S(2)}, u32[]{:S(2)}) async-start(bf16[8,64,1,1024]{3,1,2,0:T(8,128)(2,1)} %bitcast.131), calls=%async_computation.3 | async-start | bytes 2097152 | tf_op jit(solution)/shard_map/all_to_all | solution.py:1078
  (101 other events, 1233.2 us)
Sparse Core Ops, SparseCore 0:
  73.7 87.2 all-gather.3
  162.6 80.3 all-gather.5
  325.2 75.4 reduce-scatter.2
  412.1 94.7 reduce-scatter.4

commit v4 on v3

--- a/solution.py
+++ b/solution.py
@@ -661,10 +661,10 @@
             mine = slice(at, at + 256)
             v = dot32(rows_in, weight[:, :, :, mine].reshape(width, 256)) + offset[:, mine]
             square = v * v
-            t = jnp.tanh(ROOT * v * (1.0 + CUBIC * square))
+            t = jnp.tanh(v * (ROOT + (ROOT * CUBIC) * square))
             up = 0.5 + 0.5 * t
             act[:, mine] = (v * up).astype(BF)
-            slope = up + (0.5 * ROOT) * v * (1.0 - t * t) * (1.0 + (3.0 * CUBIC) * square)
+            slope = up + (1.0 - t * t) * (v * (0.5 * ROOT + (1.5 * ROOT * CUBIC) * square))
             grad = (back[:, mine].astype(F32) * slope).astype(BF)
             pre[:, mine] = grad
             total[:, mine] += jnp.sum(grad.astype(F32), axis=0, keepdims=True)
@@ -967,9 +967,10 @@
     mlp_own, two_all, grad_act, mlp_near = tick(mlp_own, two_all, grad_act, mlp_near)
     mlp_far = ring.corner(mlp_own, mlp_near)
     mlp_first = ring.first(mlp_own, mlp_near)
-    mlp_far, mlp_first, fc_all = tick(mlp_far, mlp_first, fc_all)
+    mlp_far, mlp_first = tick(mlp_far, mlp_first)
     mlp_second = ring.second(mlp_far)
-    mlp_second, fc_all = tick(mlp_second, fc_all)
+    (mlp_second,) = tick(mlp_second)
+    (fc_all,) = tick(fc_all)
     mlp_all, act_low, grad_pre, d_b_fc = feed_call(
         ring.pieces(mlp_first, mlp_second), bf_own, grad_act, fc_all
     )
@@ -1059,25 +1060,25 @@
     out_mine, out_sends = ring.seq_cut(out_share, own)
     branch_two = ring.scatter_end(branch_even, branch_other, branch_near)
     output = (hidden_one + branch_two + nat[6:7]).astype(BF).reshape(windows, span, width)
-    q_far, small_other, out_mine, out_sends, output = tick(
-        q_far, small_other, out_mine, out_sends, output
-    )
+    small_other, out_mine, out_sends, output = tick(small_other, out_mine, out_sends, output)
+    small_far = ring.send_corner(ring.corner_sums(small[:cut], small_other))
+    q_far, small_far = tick(q_far, small_far)
     cross = ring.cross_sums(d_q_even, d_q_other, q_far)
-    cross, small_other, out_sends = tick(cross, small_other, out_sends)
+    small_cross = ring.cross_sums(small[:cut], small_other, small_far)
+    cross, out_sends, small_cross = tick(cross, out_sends, small_cross)
     q_near = ring.send_cross(cross)
+    small_near = ring.send_cross(small_cross)
     d_w_out = ring.seq_sum(out_mine, out_sends)
-    small_corner = ring.corner_sums(small[:cut], small_other)
-    q_near, d_w_out, small_corner, proj_share = tick(q_near, d_w_out, small_corner, proj_share)
+    q_near, small_near, d_w_out, proj_share = tick(q_near, small_near, d_w_out, proj_share)
     q_share = ring.scatter_end(d_q_even, d_q_other, q_near)
+    small_share = ring.scatter_end(small[:cut], small_other, small_near)
     q_mine, q_sends = ring.seq_cut(q_share, own)
-    q_mine, q_sends, small_corner = tick(q_mine, q_sends, small_corner)
-    d_w_query = ring.seq_sum(q_mine, q_sends)
-    small_far = ring.send_corner(small_corner)
-    small_near = ring.send_cross(ring.cross_sums(small[:cut], small_other, small_far))
-    small_near, fc_share = tick(small_near, fc_share)
+    small_mine, small_sends = ring.seq_cut(small_share, own)
+    sends = [jnp.concatenate(pair, axis=1) for pair in zip(q_sends, small_sends)]
+    q_mine, small_mine, sends, fc_share = tick(q_mine, small_mine, sends, fc_share)
     fc_turned_back = lax.all_to_all(fc_share, "dp", split_axis=0, concat_axis=1, tiled=False)
-    small_share = ring.scatter_end(small[:cut], small_other, small_near)
-    d_small = ring.seq_sum(*ring.seq_cut(small_share, own))
+    both = ring.seq_sum(jnp.concatenate([q_mine, small_mine], axis=1), sends)
+    d_w_query, d_small = both[:, :width], both[:, width:]
     d_w_proj = proj_share.astype(F32)
     d_w_fc = fc_turned_back.reshape(own, hidden).astype(F32)
     vectors = jnp.transpose(d_small[:, 2 * HEAD :])

time: 574 us -> 568 us (0.990)
    ppermute x59, waiting for transfers between devices: 53.6 us -> 47.1 us  [swap(): return lax.ppermute(value, 'dp', [(i, i ^ mask) for i in range(self.nd)])]
    ppermute x21 -> x18, waiting for transfers between devices: 110 us -> 114 us  [up(): lax.ppermute(value, 'seq', [(i, (i + by) % self.ns) for i in range(self.n...]
    unnamed x105 -> x99, local copies, waits for them, and re-layouts: 15.6 us -> 13.5 us
    ppermute x21 -> x18, starting transfers between devices: 18.4 us -> 18 us  [up(): lax.ppermute(value, 'seq', [(i, (i + by) % self.ns) for i in range(self.n...]
  transfers between devices with their start and end apart: 86 -> 83, of which waited for: 32 -> 31; matrix products, arithmetic and copies ran while one was open for 12% -> 12% of each run, Pallas kernels for 30% -> 30%
where the time goes in v4:
time: 568 us; the launch traced here: 560 us
  Pallas kernels  198 us (35%)
  waiting for transfers between devices  173 us (30%)
  starting transfers between devices  78.1 us (14%)
  local copies, waits for them, and re-layouts  49.1 us (9%)
  other arithmetic  44.2 us (8%)
  between operations  16.7 us (3%)
    ppermute x18, waiting for transfers between devices, up(): lax.ppermute(value, 'seq', [(i, (i + by) % self.ns) for i in range(self.n...  114 us
    ppermute x59, starting transfers between devices, swap(): return lax.ppermute(value, 'dp', [(i, i ^ mask) for i in range(self.nd)])  49.2 us
    ppermute x59, waiting for transfers between devices, swap(): return lax.ppermute(value, 'dp', [(i, i ^ mask) for i in range(self.nd)])  47.1 us
    pallas_call x4, Pallas kernels, d_rows_call(): pl.pallas_call(kernel, name='d_rows', grid=(blocks,), in_specs=[pl.BlockS...  22.2 us
    pallas_call x1, Pallas kernels, feed_call(): pl.pallas_call(kernel, name='feed', grid=(rows // tile,), in_specs=[pl.Bl...  21.4 us
    pallas_call x2, Pallas kernels, grad_mlp_call(): pl.pallas_call(kernel, name='grad_mlp', grid=(rows // tile,), in_specs=[p...  19.6 us
    ppermute x18, starting transfers between devices, up(): lax.ppermute(value, 'seq', [(i, (i + by) % self.ns) for i in range(self.n...  18 us
    pallas_call x1, Pallas kernels, attend_back(): pl.pallas_call(lambda *refs: attend_back_kernel(*refs, heads=heads, scale...  17.8 us
  transfers between devices with their start and end apart: 83, of which 31 were waited for; matrix products, arithmetic and copies ran while one was open for 12% of the time, Pallas kernels for 30%

profile of v4, /device:TPU:9, one launch (start us, length us, event | category | flops | bytes accessed | tf_op | source)
XLA Modules:
  0.0 559.8 jit_solution(14810266712298791455)
XLA Ops:
  22.2 19.0 %collective-permute-done.1 = bf16[64,2432]{1,0:T(8,128)(2,1)S(1)} collective-permute-done((bf16[64,2432]{1,0:T(8,128)(2,1)S(1)}, bf16[64,2432]{1,0:T(8,128)(2,1)S(1)}, u32[]{:S(2)}, u32[]{:S(2)}) %collective-permute-start.1) | collective-permute-done | bytes 311328 | tf_op jit(solution)/shard_map/ppermute | solution.py:50
  47.7 5.6 collective-permute-done.7
  53.3 15.0 %collective-permute-done.8 = bf16[64,2048]{1,0:T(8,128)(2,1)S(1)} collective-permute-done((bf16[64,2048]{1,0:T(8,128)(2,1)}, bf16[64,2048]{1,0:T(8,128)(2,1)S(1)}, u32[]{:S(2)}, u32[]{:S(2)}) %collective-permute-start.8) | collective-permute-done | bytes 262176 | tf_op jit(solution)/shard_map/ppermute | solution.py:50
  84.7 7.9 %collective-permute-done.10 = bf16[128,2432]{1,0:T(8,128)(2,1)S(1)} collective-permute-done((bf16[128,2432]{1,0:T(8,128)(2,1)S(1)}, bf16[128,2432]{1,0:T(8,128)(2,1)S(1)}, u32[]{:S(2)}, u32[]{:S(2)}) %collective-permute-start.10) | collective-permute-done | bytes 622624 | tf_op jit(solution)/shard_map/ppermute | solution.py:47
  100.0 9.3 %enter.1 = (bf16[256,2048]{1,0:T(8,128)(2,1)}, bf16[256,2048]{1,0:T(8,128)(2,1)}, bf16[256,256]{1,0:T(8,128)(2,1)}, f32[16,2048]{1,0:T(8,128)}, f32[16,2048]{1,0:T(8,128)}) custom-call(s32[9]{0:T(128)} %stack.39.info.refs_0_, bf16[256,2048]{1,0:T(8,128)(2,1)} %bitcast.114, bf16[256,2432]{1,0:T(8,128)(2,1)} %bitcast.112, bf16[256,2432]{1,0:T(8,128)(2,1)} %copy-done.12, ...), custom_call_target="tpu_custom_call" | custom-call | flops 1024 | bytes 1024 | tf_op jit(solution)/shard_map/enter/pallas_call | solution.py:407
  123.5 11.8 %collective-permute-done.17 = bf16[256,256]{1,0:T(8,128)(2,1)S(1)} collective-permute-done((bf16[256,256]{1,0:T(8,128)(2,1)}, bf16[256,256]{1,0:T(8,128)(2,1)S(1)}, u32[]{:S(2)}, u32[]{:S(2)}) %collective-permute-start.17) | collective-permute-done | bytes 131104 | tf_op jit(solution)/shard_map/ppermute | solution.py:50
  146.7 14.6 %shard_map.314 = (bf16[256,2048]{1,0:T(8,128)(2,1)S(1)}, f32[16,1,256]{2,1,0:T(1,128)S(1)}) custom-call(s32[9]{0:T(128)S(1)} %copy-done.5, bf16[256,2048]{1,0:T(8,128)(2,1)S(1)} %copy-done.2, bf16[1024,128]{1,0:T(8,128)(2,1)S(1)} %get-tuple-element.565.refs_2_.refs_4_, bf16[128,1024]{1,0:T(8,128)(2,1)S(1)} %copy.99.refs_3_, f32[256,1]{1,0:T(8,128)S(1)} %copy.100.refs_4_.valid), custom_call_target="tpu_custom_call" | custom-call | flops 1024 | bytes 1024 | tf_op jit(solution)/shard_map/pallas_call | solution.py:213
  169.0 9.5 %leave.1 = (f32[256,2048]{1,0:T(8,128)}, bf16[256,2048]{1,0:T(8,128)(2,1)}) custom-call(bf16[256,2048]{1,0:T(8,128)(2,1)} %copy-done.1, bf16[256,2048]{1,0:T(8,128)(2,1)} %bitcast.115, f32[16,2048]{1,0:T(8,128)} %get-tuple-element.322.nat, bf16[256,2048]{1,0:T(8,128)(2,1)} %bitcast.32.refs_0_, bf16[256,2048]{1,0:T(8,128)(2,1)} %collective-permute-done.19.refs_1_, ...), custom_call_target="tpu_custom_call" | custom-call | flops 1024 | bytes 1024 | tf_op jit(solution)/shard_map/leave/pallas_call | solution.py:443
  187.4 15.3 %grad_act.1 = (bf16[2048,2048]{1,0:T(8,128)(2,1)}, bf16[2048,1024]{1,0:T(8,128)(2,1)}) custom-call(f32[2048,1]{1,0:T(8,128)} %copy.101.scale, bf16[1024,2048]{1,0:T(8,128)(2,1)} %all-gather.4.cloned.1.call-done.weight, bf16[256,2048]{1,0:T(8,128)(2,1)} %bitcast.121, bf16[256,2048]{1,0:T(8,128)(2,1)} %copy-done.24, ...), custom_call_target="tpu_custom_call" | custom-call | flops 1024 | bytes 1024 | tf_op jit(solution)/shard_map/grad_act/pallas_call | solution.py:617
  202.7 6.8 %collective-permute-done.33.refs_1_ = bf16[256,2048]{1,0:T(8,128)(2,1)S(1)} collective-permute-done((bf16[256,2048]{1,0:T(8,128)(2,1)}, bf16[256,2048]{1,0:T(8,128)(2,1)S(1)}, u32[]{:S(2)}, u32[]{:S(2)}) %collective-permute-start.33) | collective-permute-done | bytes 1048608 | tf_op jit(solution)/shard_map/ppermute | solution.py:47
  214.9 11.9 %collective-permute-done.35 = bf16[128,2048]{1,0:T(8,128)(2,1)S(1)} collective-permute-done((bf16[128,2048]{1,0:T(8,128)(2,1)S(1)}, bf16[128,2048]{1,0:T(8,128)(2,1)S(1)}, u32[]{:S(2)}, u32[]{:S(2)}) %collective-permute-start.35) | collective-permute-done | bytes 524320 | tf_op jit(solution)/shard_map/ppermute | solution.py:47
  231.6 12.1 %all-gather.6.cloned.1.call-done = bf16[32,64,1024]{2,1,0:T(8,128)(2,1)} async-done(((bf16[8,64,1024]{2,1,0:T(8,128)(2,1)}), bf16[32,64,1024]{2,1,0:T(8,128)(2,1)}) %all-gather.6.cloned.1.call-update) | async-done | bytes 4194320 | tf_op jit(solution)/shard_map/all_gather | solution.py:945
  243.7 21.4 %feed.1 = (bf16[2048,2048]{1,0:T(8,128)(2,1)}, bf16[2048,1024]{1,0:T(8,128)(2,1)}, bf16[2048,1024]{1,0:T(8,128)(2,1)}, f32[1,1024]{1,0:T(1,128)}) custom-call(f32[1,1024]{1,0:T(1,128)} %reshape.155.offset, bf16[2048,1024]{1,0:T(8,128)(2,1)} %get-tuple-element.354.back, bf16[4,8,64,1024]{3,2,1,0:T(8,128)(2,1)} %bitcast.106, ...), custom_call_target="tpu_custom_call" | custom-call | flops 1024 | bytes 1024 | tf_op jit(solution)/shard_map/feed/pallas_call | solution.py:672
  265.1 10.1 %grad_mlp.2 = bf16[1024,2048]{1,0:T(8,128)(2,1)} custom-call(bf16[2048,1024]{1,0:T(8,128)(2,1)} %get-tuple-element.375.value.grad, bf16[4,8,64,1024]{3,2,1,0:T(8,128)(2,1)} %bitcast.107), custom_call_target="tpu_custom_call" | custom-call | flops 1024 | bytes 1024 | tf_op jit(solution)/shard_map/grad_mlp/pallas_call | solution.py:719
  275.8 9.6 %grad_mlp.3.g0 = bf16[1024,2048]{1,0:T(8,128)(2,1)} custom-call(bf16[2048,1024]{1,0:T(8,128)(2,1)} %get-tuple-element.375.value.grad, bf16[4,8,64,1024]{3,2,1,0:T(8,128)(2,1)} %bitcast.108), custom_call_target="tpu_custom_call" | custom-call | flops 1024 | bytes 1024 | tf_op jit(solution)/shard_map/grad_mlp/pallas_call | solution.py:719
  291.3 14.1 %d_fc.1 = bf16[4,8,64,1024]{3,2,1,0:T(8,128)(2,1)} custom-call(bf16[2048,2048]{1,0:T(8,128)(2,1)} %get-tuple-element.385.mlp, bf16[2048,1024]{1,0:T(8,128)(2,1)} %get-tuple-element.375.value.grad), custom_call_target="tpu_custom_call" | custom-call | flops 1024 | bytes 1024 | tf_op jit(solution)/shard_map/d_fc/pallas_call | solution.py:820
  305.4 8.7 %branch.2 = bf16[1024,2048]{1,0:T(8,128)(2,1)} custom-call(bf16[2048,1024]{1,0:T(8,128)(2,1)} %get-tuple-element.394.value.act, bf16[1024,2048]{1,0:T(8,128)(2,1)} %all-gather.4.cloned.1.call-done.weight), custom_call_target="tpu_custom_call" | custom-call | flops 1024 | bytes 1024 | tf_op jit(solution)/shard_map/branch/pallas_call | solution.py:741
  319.4 8.8 %branch.3 = bf16[1024,2048]{1,0:T(8,128)(2,1)} custom-call(bf16[2048,1024]{1,0:T(8,128)(2,1)} %get-tuple-element.394.value.act, bf16[1024,2048]{1,0:T(8,128)(2,1)} %all-gather.4.cloned.1.call-done.weight), custom_call_target="tpu_custom_call" | custom-call | flops 1024 | bytes 1024 | tf_op jit(solution)/shard_map/branch/pallas_call | solution.py:741
  328.1 14.3 %d_proj.1 = bf16[1024,2048]{1,0:T(8,128)(2,1)} custom-call(bf16[2048,1024]{1,0:T(8,128)(2,1)} %get-tuple-element.394.value.act, bf16[2048,2048]{1,0:T(8,128)(2,1)} %get-tuple-element.396.two), custom_call_target="tpu_custom_call" | custom-call | flops 1024 | bytes 1024 | tf_op jit(solution)/shard_map/d_proj/pallas_call | solution.py:799
  349.2 10.4 %middle.1 = (f32[256,2048]{1,0:T(8,128)}, bf16[256,2048]{1,0:T(8,128)(2,1)}, f32[8,2048]{1,0:T(8,128)}, bf16[256,2048]{1,0:T(8,128)(2,1)}) custom-call(bf16[1024,2048]{1,0:T(8,128)(2,1)} %grad_mlp.3.g0, bf16[1024,2048]{1,0:T(8,128)(2,1)} %copy-done.9, bf16[256,2048]{1,0:T(8,128)(2,1)} %copy-done.29, bf16[256,2048]{1,0:T(8,128)(2,1)} %collective-permute-done.45.g3, ...), custom_call_target="tpu_custom_call" | custom-call | flops 1024 | bytes 1024 | tf_op jit(solution)/shard_map/middle/pallas_call | solution.py:491
  359.7 5.7 %d_rows.4 = (bf16[512,2048]{1,0:T(8,128)(2,1)}, bf16[512,2048]{1,0:T(8,128)(2,1)}) custom-call(bf16[256,2048]{1,0:T(8,128)(2,1)} %copy-done.1, bf16[256,2048]{1,0:T(8,128)(2,1)} %get-tuple-element.423.right), custom_call_target="tpu_custom_call" | custom-call | flops 1024 | bytes 1024 | tf_op jit(solution)/shard_map/d_rows/pallas_call | solution.py:775
  372.4 5.4 d_rows.5
  377.8 17.8 %shard_map.315 = (bf16[256,2048]{1,0:T(8,128)(2,1)S(1)}, f32[1024,128]{1,0:T(8,128)S(1)}, f32[1024,128]{1,0:T(8,128)S(1)}) custom-call(s32[9]{0:T(128)S(1)} %copy-done.5, bf16[256,2048]{1,0:T(8,128)(2,1)S(1)} %copy-done.2, bf16[256,2048]{1,0:T(8,128)(2,1)S(1)} %copy-done.4, f32[16,1,256]{2,1,0:T(1,128)S(1)} %get-tuple-element.419.refs_3_, ...), custom_call_target="tpu_custom_call" | custom-call | flops 1024 | bytes 1024 | tf_op jit(solution)/shard_map/pallas_call | solution.py:272
  405.4 5.8 %d_rows.6 = (bf16[512,2048]{1,0:T(8,128)(2,1)}, bf16[512,2048]{1,0:T(8,128)(2,1)}) custom-call(bf16[256,2048]{1,0:T(8,128)(2,1)} %get-tuple-element.439.left.attn, bf16[256,2048]{1,0:T(8,128)(2,1)} %copy-done), custom_call_target="tpu_custom_call" | custom-call | flops 1024 | bytes 1024 | tf_op jit(solution)/shard_map/d_rows/pallas_call | solution.py:775
  414.1 5.7 %collective-permute-done.57 = bf16[256,256]{1,0:T(8,128)(2,1)S(1)} collective-permute-done((bf16[256,256]{1,0:T(8,128)(2,1)S(1)}, bf16[256,256]{1,0:T(8,128)(2,1)S(1)}, u32[]{:S(2)}, u32[]{:S(2)}) %collective-permute-start.57) | collective-permute-done | bytes 131104 | tf_op jit(solution)/shard_map/ppermute | solution.py:50
  424.8 6.3 %collective-permute-start.60 = (bf16[512,2048]{1,0:T(8,128)(2,1)}, bf16[512,2048]{1,0:T(8,128)(2,1)}, u32[]{:S(2)}, u32[]{:S(2)}) collective-permute-start(bf16[512,2048]{1,0:T(8,128)(2,1)} %get-tuple-element.451), channel_id=1, source_target_pairs={{0,4},{4,0},{8,12},{12,8},{16,20},{20,16},{24,28},{28,24},{1,5},{5... | collective-permute-start | bytes 6291464 | tf_op jit(solution)/shard_map/ppermute | solution.py:47
  440.4 12.1 %last.1 = (bf16[256,2048]{1,0:T(8,128)(2,1)}, bf16[2048,384]{1,0:T(8,128)(2,1)}) custom-call(s32[9]{0:T(128)} %stack.39.info.refs_0_, bf16[256,2048]{1,0:T(8,128)(2,1)} %copy-done, bf16[256,256]{1,0:T(8,128)(2,1)} %add_convert_fusion.22.kv, bf16[256,2048]{1,0:T(8,128)(2,1)} %bitcast.116, bf16[256,2048]{1,0:T(8,128)(2,1)} %get-tuple-element.439.left.attn, ...), custom_call_target="tpu_custom_call" | custom-call | flops 1024 | bytes 1024 | tf_op jit(solution)/shard_map/last/pallas_call | solution.py:571
  481.0 17.6 %collective-permute-done.71 = bf16[64,2048]{1,0:T(8,128)(2,1)S(1)} collective-permute-done((bf16[64,2048]{1,0:T(8,128)(2,1)S(1)}, bf16[64,2048]{1,0:T(8,128)(2,1)S(1)}, u32[]{:S(2)}, u32[]{:S(2)}) %collective-permute-start.71) | collective-permute-done | bytes 262176 | tf_op jit(solution)/shard_map/ppermute | solution.py:50
  498.6 5.8 %collective-permute-done.72 = bf16[64,2048]{1,0:T(8,128)(2,1)S(1)} collective-permute-done((bf16[64,2048]{1,0:T(8,128)(2,1)S(1)}, bf16[64,2048]{1,0:T(8,128)(2,1)S(1)}, u32[]{:S(2)}, u32[]{:S(2)}) %collective-permute-start.72) | collective-permute-done | bytes 262176 | tf_op jit(solution)/shard_map/ppermute | solution.py:50
  519.3 5.9 %all-to-all-start.1 = ((bf16[8,64,1,1024]{3,1,2,0:T(8,128)(2,1)}), bf16[8,64,1,1024]{3,1,2,0:T(8,128)(2,1)S(1)}, u32[]{:S(2)}, u32[]{:S(2)}) async-start(bf16[8,64,1,1024]{3,1,2,0:T(8,128)(2,1)} %bitcast.127), calls=%async_computation.3 | async-start | bytes 2097152 | tf_op jit(solution)/shard_map/all_to_all | solution.py:1079
  526.8 13.5 %collective-permute-done.75 = bf16[64,2432]{1,0:T(8,128)(2,1)} collective-permute-done((bf16[64,2432]{1,0:T(8,128)(2,1)S(1)}, bf16[64,2432]{1,0:T(8,128)(2,1)}, u32[]{:S(2)}, u32[]{:S(2)}) %collective-permute-start.75) | collective-permute-done | bytes 311328 | tf_op jit(solution)/shard_map/ppermute | solution.py:50
  540.3 5.7 %collective-permute-done.76 = bf16[64,2432]{1,0:T(8,128)(2,1)} collective-permute-done((bf16[64,2432]{1,0:T(8,128)(2,1)S(1)}, bf16[64,2432]{1,0:T(8,128)(2,1)}, u32[]{:S(2)}, u32[]{:S(2)}) %collective-permute-start.76) | collective-permute-done | bytes 311328 | tf_op jit(solution)/shard_map/ppermute | solution.py:50
  (373 shorter events, 199.7 us)
Async XLA Ops:
  7.2 180.2 %all-gather.4.cloned.1.call-start = ((), (), s32[]{:S(2)}) async-start(), calls=%async_computation.4 | async-start | bytes 5242880 | tf_op jit(solution)/shard_map/all_gather | solution.py:910
  7.2 37.4 %collective-permute-start.3 = (bf16[256,2048]{1,0:T(8,128)(2,1)}, bf16[256,2048]{1,0:T(8,128)(2,1)S(1)}, u32[]{:S(2)}, u32[]{:S(2)}) collective-permute-start(bf16[256,2048]{1,0:T(8,128)(2,1)} %bitcast.119), channel_id=1, source_target_pairs={{0,8},{4,12},{8,0},{12,4},{16,24},{20,28},{24,16},{28,20},{1,9},{5... | collective-permute-start | bytes 3145736 | tf_op jit(solution)/shard_map/ppermute | solution.py:47
  8.5 36.2 %collective-permute-start.4 = (bf16[256,2048]{1,0:T(8,128)(2,1)}, bf16[256,2048]{1,0:T(8,128)(2,1)}, u32[]{:S(2)}, u32[]{:S(2)}) collective-permute-start(bf16[256,2048]{1,0:T(8,128)(2,1)} %bitcast.120), channel_id=1, source_target_pairs={{0,16},{4,20},{8,24},{12,28},{16,0},{20,4},{24,8},{28,12},{1,17},{... | collective-permute-start | bytes 3145736 | tf_op jit(solution)/shard_map/ppermute | solution.py:47
  15.8 25.4 %collective-permute-start.1 = (bf16[64,2432]{1,0:T(8,128)(2,1)S(1)}, bf16[64,2432]{1,0:T(8,128)(2,1)S(1)}, u32[]{:S(2)}, u32[]{:S(2)}) collective-permute-start(bf16[64,2432]{1,0:T(8,128)(2,1)S(1)} %fusion.4), channel_id=1, source_target_pairs={{0,2},{1,3},{2,0},{3,1},{4,6},{5,7},{6,4},{7,5},{8,10},{9,11},{10,... | collective-permute-start | bytes 933896 | tf_op jit(solution)/shard_map/ppermute | solution.py:50
  16.9 27.8 %collective-permute-start.2 = (bf16[64,2432]{1,0:T(8,128)(2,1)S(1)}, bf16[64,2432]{1,0:T(8,128)(2,1)S(1)}, u32[]{:S(2)}, u32[]{:S(2)}) collective-permute-start(bf16[64,2432]{1,0:T(8,128)(2,1)S(1)} %fusion.4), channel_id=1, source_target_pairs={{0,3},{1,0},{2,1},{3,2},{4,7},{5,4},{6,5},{7,6},{8,11},{9,8},{10,9... | collective-permute-start | bytes 933896 | tf_op jit(solution)/shard_map/ppermute | solution.py:50
  45.7 28.6 %collective-permute-start.5 = (bf16[256,2432]{1,0:T(8,128)(2,1)S(1)}, bf16[256,2432]{1,0:T(8,128)(2,1)S(1)}, u32[]{:S(2)}, u32[]{:S(2)}) collective-permute-start(bf16[256,2432]{1,0:T(8,128)(2,1)S(1)} %bitcast.109), channel_id=1, source_target_pairs={{0,8},{4,12},{8,0},{12,4},{16,24},{20,28},{24,16},{28,20},{1,9},{5... | collective-permute-start | bytes 3735560 | tf_op jit(solution)/shard_map/ppermute | solution.py:47
  46.0 28.3 %collective-permute-start.6 = (bf16[256,2432]{1,0:T(8,128)(2,1)S(1)}, bf16[256,2432]{1,0:T(8,128)(2,1)}, u32[]{:S(2)}, u32[]{:S(2)}) collective-permute-start(bf16[256,2432]{1,0:T(8,128)(2,1)S(1)} %bitcast.110), channel_id=1, source_target_pairs={{0,16},{4,20},{8,24},{12,28},{16,0},{20,4},{24,8},{28,12},{1,17},{... | collective-permute-start | bytes 3735560 | tf_op jit(solution)/shard_map/ppermute | solution.py:47
  96.5 27.0 %collective-permute-start.19 = (bf16[256,2048]{1,0:T(8,128)(2,1)}, bf16[256,2048]{1,0:T(8,128)(2,1)}, u32[]{:S(2)}, u32[]{:S(2)}) collective-permute-start(bf16[256,2048]{1,0:T(8,128)(2,1)} %bitcast.32.refs_0_), channel_id=1, source_target_pairs={{0,8},{4,12},{8,0},{12,4},{16,24},{20,28},{24,16},{28,20},{1,9},{5... | collective-permute-start | bytes 3145736 | tf_op jit(solution)/shard_map/ppermute | solution.py:47
  97.7 25.8 %collective-permute-start.20 = (bf16[256,2048]{1,0:T(8,128)(2,1)}, bf16[256,2048]{1,0:T(8,128)(2,1)}, u32[]{:S(2)}, u32[]{:S(2)}) collective-permute-start(bf16[256,2048]{1,0:T(8,128)(2,1)} %bitcast.32.refs_0_), channel_id=1, source_target_pairs={{0,16},{4,20},{8,24},{12,28},{16,0},{20,4},{24,8},{28,12},{1,17},{... | collective-permute-start | bytes 3145736 | tf_op jit(solution)/shard_map/ppermute | solution.py:47
  109.4 25.8 %collective-permute-start.17 = (bf16[256,256]{1,0:T(8,128)(2,1)}, bf16[256,256]{1,0:T(8,128)(2,1)S(1)}, u32[]{:S(2)}, u32[]{:S(2)}) collective-permute-start(bf16[256,256]{1,0:T(8,128)(2,1)} %get-tuple-element.307), channel_id=1, source_target_pairs={{0,2},{1,3},{2,0},{3,1},{4,6},{5,7},{6,4},{7,5},{8,10},{9,11},{10,... | collective-permute-start | bytes 393224 | tf_op jit(solution)/shard_map/ppermute | solution.py:50
  109.5 27.8 %collective-permute-start.18 = (bf16[256,256]{1,0:T(8,128)(2,1)}, bf16[256,256]{1,0:T(8,128)(2,1)S(1)}, u32[]{:S(2)}, u32[]{:S(2)}) collective-permute-start(bf16[256,256]{1,0:T(8,128)(2,1)} %get-tuple-element.307), channel_id=1, source_target_pairs={{0,3},{1,0},{2,1},{3,2},{4,7},{5,4},{6,5},{7,6},{8,11},{9,8},{10,9... | collective-permute-start | bytes 393224 | tf_op jit(solution)/shard_map/ppermute | solution.py:50
  120.8 122.8 %all-gather.6.cloned.1.call-start = ((), (), s32[]{:S(2)}) async-start(), calls=%async_computation.7 | async-start | bytes 5242880 | tf_op jit(solution)/shard_map/all_gather | solution.py:945
  145.3 251.5 %reduce-scatter.3.cloned.1.call-start = ((), (), s32[]{:S(2)}) async-start(), calls=%async_computation.5 | async-start | bytes 5242880 | tf_op jit(solution)/shard_map/reduce_scatter | solution.py:988
  184.5 25.0 %collective-permute-start.33 = (bf16[256,2048]{1,0:T(8,128)(2,1)}, bf16[256,2048]{1,0:T(8,128)(2,1)S(1)}, u32[]{:S(2)}, u32[]{:S(2)}) collective-permute-start(bf16[256,2048]{1,0:T(8,128)(2,1)} %get-tuple-element.365.refs_0_), channel_id=1, source_target_pairs={{0,8},{4,12},{8,0},{12,4},{16,24},{20,28},{24,16},{28,20},{1,9},{5... | collective-permute-start | bytes 3145736 | tf_op jit(solution)/shard_map/ppermute | solution.py:47
  185.5 24.7 %collective-permute-start.34 = (bf16[256,2048]{1,0:T(8,128)(2,1)}, bf16[256,2048]{1,0:T(8,128)(2,1)}, u32[]{:S(2)}, u32[]{:S(2)}) collective-permute-start(bf16[256,2048]{1,0:T(8,128)(2,1)} %get-tuple-element.365.refs_0_), channel_id=1, source_target_pairs={{0,16},{4,20},{8,24},{12,28},{16,0},{20,4},{24,8},{28,12},{1,17},{... | collective-permute-start | bytes 3145736 | tf_op jit(solution)/shard_map/ppermute | solution.py:47
  288.7 25.4 %collective-permute-start.42 = (bf16[128,2048]{1,0:T(8,128)(2,1)}, bf16[128,2048]{1,0:T(8,128)(2,1)S(1)}, u32[]{:S(2)}, u32[]{:S(2)}) collective-permute-start(bf16[128,2048]{1,0:T(8,128)(2,1)} %get-tuple-element.382), channel_id=1, source_target_pairs={{0,16},{4,20},{8,24},{12,28},{16,0},{20,4},{24,8},{28,12},{1,17},{... | collective-permute-start | bytes 1572872 | tf_op jit(solution)/shard_map/ppermute | solution.py:47
  318.3 25.8 %collective-permute-start.46 = (bf16[1024,2048]{1,0:T(8,128)(2,1)}, bf16[1024,2048]{1,0:T(8,128)(2,1)}, u32[]{:S(2)}, u32[]{:S(2)}) collective-permute-start(bf16[1024,2048]{1,0:T(8,128)(2,1)} %branch.2), channel_id=1, source_target_pairs={{0,4},{4,0},{8,12},{12,8},{16,20},{20,16},{24,28},{28,24},{1,5},{5... | collective-permute-start | bytes 12582920 | tf_op jit(solution)/shard_map/ppermute | solution.py:47
  318.9 191.1 %reduce-scatter.5.cloned.1.call-start = ((), (), s32[]{:S(2)}) async-start(), calls=%async_computation.6 | async-start | bytes 5242880 | tf_op jit(solution)/shard_map/reduce_scatter | solution.py:996
  319.0 25.2 %collective-permute-start.44 = (bf16[256,2048]{1,0:T(8,128)(2,1)}, bf16[256,2048]{1,0:T(8,128)(2,1)S(1)}, u32[]{:S(2)}, u32[]{:S(2)}) collective-permute-start(bf16[256,2048]{1,0:T(8,128)(2,1)} %get-tuple-element.392), channel_id=1, source_target_pairs={{0,8},{4,12},{8,0},{12,4},{16,24},{20,28},{24,16},{28,20},{1,9},{5... | collective-permute-start | bytes 3145736 | tf_op jit(solution)/shard_map/ppermute | solution.py:47
  319.3 24.8 %collective-permute-start.45 = (bf16[256,2048]{1,0:T(8,128)(2,1)}, bf16[256,2048]{1,0:T(8,128)(2,1)}, u32[]{:S(2)}, u32[]{:S(2)}) collective-permute-start(bf16[256,2048]{1,0:T(8,128)(2,1)} %get-tuple-element.393), channel_id=1, source_target_pairs={{0,16},{4,20},{8,24},{12,28},{16,0},{20,4},{24,8},{28,12},{1,17},{... | collective-permute-start | bytes 3145736 | tf_op jit(solution)/shard_map/ppermute | solution.py:47
  369.1 27.7 %collective-permute-start.49 = (bf16[512,2048]{1,0:T(8,128)(2,1)}, bf16[512,2048]{1,0:T(8,128)(2,1)}, u32[]{:S(2)}, u32[]{:S(2)}) collective-permute-start(bf16[512,2048]{1,0:T(8,128)(2,1)} %get-tuple-element.424), channel_id=1, source_target_pairs={{0,4},{4,0},{8,12},{12,8},{16,20},{20,16},{24,28},{28,24},{1,5},{5... | collective-permute-start | bytes 6291464 | tf_op jit(solution)/shard_map/ppermute | solution.py:47
  370.8 26.0 %collective-permute-start.50 = (bf16[512,2048]{1,0:T(8,128)(2,1)}, bf16[512,2048]{1,0:T(8,128)(2,1)}, u32[]{:S(2)}, u32[]{:S(2)}) collective-permute-start(bf16[512,2048]{1,0:T(8,128)(2,1)} %get-tuple-element.425), channel_id=1, source_target_pairs={{0,4},{4,0},{8,12},{12,8},{16,20},{20,16},{24,28},{28,24},{1,5},{5... | collective-permute-start | bytes 6291464 | tf_op jit(solution)/shard_map/ppermute | solution.py:47
  370.8 26.0 %collective-permute-start.51 = (bf16[256,2048]{1,0:T(8,128)(2,1)}, bf16[256,2048]{1,0:T(8,128)(2,1)}, u32[]{:S(2)}, u32[]{:S(2)}) collective-permute-start(bf16[256,2048]{1,0:T(8,128)(2,1)} %pad_maximum_fusion.2), channel_id=1, source_target_pairs={{0,8},{4,12},{8,0},{12,4},{16,24},{20,28},{24,16},{28,20},{1,9},{5... | collective-permute-start | bytes 3145736 | tf_op jit(solution)/shard_map/ppermute | solution.py:47
  371.1 25.7 %collective-permute-start.52 = (bf16[256,2048]{1,0:T(8,128)(2,1)S(1)}, bf16[256,2048]{1,0:T(8,128)(2,1)}, u32[]{:S(2)}, u32[]{:S(2)}) collective-permute-start(bf16[256,2048]{1,0:T(8,128)(2,1)S(1)} %pad_maximum_fusion.3), channel_id=1, source_target_pairs={{0,16},{4,20},{8,24},{12,28},{16,0},{20,4},{24,8},{28,12},{1,17},{... | collective-permute-start | bytes 3145736 | tf_op jit(solution)/shard_map/ppermute | solution.py:47
  424.8 30.9 %collective-permute-start.60 = (bf16[512,2048]{1,0:T(8,128)(2,1)}, bf16[512,2048]{1,0:T(8,128)(2,1)}, u32[]{:S(2)}, u32[]{:S(2)}) collective-permute-start(bf16[512,2048]{1,0:T(8,128)(2,1)} %get-tuple-element.451), channel_id=1, source_target_pairs={{0,4},{4,0},{8,12},{12,8},{16,20},{20,16},{24,28},{28,24},{1,5},{5... | collective-permute-start | bytes 6291464 | tf_op jit(solution)/shard_map/ppermute | solution.py:47
  477.6 32.4 %collective-permute-start.67 = (bf16[256,2048]{1,0:T(8,128)(2,1)S(1)}, bf16[256,2048]{1,0:T(8,128)(2,1)S(1)}, u32[]{:S(2)}, u32[]{:S(2)}) collective-permute-start(bf16[256,2048]{1,0:T(8,128)(2,1)S(1)} %pad_maximum_fusion.6), channel_id=1, source_target_pairs={{0,8},{4,12},{8,0},{12,4},{16,24},{20,28},{24,16},{28,20},{1,9},{5... | collective-permute-start | bytes 3145736 | tf_op jit(solution)/shard_map/ppermute | solution.py:47
  479.0 31.1 %collective-permute-start.68 = (bf16[256,2048]{1,0:T(8,128)(2,1)S(1)}, bf16[256,2048]{1,0:T(8,128)(2,1)}, u32[]{:S(2)}, u32[]{:S(2)}) collective-permute-start(bf16[256,2048]{1,0:T(8,128)(2,1)S(1)} %pad_maximum_fusion.7), channel_id=1, source_target_pairs={{0,16},{4,20},{8,24},{12,28},{16,0},{20,4},{24,8},{28,12},{1,17},{... | collective-permute-start | bytes 3145736 | tf_op jit(solution)/shard_map/ppermute | solution.py:47
  479.3 25.0 %collective-permute-start.72 = (bf16[64,2048]{1,0:T(8,128)(2,1)S(1)}, bf16[64,2048]{1,0:T(8,128)(2,1)S(1)}, u32[]{:S(2)}, u32[]{:S(2)}) collective-permute-start(bf16[64,2048]{1,0:T(8,128)(2,1)S(1)} %get-tuple-element.493), channel_id=1, source_target_pairs={{0,2},{1,3},{2,0},{3,1},{4,6},{5,7},{6,4},{7,5},{8,10},{9,11},{10,... | collective-permute-start | bytes 786440 | tf_op jit(solution)/shard_map/ppermute | solution.py:50
  479.3 27.2 %collective-permute-start.73 = (bf16[64,2048]{1,0:T(8,128)(2,1)S(1)}, bf16[64,2048]{1,0:T(8,128)(2,1)S(1)}, u32[]{:S(2)}, u32[]{:S(2)}) collective-permute-start(bf16[64,2048]{1,0:T(8,128)(2,1)S(1)} %get-tuple-element.494), channel_id=1, source_target_pairs={{0,3},{1,0},{2,1},{3,2},{4,7},{5,4},{6,5},{7,6},{8,11},{9,8},{10,9... | collective-permute-start | bytes 786440 | tf_op jit(solution)/shard_map/ppermute | solution.py:50
  514.7 25.6 %collective-permute-start.75 = (bf16[64,2432]{1,0:T(8,128)(2,1)S(1)}, bf16[64,2432]{1,0:T(8,128)(2,1)}, u32[]{:S(2)}, u32[]{:S(2)}) collective-permute-start(bf16[64,2432]{1,0:T(8,128)(2,1)S(1)} %pad_maximum_fusion.9), channel_id=1, source_target_pairs={{0,2},{1,3},{2,0},{3,1},{4,6},{5,7},{6,4},{7,5},{8,10},{9,11},{10,... | collective-permute-start | bytes 933896 | tf_op jit(solution)/shard_map/ppermute | solution.py:50
  517.8 28.2 %collective-permute-start.76 = (bf16[64,2432]{1,0:T(8,128)(2,1)S(1)}, bf16[64,2432]{1,0:T(8,128)(2,1)}, u32[]{:S(2)}, u32[]{:S(2)}) collective-permute-start(bf16[64,2432]{1,0:T(8,128)(2,1)S(1)} %pad_maximum_fusion.10), channel_id=1, source_target_pairs={{0,3},{1,0},{2,1},{3,2},{4,7},{5,4},{6,5},{7,6},{8,11},{9,8},{10,9... | collective-permute-start | bytes 933896 | tf_op jit(solution)/shard_map/ppermute | solution.py:50
  519.3 31.8 %all-to-all-start.1 = ((bf16[8,64,1,1024]{3,1,2,0:T(8,128)(2,1)}), bf16[8,64,1,1024]{3,1,2,0:T(8,128)(2,1)S(1)}, u32[]{:S(2)}, u32[]{:S(2)}) async-start(bf16[8,64,1,1024]{3,1,2,0:T(8,128)(2,1)} %bitcast.127), calls=%async_computation.3 | async-start | bytes 2097152 | tf_op jit(solution)/shard_map/all_to_all | solution.py:1079
  (95 other events, 1128.8 us)
Sparse Core Ops, SparseCore 0:
  74.4 87.2 all-gather.3
  163.3 80.3 all-gather.5
  319.0 75.4 reduce-scatter.2
  405.5 94.0 reduce-scatter.4

commit v5 on v4

--- a/solution.py
+++ b/solution.py
@@ -982,10 +982,11 @@
     corner = ring.corner_sums(even, other)
     corner, act_low = tick(corner, act_low)
     far = ring.send_corner(corner)
+    d_fc = d_fc_call(mlp_all, grad_pre, dp, seq)
+    d_fc, act_low = tick(d_fc, act_low)
+    fc_share = lax.psum_scatter(d_fc, "seq", scatter_dimension=0, tiled=False)
     branch_odd = branch_call(act_low, True, proj_all)
-    d_fc = d_fc_call(mlp_all, grad_pre, dp, seq)
-    far, branch_odd, act_low, d_fc = tick(far, branch_odd, act_low, d_fc)
-    fc_share = lax.psum_scatter(d_fc, "seq", scatter_dimension=0, tiled=False)
+    far, branch_odd, act_low = tick(far, branch_odd, act_low)
     cross = ring.cross_sums(even, other, far)
     cross, act_low, branch_odd = tick(cross, act_low, branch_odd)
     near = ring.send_cross(cross)
@@ -1062,14 +1063,14 @@
     output = (hidden_one + branch_two + nat[6:7]).astype(BF).reshape(windows, span, width)
     small_other, out_mine, out_sends, output = tick(small_other, out_mine, out_sends, output)
     small_far = ring.send_corner(ring.corner_sums(small[:cut], small_other))
-    q_far, small_far = tick(q_far, small_far)
+    q_far, small_far, proj_share = tick(q_far, small_far, proj_share)
     cross = ring.cross_sums(d_q_even, d_q_other, q_far)
     small_cross = ring.cross_sums(small[:cut], small_other, small_far)
     cross, out_sends, small_cross = tick(cross, out_sends, small_cross)
     q_near = ring.send_cross(cross)
     small_near = ring.send_cross(small_cross)
     d_w_out = ring.seq_sum(out_mine, out_sends)
-    q_near, small_near, d_w_out, proj_share = tick(q_near, small_near, d_w_out, proj_share)
+    q_near, small_near, d_w_out = tick(q_near, small_near, d_w_out)
     q_share = ring.scatter_end(d_q_even, d_q_other, q_near)
     small_share = ring.scatter_end(small[:cut], small_other, small_near)
     q_mine, q_sends = ring.seq_cut(q_share, own)

time: 568 us -> 575 us (1.012)
    unnamed x99 -> x101, local copies, waits for them, and re-layouts: 13.5 us -> 14.5 us
  transfers between devices with their start and end apart: 83 -> 83, of which waited for: 31 -> 34; matrix products, arithmetic and copies ran while one was open for 12% -> 12% of each run, Pallas kernels for 30% -> 29%
where the time goes in v5:
time: 575 us; the launch traced here: 566 us
  Pallas kernels  198 us (34%)
  waiting for transfers between devices  178 us (31%)
  starting transfers between devices  77.4 us (13%)
  local copies, waits for them, and re-layouts  51.5 us (9%)
  other arithmetic  44.6 us (8%)
  between operations  16.7 us (3%)
    ppermute x18, waiting for transfers between devices, up(): lax.ppermute(value, 'seq', [(i, (i + by) % self.ns) for i in range(self.n...  119 us
    ppermute x59, waiting for transfers between devices, swap(): return lax.ppermute(value, 'dp', [(i, i ^ mask) for i in range(self.nd)])  49.3 us
    ppermute x59, starting transfers between devices, swap(): return lax.ppermute(value, 'dp', [(i, i ^ mask) for i in range(self.nd)])  46.5 us
    pallas_call x4, Pallas kernels, d_rows_call(): pl.pallas_call(kernel, name='d_rows', grid=(blocks,), in_specs=[pl.BlockS...  22.3 us
    pallas_call x1, Pallas kernels, feed_call(): pl.pallas_call(kernel, name='feed', grid=(rows // tile,), in_specs=[pl.Bl...  21.4 us
    pallas_call x2, Pallas kernels, grad_mlp_call(): pl.pallas_call(kernel, name='grad_mlp', grid=(rows // tile,), in_specs=[p...  19.6 us
    ppermute x18, starting transfers between devices, up(): lax.ppermute(value, 'seq', [(i, (i + by) % self.ns) for i in range(self.n...  18.2 us
    pallas_call x1, Pallas kernels, attend_back(): pl.pallas_call(lambda *refs: attend_back_kernel(*refs, heads=heads, scale...  17.8 us
  transfers between devices with their start and end apart: 83, of which 34 were waited for; matrix products, arithmetic and copies ran while one was open for 12% of the time, Pallas kernels for 29%

profile of v5, /device:TPU:9, one launch (start us, length us, event | category | flops | bytes accessed | tf_op | source)
XLA Modules:
  0.0 566.1 jit_solution(2486605717614240261)
XLA Ops:
  22.2 19.0 %collective-permute-done.1 = bf16[64,2432]{1,0:T(8,128)(2,1)S(1)} collective-permute-done((bf16[64,2432]{1,0:T(8,128)(2,1)S(1)}, bf16[64,2432]{1,0:T(8,128)(2,1)S(1)}, u32[]{:S(2)}, u32[]{:S(2)}) %collective-permute-start.1) | collective-permute-done | bytes 311328 | tf_op jit(solution)/shard_map/ppermute | solution.py:50
  48.1 5.4 collective-permute-done.7
  53.5 14.9 %collective-permute-done.8 = bf16[64,2048]{1,0:T(8,128)(2,1)S(1)} collective-permute-done((bf16[64,2048]{1,0:T(8,128)(2,1)S(1)}, bf16[64,2048]{1,0:T(8,128)(2,1)S(1)}, u32[]{:S(2)}, u32[]{:S(2)}) %collective-permute-start.8) | collective-permute-done | bytes 262176 | tf_op jit(solution)/shard_map/ppermute | solution.py:50
  82.5 11.6 %collective-permute-done.10 = bf16[128,2432]{1,0:T(8,128)(2,1)S(1)} collective-permute-done((bf16[128,2432]{1,0:T(8,128)(2,1)S(1)}, bf16[128,2432]{1,0:T(8,128)(2,1)S(1)}, u32[]{:S(2)}, u32[]{:S(2)}) %collective-permute-start.10) | collective-permute-done | bytes 622624 | tf_op jit(solution)/shard_map/ppermute | solution.py:47
  100.4 9.3 %enter.1 = (bf16[256,2048]{1,0:T(8,128)(2,1)}, bf16[256,2048]{1,0:T(8,128)(2,1)}, bf16[256,256]{1,0:T(8,128)(2,1)}, f32[16,2048]{1,0:T(8,128)}, f32[16,2048]{1,0:T(8,128)}) custom-call(s32[9]{0:T(128)} %stack.39.info.refs_0_, bf16[256,2048]{1,0:T(8,128)(2,1)} %bitcast.119, bf16[256,2432]{1,0:T(8,128)(2,1)} %bitcast.112, ...), custom_call_target="tpu_custom_call" | custom-call | flops 1024 | bytes 1024 | tf_op jit(solution)/shard_map/enter/pallas_call | solution.py:407
  116.4 4.8 all-to-all-start
  123.9 11.7 %collective-permute-done.17 = bf16[256,256]{1,0:T(8,128)(2,1)S(1)} collective-permute-done((bf16[256,256]{1,0:T(8,128)(2,1)}, bf16[256,256]{1,0:T(8,128)(2,1)S(1)}, u32[]{:S(2)}, u32[]{:S(2)}) %collective-permute-start.17) | collective-permute-done | bytes 131104 | tf_op jit(solution)/shard_map/ppermute | solution.py:50
  150.0 14.6 %shard_map.314 = (bf16[256,2048]{1,0:T(8,128)(2,1)S(1)}, f32[16,1,256]{2,1,0:T(1,128)S(1)}) custom-call(s32[9]{0:T(128)S(1)} %copy-done.5, bf16[256,2048]{1,0:T(8,128)(2,1)S(1)} %copy-done.2, bf16[1024,128]{1,0:T(8,128)(2,1)S(1)} %get-tuple-element.569.refs_2_.refs_4_, bf16[128,1024]{1,0:T(8,128)(2,1)S(1)} %copy.99.refs_3_, f32[256,1]{1,0:T(8,128)S(1)} %copy.100.refs_4_.valid), custom_call_target="tpu_custom_call" | custom-call | flops 1024 | bytes 1024 | tf_op jit(solution)/shard_map/pallas_call | solution.py:213
  172.2 9.8 %leave.1 = (f32[256,2048]{1,0:T(8,128)}, bf16[256,2048]{1,0:T(8,128)(2,1)}) custom-call(bf16[256,2048]{1,0:T(8,128)(2,1)} %copy-done.1, bf16[256,2048]{1,0:T(8,128)(2,1)} %bitcast.120, f32[16,2048]{1,0:T(8,128)} %get-tuple-element.324.nat, bf16[256,2048]{1,0:T(8,128)(2,1)} %bitcast.117, bf16[256,2048]{1,0:T(8,128)(2,1)} %collective-permute-done.19.refs_1_, ...), custom_call_target="tpu_custom_call" | custom-call | flops 1024 | bytes 1024 | tf_op jit(solution)/shard_map/leave/pallas_call | solution.py:443
  191.9 15.3 %grad_act.1 = (bf16[2048,2048]{1,0:T(8,128)(2,1)}, bf16[2048,1024]{1,0:T(8,128)(2,1)}) custom-call(f32[2048,1]{1,0:T(8,128)} %copy.101.scale, bf16[1024,2048]{1,0:T(8,128)(2,1)} %all-gather.4.cloned.1.call-done.weight, bf16[256,2048]{1,0:T(8,128)(2,1)} %bitcast.126, bf16[256,2048]{1,0:T(8,128)(2,1)} %copy-done.23, ...), custom_call_target="tpu_custom_call" | custom-call | flops 1024 | bytes 1024 | tf_op jit(solution)/shard_map/grad_act/pallas_call | solution.py:617
  207.3 6.9 %collective-permute-done.33.refs_1_ = bf16[256,2048]{1,0:T(8,128)(2,1)S(1)} collective-permute-done((bf16[256,2048]{1,0:T(8,128)(2,1)}, bf16[256,2048]{1,0:T(8,128)(2,1)S(1)}, u32[]{:S(2)}, u32[]{:S(2)}) %collective-permute-start.33) | collective-permute-done | bytes 1048608 | tf_op jit(solution)/shard_map/ppermute | solution.py:47
  219.4 11.7 %collective-permute-done.35 = bf16[128,2048]{1,0:T(8,128)(2,1)S(1)} collective-permute-done((bf16[128,2048]{1,0:T(8,128)(2,1)S(1)}, bf16[128,2048]{1,0:T(8,128)(2,1)S(1)}, u32[]{:S(2)}, u32[]{:S(2)}) %collective-permute-start.35) | collective-permute-done | bytes 524320 | tf_op jit(solution)/shard_map/ppermute | solution.py:47
  236.1 7.9 %all-gather.6.cloned.1.call-done = bf16[32,64,1024]{2,1,0:T(8,128)(2,1)} async-done(((bf16[8,64,1024]{2,1,0:T(8,128)(2,1)}), bf16[32,64,1024]{2,1,0:T(8,128)(2,1)}) %all-gather.6.cloned.1.call-update) | async-done | bytes 4194320 | tf_op jit(solution)/shard_map/all_gather | solution.py:945
  244.1 21.4 %feed.1 = (bf16[2048,2048]{1,0:T(8,128)(2,1)}, bf16[2048,1024]{1,0:T(8,128)(2,1)}, bf16[2048,1024]{1,0:T(8,128)(2,1)}, f32[1,1024]{1,0:T(1,128)}) custom-call(f32[1,1024]{1,0:T(1,128)} %reshape.155.offset, bf16[2048,1024]{1,0:T(8,128)(2,1)} %get-tuple-element.356.back, bf16[4,8,64,1024]{3,2,1,0:T(8,128)(2,1)} %bitcast.106, ...), custom_call_target="tpu_custom_call" | custom-call | flops 1024 | bytes 1024 | tf_op jit(solution)/shard_map/feed/pallas_call | solution.py:672
  265.5 10.1 %grad_mlp.2 = bf16[1024,2048]{1,0:T(8,128)(2,1)} custom-call(bf16[2048,1024]{1,0:T(8,128)(2,1)} %get-tuple-element.377.value.grad, bf16[4,8,64,1024]{3,2,1,0:T(8,128)(2,1)} %bitcast.107), custom_call_target="tpu_custom_call" | custom-call | flops 1024 | bytes 1024 | tf_op jit(solution)/shard_map/grad_mlp/pallas_call | solution.py:719
  276.2 9.6 %grad_mlp.3.g0 = bf16[1024,2048]{1,0:T(8,128)(2,1)} custom-call(bf16[2048,1024]{1,0:T(8,128)(2,1)} %get-tuple-element.377.value.grad, bf16[4,8,64,1024]{3,2,1,0:T(8,128)(2,1)} %bitcast.108), custom_call_target="tpu_custom_call" | custom-call | flops 1024 | bytes 1024 | tf_op jit(solution)/shard_map/grad_mlp/pallas_call | solution.py:719
  291.9 14.1 %d_fc.1 = bf16[4,8,64,1024]{3,2,1,0:T(8,128)(2,1)} custom-call(bf16[2048,2048]{1,0:T(8,128)(2,1)} %get-tuple-element.386.mlp, bf16[2048,1024]{1,0:T(8,128)(2,1)} %get-tuple-element.377.value.grad), custom_call_target="tpu_custom_call" | custom-call | flops 1024 | bytes 1024 | tf_op jit(solution)/shard_map/d_fc/pallas_call | solution.py:820
  306.0 8.7 %branch.2 = bf16[1024,2048]{1,0:T(8,128)(2,1)} custom-call(bf16[2048,1024]{1,0:T(8,128)(2,1)} %get-tuple-element.398.value.act, bf16[1024,2048]{1,0:T(8,128)(2,1)} %all-gather.4.cloned.1.call-done.weight), custom_call_target="tpu_custom_call" | custom-call | flops 1024 | bytes 1024 | tf_op jit(solution)/shard_map/branch/pallas_call | solution.py:741
  319.9 8.8 %branch.3 = bf16[1024,2048]{1,0:T(8,128)(2,1)} custom-call(bf16[2048,1024]{1,0:T(8,128)(2,1)} %get-tuple-element.398.value.act, bf16[1024,2048]{1,0:T(8,128)(2,1)} %all-gather.4.cloned.1.call-done.weight), custom_call_target="tpu_custom_call" | custom-call | flops 1024 | bytes 1024 | tf_op jit(solution)/shard_map/branch/pallas_call | solution.py:741
  328.7 14.3 %d_proj.1 = bf16[1024,2048]{1,0:T(8,128)(2,1)} custom-call(bf16[2048,1024]{1,0:T(8,128)(2,1)} %get-tuple-element.398.value.act, bf16[2048,2048]{1,0:T(8,128)(2,1)} %get-tuple-element.400.two), custom_call_target="tpu_custom_call" | custom-call | flops 1024 | bytes 1024 | tf_op jit(solution)/shard_map/d_proj/pallas_call | solution.py:799
  350.0 10.4 %middle.1 = (f32[256,2048]{1,0:T(8,128)}, bf16[256,2048]{1,0:T(8,128)(2,1)}, f32[8,2048]{1,0:T(8,128)}, bf16[256,2048]{1,0:T(8,128)(2,1)}) custom-call(bf16[1024,2048]{1,0:T(8,128)(2,1)} %grad_mlp.3.g0, bf16[1024,2048]{1,0:T(8,128)(2,1)} %copy-done.9, bf16[256,2048]{1,0:T(8,128)(2,1)} %copy-done.29, bf16[256,2048]{1,0:T(8,128)(2,1)} %collective-permute-done.45.g3, ...), custom_call_target="tpu_custom_call" | custom-call | flops 1024 | bytes 1024 | tf_op jit(solution)/shard_map/middle/pallas_call | solution.py:491
  360.4 5.8 %d_rows.4 = (bf16[512,2048]{1,0:T(8,128)(2,1)}, bf16[512,2048]{1,0:T(8,128)(2,1)}) custom-call(bf16[256,2048]{1,0:T(8,128)(2,1)} %copy-done.1, bf16[256,2048]{1,0:T(8,128)(2,1)} %get-tuple-element.427.right), custom_call_target="tpu_custom_call" | custom-call | flops 1024 | bytes 1024 | tf_op jit(solution)/shard_map/d_rows/pallas_call | solution.py:775
  375.4 17.8 %shard_map.315 = (bf16[256,2048]{1,0:T(8,128)(2,1)S(1)}, f32[1024,128]{1,0:T(8,128)S(1)}, f32[1024,128]{1,0:T(8,128)S(1)}) custom-call(s32[9]{0:T(128)S(1)} %copy-done.5, bf16[256,2048]{1,0:T(8,128)(2,1)S(1)} %copy-done.2, bf16[256,2048]{1,0:T(8,128)(2,1)S(1)} %copy-done.4, f32[16,1,256]{2,1,0:T(1,128)S(1)} %get-tuple-element.423.refs_3_, ...), custom_call_target="tpu_custom_call" | custom-call | flops 1024 | bytes 1024 | tf_op jit(solution)/shard_map/pallas_call | solution.py:272
  394.3 5.4 d_rows.5
  408.3 5.8 %d_rows.6 = (bf16[512,2048]{1,0:T(8,128)(2,1)}, bf16[512,2048]{1,0:T(8,128)(2,1)}) custom-call(bf16[256,2048]{1,0:T(8,128)(2,1)} %get-tuple-element.443.left.attn, bf16[256,2048]{1,0:T(8,128)(2,1)} %copy-done), custom_call_target="tpu_custom_call" | custom-call | flops 1024 | bytes 1024 | tf_op jit(solution)/shard_map/d_rows/pallas_call | solution.py:775
  414.3 16.6 %collective-permute-done.56 = bf16[256,256]{1,0:T(8,128)(2,1)S(1)} collective-permute-done((bf16[256,256]{1,0:T(8,128)(2,1)S(1)}, bf16[256,256]{1,0:T(8,128)(2,1)S(1)}, u32[]{:S(2)}, u32[]{:S(2)}) %collective-permute-start.56) | collective-permute-done | bytes 131104 | tf_op jit(solution)/shard_map/ppermute | solution.py:50
  444.5 5.3 d_rows.7
  449.8 11.8 %last.1 = (bf16[256,2048]{1,0:T(8,128)(2,1)}, bf16[2048,384]{1,0:T(8,128)(2,1)}) custom-call(s32[9]{0:T(128)} %stack.39.info.refs_0_, bf16[256,2048]{1,0:T(8,128)(2,1)} %copy-done, bf16[256,256]{1,0:T(8,128)(2,1)} %add_convert_fusion.22.kv, bf16[256,2048]{1,0:T(8,128)(2,1)} %bitcast.121, bf16[256,2048]{1,0:T(8,128)(2,1)} %get-tuple-element.443.left.attn, ...), custom_call_target="tpu_custom_call" | custom-call | flops 1024 | bytes 1024 | tf_op jit(solution)/shard_map/last/pallas_call | solution.py:571
  499.8 14.6 %collective-permute-done.72 = bf16[64,2048]{1,0:T(8,128)(2,1)S(1)} collective-permute-done((bf16[64,2048]{1,0:T(8,128)(2,1)S(1)}, bf16[64,2048]{1,0:T(8,128)(2,1)S(1)}, u32[]{:S(2)}, u32[]{:S(2)}) %collective-permute-start.72) | collective-permute-done | bytes 262176 | tf_op jit(solution)/shard_map/ppermute | solution.py:50
  528.7 7.5 %all-to-all-start.1 = ((bf16[8,64,1,1024]{3,1,2,0:T(8,128)(2,1)}), bf16[8,64,1,1024]{3,1,2,0:T(8,128)(2,1)S(1)}, u32[]{:S(2)}, u32[]{:S(2)}) async-start(bf16[8,64,1,1024]{3,1,2,0:T(8,128)(2,1)} %bitcast.56), calls=%async_computation.3 | async-start | bytes 2097152 | tf_op jit(solution)/shard_map/all_to_all | solution.py:1080
  536.3 11.8 %collective-permute-done.75 = bf16[64,2432]{1,0:T(8,128)(2,1)S(1)} collective-permute-done((bf16[64,2432]{1,0:T(8,128)(2,1)S(1)}, bf16[64,2432]{1,0:T(8,128)(2,1)S(1)}, u32[]{:S(2)}, u32[]{:S(2)}) %collective-permute-start.75) | collective-permute-done | bytes 311328 | tf_op jit(solution)/shard_map/ppermute | solution.py:50
  548.1 5.4 collective-permute-done.76
  (375 shorter events, 201.1 us)
Async XLA Ops:
  7.2 184.8 %all-gather.4.cloned.1.call-start = ((), (), s32[]{:S(2)}) async-start(), calls=%async_computation.4 | async-start | bytes 5242880 | tf_op jit(solution)/shard_map/all_gather | solution.py:910
  7.2 37.5 %collective-permute-start.3 = (bf16[256,2048]{1,0:T(8,128)(2,1)}, bf16[256,2048]{1,0:T(8,128)(2,1)S(1)}, u32[]{:S(2)}, u32[]{:S(2)}) collective-permute-start(bf16[256,2048]{1,0:T(8,128)(2,1)} %bitcast.124), channel_id=1, source_target_pairs={{0,8},{4,12},{8,0},{12,4},{16,24},{20,28},{24,16},{28,20},{1,9},{5... | collective-permute-start | bytes 3145736 | tf_op jit(solution)/shard_map/ppermute | solution.py:47
  8.5 37.3 %collective-permute-start.4 = (bf16[256,2048]{1,0:T(8,128)(2,1)}, bf16[256,2048]{1,0:T(8,128)(2,1)}, u32[]{:S(2)}, u32[]{:S(2)}) collective-permute-start(bf16[256,2048]{1,0:T(8,128)(2,1)} %bitcast.125), channel_id=1, source_target_pairs={{0,16},{4,20},{8,24},{12,28},{16,0},{20,4},{24,8},{28,12},{1,17},{... | collective-permute-start | bytes 3145736 | tf_op jit(solution)/shard_map/ppermute | solution.py:47
  15.8 25.4 %collective-permute-start.1 = (bf16[64,2432]{1,0:T(8,128)(2,1)S(1)}, bf16[64,2432]{1,0:T(8,128)(2,1)S(1)}, u32[]{:S(2)}, u32[]{:S(2)}) collective-permute-start(bf16[64,2432]{1,0:T(8,128)(2,1)S(1)} %fusion.4), channel_id=1, source_target_pairs={{0,2},{1,3},{2,0},{3,1},{4,6},{5,7},{6,4},{7,5},{8,10},{9,11},{10,... | collective-permute-start | bytes 933896 | tf_op jit(solution)/shard_map/ppermute | solution.py:50
  16.9 27.8 %collective-permute-start.2 = (bf16[64,2432]{1,0:T(8,128)(2,1)S(1)}, bf16[64,2432]{1,0:T(8,128)(2,1)S(1)}, u32[]{:S(2)}, u32[]{:S(2)}) collective-permute-start(bf16[64,2432]{1,0:T(8,128)(2,1)S(1)} %fusion.4), channel_id=1, source_target_pairs={{0,3},{1,0},{2,1},{3,2},{4,7},{5,4},{6,5},{7,6},{8,11},{9,8},{10,9... | collective-permute-start | bytes 933896 | tf_op jit(solution)/shard_map/ppermute | solution.py:50
  46.0 28.6 %collective-permute-start.5 = (bf16[256,2432]{1,0:T(8,128)(2,1)S(1)}, bf16[256,2432]{1,0:T(8,128)(2,1)}, u32[]{:S(2)}, u32[]{:S(2)}) collective-permute-start(bf16[256,2432]{1,0:T(8,128)(2,1)S(1)} %bitcast.109), channel_id=1, source_target_pairs={{0,8},{4,12},{8,0},{12,4},{16,24},{20,28},{24,16},{28,20},{1,9},{5... | collective-permute-start | bytes 3735560 | tf_op jit(solution)/shard_map/ppermute | solution.py:47
  46.4 28.3 %collective-permute-start.6 = (bf16[256,2432]{1,0:T(8,128)(2,1)S(1)}, bf16[256,2432]{1,0:T(8,128)(2,1)}, u32[]{:S(2)}, u32[]{:S(2)}) collective-permute-start(bf16[256,2432]{1,0:T(8,128)(2,1)S(1)} %bitcast.110), channel_id=1, source_target_pairs={{0,16},{4,20},{8,24},{12,28},{16,0},{20,4},{24,8},{28,12},{1,17},{... | collective-permute-start | bytes 3735560 | tf_op jit(solution)/shard_map/ppermute | solution.py:47
  97.9 25.9 %collective-permute-start.19 = (bf16[256,2048]{1,0:T(8,128)(2,1)S(1)}, bf16[256,2048]{1,0:T(8,128)(2,1)}, u32[]{:S(2)}, u32[]{:S(2)}) collective-permute-start(bf16[256,2048]{1,0:T(8,128)(2,1)S(1)} %bitcast.114), channel_id=1, source_target_pairs={{0,8},{4,12},{8,0},{12,4},{16,24},{20,28},{24,16},{28,20},{1,9},{5... | collective-permute-start | bytes 3145736 | tf_op jit(solution)/shard_map/ppermute | solution.py:47
  99.2 24.7 %collective-permute-start.20 = (bf16[256,2048]{1,0:T(8,128)(2,1)S(1)}, bf16[256,2048]{1,0:T(8,128)(2,1)}, u32[]{:S(2)}, u32[]{:S(2)}) collective-permute-start(bf16[256,2048]{1,0:T(8,128)(2,1)S(1)} %bitcast.115), channel_id=1, source_target_pairs={{0,16},{4,20},{8,24},{12,28},{16,0},{20,4},{24,8},{28,12},{1,17},{... | collective-permute-start | bytes 3145736 | tf_op jit(solution)/shard_map/ppermute | solution.py:47
  109.8 25.8 %collective-permute-start.17 = (bf16[256,256]{1,0:T(8,128)(2,1)}, bf16[256,256]{1,0:T(8,128)(2,1)S(1)}, u32[]{:S(2)}, u32[]{:S(2)}) collective-permute-start(bf16[256,256]{1,0:T(8,128)(2,1)} %get-tuple-element.309), channel_id=1, source_target_pairs={{0,2},{1,3},{2,0},{3,1},{4,6},{5,7},{6,4},{7,5},{8,10},{9,11},{10,... | collective-permute-start | bytes 393224 | tf_op jit(solution)/shard_map/ppermute | solution.py:50
  109.9 27.8 %collective-permute-start.18 = (bf16[256,256]{1,0:T(8,128)(2,1)}, bf16[256,256]{1,0:T(8,128)(2,1)S(1)}, u32[]{:S(2)}, u32[]{:S(2)}) collective-permute-start(bf16[256,256]{1,0:T(8,128)(2,1)} %get-tuple-element.309), channel_id=1, source_target_pairs={{0,3},{1,0},{2,1},{3,2},{4,7},{5,4},{6,5},{7,6},{8,11},{9,8},{10,9... | collective-permute-start | bytes 393224 | tf_op jit(solution)/shard_map/ppermute | solution.py:50
  121.2 122.8 %all-gather.6.cloned.1.call-start = ((), (), s32[]{:S(2)}) async-start(), calls=%async_computation.7 | async-start | bytes 5242880 | tf_op jit(solution)/shard_map/all_gather | solution.py:945
  139.9 24.8 %collective-permute-start.24 = (bf16[256,2048]{1,0:T(8,128)(2,1)}, bf16[256,2048]{1,0:T(8,128)(2,1)}, u32[]{:S(2)}, u32[]{:S(2)}) collective-permute-start(bf16[256,2048]{1,0:T(8,128)(2,1)} %collective-permute-done.19.refs_1_), channel_id=1, source_target_pairs={{0,4},{4,0},{8,12},{12,8},{16,20},{20,16},{24,28},{28,24},{1,5},{5... | collective-permute-start | bytes 3145736 | tf_op jit(solution)/shard_map/ppermute | solution.py:47
  145.9 254.0 %reduce-scatter.3.cloned.1.call-start = ((), (), s32[]{:S(2)}) async-start(), calls=%async_computation.5 | async-start | bytes 5242880 | tf_op jit(solution)/shard_map/reduce_scatter | solution.py:987
  189.1 25.0 %collective-permute-start.33 = (bf16[256,2048]{1,0:T(8,128)(2,1)}, bf16[256,2048]{1,0:T(8,128)(2,1)S(1)}, u32[]{:S(2)}, u32[]{:S(2)}) collective-permute-start(bf16[256,2048]{1,0:T(8,128)(2,1)} %get-tuple-element.367.refs_0_), channel_id=1, source_target_pairs={{0,8},{4,12},{8,0},{12,4},{16,24},{20,28},{24,16},{28,20},{1,9},{5... | collective-permute-start | bytes 3145736 | tf_op jit(solution)/shard_map/ppermute | solution.py:47
  289.3 25.4 %collective-permute-start.42 = (bf16[128,2048]{1,0:T(8,128)(2,1)}, bf16[128,2048]{1,0:T(8,128)(2,1)S(1)}, u32[]{:S(2)}, u32[]{:S(2)}) collective-permute-start(bf16[128,2048]{1,0:T(8,128)(2,1)} %get-tuple-element.384), channel_id=1, source_target_pairs={{0,16},{4,20},{8,24},{12,28},{16,0},{20,4},{24,8},{28,12},{1,17},{... | collective-permute-start | bytes 1572872 | tf_op jit(solution)/shard_map/ppermute | solution.py:47
  318.9 25.8 %collective-permute-start.46 = (bf16[1024,2048]{1,0:T(8,128)(2,1)}, bf16[1024,2048]{1,0:T(8,128)(2,1)}, u32[]{:S(2)}, u32[]{:S(2)}) collective-permute-start(bf16[1024,2048]{1,0:T(8,128)(2,1)} %branch.2), channel_id=1, source_target_pairs={{0,4},{4,0},{8,12},{12,8},{16,20},{20,16},{24,28},{28,24},{1,5},{5... | collective-permute-start | bytes 12582920 | tf_op jit(solution)/shard_map/ppermute | solution.py:47
  319.5 166.4 %reduce-scatter.5.cloned.1.call-start = ((), (), s32[]{:S(2)}) async-start(), calls=%async_computation.6 | async-start | bytes 5242880 | tf_op jit(solution)/shard_map/reduce_scatter | solution.py:997
  319.5 25.2 %collective-permute-start.44 = (bf16[256,2048]{1,0:T(8,128)(2,1)}, bf16[256,2048]{1,0:T(8,128)(2,1)S(1)}, u32[]{:S(2)}, u32[]{:S(2)}) collective-permute-start(bf16[256,2048]{1,0:T(8,128)(2,1)} %get-tuple-element.396), channel_id=1, source_target_pairs={{0,8},{4,12},{8,0},{12,4},{16,24},{20,28},{24,16},{28,20},{1,9},{5... | collective-permute-start | bytes 3145736 | tf_op jit(solution)/shard_map/ppermute | solution.py:47
  319.9 24.8 %collective-permute-start.45 = (bf16[256,2048]{1,0:T(8,128)(2,1)}, bf16[256,2048]{1,0:T(8,128)(2,1)}, u32[]{:S(2)}, u32[]{:S(2)}) collective-permute-start(bf16[256,2048]{1,0:T(8,128)(2,1)} %get-tuple-element.397), channel_id=1, source_target_pairs={{0,16},{4,20},{8,24},{12,28},{16,0},{20,4},{24,8},{28,12},{1,17},{... | collective-permute-start | bytes 3145736 | tf_op jit(solution)/shard_map/ppermute | solution.py:47
  371.0 28.8 %collective-permute-start.49 = (bf16[512,2048]{1,0:T(8,128)(2,1)}, bf16[512,2048]{1,0:T(8,128)(2,1)}, u32[]{:S(2)}, u32[]{:S(2)}) collective-permute-start(bf16[512,2048]{1,0:T(8,128)(2,1)} %get-tuple-element.428), channel_id=1, source_target_pairs={{0,4},{4,0},{8,12},{12,8},{16,20},{20,16},{24,28},{28,24},{1,5},{5... | collective-permute-start | bytes 6291464 | tf_op jit(solution)/shard_map/ppermute | solution.py:47
  372.6 27.2 %collective-permute-start.50 = (bf16[512,2048]{1,0:T(8,128)(2,1)}, bf16[512,2048]{1,0:T(8,128)(2,1)}, u32[]{:S(2)}, u32[]{:S(2)}) collective-permute-start(bf16[512,2048]{1,0:T(8,128)(2,1)} %get-tuple-element.429), channel_id=1, source_target_pairs={{0,4},{4,0},{8,12},{12,8},{16,20},{20,16},{24,28},{28,24},{1,5},{5... | collective-permute-start | bytes 6291464 | tf_op jit(solution)/shard_map/ppermute | solution.py:47
  372.6 27.2 %collective-permute-start.51 = (bf16[256,2048]{1,0:T(8,128)(2,1)}, bf16[256,2048]{1,0:T(8,128)(2,1)}, u32[]{:S(2)}, u32[]{:S(2)}) collective-permute-start(bf16[256,2048]{1,0:T(8,128)(2,1)} %pad_maximum_fusion.2), channel_id=1, source_target_pairs={{0,8},{4,12},{8,0},{12,4},{16,24},{20,28},{24,16},{28,20},{1,9},{5... | collective-permute-start | bytes 3145736 | tf_op jit(solution)/shard_map/ppermute | solution.py:47
  372.9 26.9 %collective-permute-start.52 = (bf16[256,2048]{1,0:T(8,128)(2,1)}, bf16[256,2048]{1,0:T(8,128)(2,1)}, u32[]{:S(2)}, u32[]{:S(2)}) collective-permute-start(bf16[256,2048]{1,0:T(8,128)(2,1)} %pad_maximum_fusion.3), channel_id=1, source_target_pairs={{0,16},{4,20},{8,24},{12,28},{16,0},{20,4},{24,8},{28,12},{1,17},{... | collective-permute-start | bytes 3145736 | tf_op jit(solution)/shard_map/ppermute | solution.py:47
  401.9 31.2 %collective-permute-start.53 = (bf16[128,2048]{1,0:T(8,128)(2,1)S(1)}, bf16[128,2048]{1,0:T(8,128)(2,1)S(1)}, u32[]{:S(2)}, u32[]{:S(2)}) collective-permute-start(bf16[128,2048]{1,0:T(8,128)(2,1)S(1)} %get-tuple-element.437), channel_id=1, source_target_pairs={{0,16},{4,20},{8,24},{12,28},{16,0},{20,4},{24,8},{28,12},{1,17},{... | collective-permute-start | bytes 1572872 | tf_op jit(solution)/shard_map/ppermute | solution.py:47
  402.3 30.9 %collective-permute-start.54 = (bf16[128,2048]{1,0:T(8,128)(2,1)S(1)}, bf16[128,2048]{1,0:T(8,128)(2,1)S(1)}, u32[]{:S(2)}, u32[]{:S(2)}) collective-permute-start(bf16[128,2048]{1,0:T(8,128)(2,1)S(1)} %get-tuple-element.438), channel_id=1, source_target_pairs={{0,8},{4,12},{8,0},{12,4},{16,24},{20,28},{24,16},{28,20},{1,9},{5... | collective-permute-start | bytes 1572872 | tf_op jit(solution)/shard_map/ppermute | solution.py:47
  405.6 25.3 %collective-permute-start.56 = (bf16[256,256]{1,0:T(8,128)(2,1)S(1)}, bf16[256,256]{1,0:T(8,128)(2,1)S(1)}, u32[]{:S(2)}, u32[]{:S(2)}) collective-permute-start(bf16[256,256]{1,0:T(8,128)(2,1)S(1)} %get-tuple-element.441), channel_id=1, source_target_pairs={{0,2},{1,3},{2,0},{3,1},{4,6},{5,7},{6,4},{7,5},{8,10},{9,11},{10,... | collective-permute-start | bytes 393224 | tf_op jit(solution)/shard_map/ppermute | solution.py:50
  436.9 28.0 %collective-permute-start.60 = (bf16[512,2048]{1,0:T(8,128)(2,1)}, bf16[512,2048]{1,0:T(8,128)(2,1)}, u32[]{:S(2)}, u32[]{:S(2)}) collective-permute-start(bf16[512,2048]{1,0:T(8,128)(2,1)} %get-tuple-element.455), channel_id=1, source_target_pairs={{0,4},{4,0},{8,12},{12,8},{16,20},{20,16},{24,28},{28,24},{1,5},{5... | collective-permute-start | bytes 6291464 | tf_op jit(solution)/shard_map/ppermute | solution.py:47
  490.5 28.8 %collective-permute-start.67 = (bf16[256,2048]{1,0:T(8,128)(2,1)S(1)}, bf16[256,2048]{1,0:T(8,128)(2,1)S(1)}, u32[]{:S(2)}, u32[]{:S(2)}) collective-permute-start(bf16[256,2048]{1,0:T(8,128)(2,1)S(1)} %pad_maximum_fusion.6), channel_id=1, source_target_pairs={{0,8},{4,12},{8,0},{12,4},{16,24},{20,28},{24,16},{28,20},{1,9},{5... | collective-permute-start | bytes 3145736 | tf_op jit(solution)/shard_map/ppermute | solution.py:47
  491.7 27.6 %collective-permute-start.68 = (bf16[256,2048]{1,0:T(8,128)(2,1)S(1)}, bf16[256,2048]{1,0:T(8,128)(2,1)S(1)}, u32[]{:S(2)}, u32[]{:S(2)}) collective-permute-start(bf16[256,2048]{1,0:T(8,128)(2,1)S(1)} %pad_maximum_fusion.7), channel_id=1, source_target_pairs={{0,16},{4,20},{8,24},{12,28},{16,0},{20,4},{24,8},{28,12},{1,17},{... | collective-permute-start | bytes 3145736 | tf_op jit(solution)/shard_map/ppermute | solution.py:47
  525.8 27.8 %collective-permute-start.76 = (bf16[64,2432]{1,0:T(8,128)(2,1)S(1)}, bf16[64,2432]{1,0:T(8,128)(2,1)S(1)}, u32[]{:S(2)}, u32[]{:S(2)}) collective-permute-start(bf16[64,2432]{1,0:T(8,128)(2,1)S(1)} %pad_maximum_fusion.10), channel_id=1, source_target_pairs={{0,3},{1,0},{2,1},{3,2},{4,7},{5,4},{6,5},{7,6},{8,11},{9,8},{10,9... | collective-permute-start | bytes 933896 | tf_op jit(solution)/shard_map/ppermute | solution.py:50
  528.7 28.7 %all-to-all-start.1 = ((bf16[8,64,1,1024]{3,1,2,0:T(8,128)(2,1)}), bf16[8,64,1,1024]{3,1,2,0:T(8,128)(2,1)S(1)}, u32[]{:S(2)}, u32[]{:S(2)}) async-start(bf16[8,64,1,1024]{3,1,2,0:T(8,128)(2,1)} %bitcast.56), calls=%async_computation.3 | async-start | bytes 2097152 | tf_op jit(solution)/shard_map/all_to_all | solution.py:1080
  (96 other events, 1230.5 us)
Sparse Core Ops, SparseCore 0:
  74.8 87.2 all-gather.3
  163.7 80.3 all-gather.5
  319.6 75.4 reduce-scatter.2
  397.3 88.5 reduce-scatter.4
